TPU v7x, 32 devices: a whole 2x2x4 slice. The times are simulated.
32 devices in a mesh: row: 4 (over x, core), col: 8 (over z, y).
Axes of the slice: x: 2, y: 2, z: 4, core: 2. Of those that a mesh axis runs over, the one named last changes fastest.
Arguments:
- density: bfloat16 [6144, 6144], P('row', 'col'), may hold values from -5 to 5
- strips: bfloat16 [1024, 8, 128], P(('row', 'col')), may hold values from -5 to 5
- dest_device: int32 [1024, 1], P(('row', 'col')), may hold values from 0 to 31; in each aligned block of 32 rows (0 to 31, 32 to 63, ...) at most 2 rows name the same one
- atom_slot: int32 [1024], P(('row', 'col')), may hold values from 0 to 191
- block_slot: int32 [1024], P(('row', 'col')), may hold values from 0 to 5
- patterns: int32 [3, 48, 48], replicated, may hold values 0 or 1
Outputs:
- density_next: float32 [6144, 6144], P('row', 'col')
- response_next: float32 [6144, 6144], P('row', 'col')
Inputs may be any that keep to these rules, and one draw needn't show every extreme that they name: `dest_device`: of the 32 strips of one device, at most 2 name the same owner, and some owner is named that often.
All inputs are finite; a program needn't handle non-finite values.
Results may differ from a plain program's by a relative error of at most 0.0036.
Values may be sent and summed in bfloat16 or wider, within the bound.
No kernel may reach another device: no remote copies, remote signals or barrier semaphores. Data moves between devices by JAX's collectives and lax.ppermute only.
A program may use at most 128 MiB of HBM per device.

v0:
```python
import math

import jax
import jax.numpy as jnp
from jax import lax
from jax.sharding import PartitionSpec as P

STEPS = 2
CAPACITY = 2


def tile_kept(patterns, which, row_offset, col_offset, block_rows, block_cols, block_width):
    window = lax.dynamic_slice(patterns[which], (row_offset, col_offset), (block_rows, block_cols))
    global_rows = row_offset + lax.iota(jnp.int32, block_rows)
    global_cols = col_offset + lax.iota(jnp.int32, block_cols)
    diagonal = (global_rows[:, None] == global_cols[None, :]).astype(jnp.int32)
    kept = jnp.maximum(window, diagonal).astype(jnp.float32)
    return jnp.repeat(jnp.repeat(kept, block_width, axis=0), block_width, axis=1)


def products(zeroth, linear):
    col_zero, col_first = (
        lax.all_gather(zeroth, "row", axis=0, tiled=True),
        lax.all_gather(linear, "row", axis=0, tiled=True),
    )
    pieces = (
        lax.all_gather(zeroth, "col", axis=1, tiled=True),
        lax.all_gather(linear, "col", axis=1, tiled=True),
    )
    square = jnp.dot(pieces[0], col_zero, preferred_element_type=jnp.float32)
    left_part = jnp.dot(pieces[0], col_first, preferred_element_type=jnp.float32)
    right_part = jnp.dot(pieces[1], col_zero, preferred_element_type=jnp.float32)
    return (square, left_part + right_part)


def on_device(density, strips, dest_device, atom_slot, block_slot, patterns):
    tile_rows, tile_cols = density.shape
    mesh_rows = lax.axis_size("row")
    mesh_cols = lax.axis_size("col")
    devices = mesh_rows * mesh_cols
    matrix_order = tile_rows * mesh_rows
    atom_width = strips.shape[1]
    block_width = strips.shape[2]
    block_rows = tile_rows // block_width
    block_cols = tile_cols // block_width
    row_offset = lax.axis_index("row") * block_rows
    col_offset = lax.axis_index("col") * block_cols
    kept_zero = tile_kept(patterns, 0, row_offset, col_offset, block_rows, block_cols, block_width)
    kept_first = tile_kept(patterns, 1, row_offset, col_offset, block_rows, block_cols, block_width)
    kept_field = tile_kept(patterns, 2, row_offset, col_offset, block_rows, block_cols, block_width)
    capacity = CAPACITY
    targets = dest_device[:, 0]
    matches = (targets[:, None] == lax.iota(jnp.int32, devices)[None, :]).astype(jnp.int32)
    before = jnp.cumsum(matches, axis=0) - matches
    ranking = jnp.sum(before * matches, axis=1)
    position = targets * capacity + ranking
    sent_strips = (
        jnp.zeros((devices * capacity, atom_width, block_width), strips.dtype)
        .at[position]
        .set(strips)
    )
    sent_atoms = jnp.full((devices * capacity,), -1, jnp.int32).at[position].set(atom_slot)
    sent_blocks = jnp.zeros((devices * capacity,), jnp.int32).at[position].set(block_slot)
    arrived = (
        lax.all_to_all(
            sent_strips.reshape(devices, capacity, atom_width, block_width),
            ("row", "col"),
            split_axis=0,
            concat_axis=0,
            tiled=True,
        ),
        lax.all_to_all(
            sent_atoms.reshape(devices, capacity),
            ("row", "col"),
            split_axis=0,
            concat_axis=0,
            tiled=True,
        ),
        lax.all_to_all(
            sent_blocks.reshape(devices, capacity),
            ("row", "col"),
            split_axis=0,
            concat_axis=0,
            tiled=True,
        ),
    )
    recv_strips = arrived[0].reshape(-1, atom_width * block_width)
    recv_atoms = arrived[1].reshape(-1)
    recv_blocks = arrived[2].reshape(-1)
    atoms_here = tile_rows // atom_width
    atom_match = recv_atoms[:, None] == lax.iota(jnp.int32, atoms_here)[None, :]
    block_match = recv_blocks[:, None] == lax.iota(jnp.int32, block_cols)[None, :]
    placing = (
        (atom_match[:, :, None] & block_match[:, None, :])
        .astype(jnp.bfloat16)
        .reshape(-1, atoms_here * block_cols)
    )
    summed = lax.dot_general(
        placing, recv_strips, (((0,), (0,)), ((), ())), preferred_element_type=jnp.float32
    )
    h_field = (
        summed.reshape(atoms_here, block_cols, atom_width, block_width)
        .transpose(0, 2, 1, 3)
        .reshape(tile_rows, tile_cols)
    )
    linear = (-(kept_field * h_field)).astype(jnp.bfloat16)
    zeroth = density
    inv_root = 1.0 / math.sqrt(matrix_order)
    new_zeroth = None
    new_linear = None
    for iteration in range(STEPS):
        square, crossed = products(zeroth, linear)
        if iteration % 2 == 0:
            new_zeroth = kept_zero * (square * inv_root)
            new_linear = kept_first * (crossed * inv_root)
        else:
            new_zeroth = kept_zero * (2.0 * zeroth.astype(jnp.float32) - square * inv_root)
            new_linear = kept_first * (2.0 * linear.astype(jnp.float32) - crossed * inv_root)
        zeroth = new_zeroth.astype(jnp.bfloat16)
        linear = new_linear.astype(jnp.bfloat16)
    return (new_zeroth, new_linear)


def solution(mesh):
    return jax.shard_map(
        on_device,
        mesh=mesh,
        in_specs=(
            P("row", "col"),
            P(("row", "col"), None, None),
            P(("row", "col"), None),
            P(("row", "col")),
            P(("row", "col")),
            P(),
        ),
        out_specs=(P("row", "col"), P("row", "col")),
        check_vma=False,
    )
```

profile of v0, /device:TPU:1, one launch (start us, length us, event | category | flops | bytes accessed | tf_op | source)
XLA Modules:
  0.0 1831.9 jit_solution(11326931074219280704)
XLA Ops:
  7.2 0.7 fusion.7
  7.9 0.1 reduce_window_sum.11
  7.9 0.8 select_reduce_fusion
  8.8 0.7 fusion.11
  9.5 0.8 scatter_custom_fusion
  10.3 0.7 all_to_all.15
  11.0 7.1 all-to-all-start
  18.1 0.8 fusion.16
  18.9 0.1 constant_dynamic-slice_fusion
  19.0 0.1 copy.48
  19.1 0.1 copy.50
  19.1 0.1 constant_dynamic-slice_fusion.2
  19.2 0.1 copy.46
  19.3 0.1 fusion.10
  19.4 0.1 broadcast_bitcast_fusion
  19.5 0.8 scatter_custom_fusion.1
  20.3 0.7 all_to_all.17
  21.0 0.7 broadcast_in_dim.49
  21.7 3.9 scatter_fusion
  25.6 5.8 all-to-all-start.1
  31.4 0.5 broadcast.69
  32.0 0.7 reduce.7
  32.7 0.1 eq.87
  32.8 5.3 all-to-all-done.1
  38.1 2.9 all-to-all-start.2
  40.9 0.0 all-gather.17.cloned.1.call-start
  41.0 0.7 reduce.6
  41.7 0.1 eq.91
  41.8 0.1 broadcast_and_fusion
  41.9 0.2 and.22
  42.1 0.1 dot_general.34
  42.2 6.4 all-to-all-done.2
  48.7 0.7 convolution_bitcast_fusion
  49.4 4.9 copy.69
  54.3 6.0 copy.37
  60.4 4.4 fusion.4
  64.9 0.7 all-gather.9.cloned.1.call-update
  65.6 0.7 all-gather.11.cloned.1.call-update
  66.4 0.5 all-gather.19.cloned.1.call-update
  66.9 0.2 all-gather.21.cloned.1.call-start
  67.1 0.1 broadcast_bitcast_fusion.1
  67.2 2.9 broadcast_in_dim.21
  70.1 6.6 copy.40
  76.7 50.5 %all-gather.17.cloned.1.call-done = bf16[6144,768]{0,1:T(8,128)(2,1)} async-done(((bf16[1536,768]{0,1:T(8,128)(2,1)}), bf16[6144,768]{0,1:T(8,128)(2,1)}) %all-gather.17.cloned.1.call-update) | async-done | bytes 9437200 | tf_op jit(solution)/shard_map/all_gather | solution.py:24
  127.1 363.6 %all-gather.9.cloned.1.call-done = bf16[1536,6144]{1,0:T(8,128)(2,1)} async-done(((bf16[1536,768]{1,0:T(8,128)(2,1)}), bf16[1536,6144]{1,0:T(8,128)(2,1)}) %all-gather.9.cloned.1.call-update) | async-done | bytes 18874384 | tf_op jit(solution)/shard_map/all_gather | solution.py:27
  490.8 21.3 %fusion.17 = f32[768,1536]{0,1:T(8,128)} fusion(bf16[6144,768]{0,1:T(8,128)(2,1)} %all-gather.17.cloned.1.call-done, bf16[1536,6144]{1,0:T(8,128)(2,1)} %all-gather.9.cloned.1.call-done), kind=kOutput, calls=%fused_computation.50 | convolution fusion | flops 14495514624 | bytes 33030144 | tf_op jit(solution)/shard_map/dot_general | solution.py:31
  512.1 44.9 %all-gather.11.cloned.1.call-done = bf16[6144,768]{1,0:T(8,128)(2,1)} async-done(((bf16[1536,768]{1,0:T(8,128)(2,1)}), bf16[6144,768]{1,0:T(8,128)(2,1)}) %all-gather.11.cloned.1.call-update) | async-done | bytes 9437200 | tf_op jit(solution)/shard_map/all_gather | solution.py:23
  557.0 363.5 %all-gather.19.cloned.1.call-done = bf16[1536,6144]{0,1:T(8,128)(2,1)} async-done(((bf16[1536,768]{0,1:T(8,128)(2,1)}), bf16[1536,6144]{0,1:T(8,128)(2,1)}) %all-gather.19.cloned.1.call-update) | async-done | bytes 18874384 | tf_op jit(solution)/shard_map/all_gather | solution.py:28
  920.5 23.2 %fusion.2 = bf16[1536,768]{1,0:T(8,128)(2,1)} fusion(f32[1536,768]{1,0:T(8,128)} %copy.40, f32[768,1536]{0,1:T(8,128)} %fusion.17, bf16[1536,6144]{0,1:T(8,128)(2,1)} %all-gather.19.cloned.1.call-done, bf16[6144,768]{1,0:T(8,128)(2,1)} %all-gather.11.cloned.1.call-done), kind=kOutput, calls=%fused_computation.6 | convolution fusion | flops 14500233216 | bytes 40108032 | tf_op jit(solution)/shard_map/dot_general | solution.py:32
  943.7 0.3 all-gather.13.cloned.1.call-start
  943.9 0.1 broadcast_bitcast_fusion.2
  944.0 2.8 broadcast_in_dim.19
  946.8 6.1 copy.29
  952.9 23.8 %multiply_convert_fusion = bf16[1536,768]{1,0:T(8,128)(2,1)} fusion(f32[1536,768]{1,0:T(8,128)} %copy.29, bf16[1536,6144]{1,0:T(8,128)(2,1)} %all-gather.9.cloned.1.call-done, bf16[6144,768]{1,0:T(8,128)(2,1)} %all-gather.11.cloned.1.call-done), kind=kOutput, calls=%fused_computation.13 | convolution fusion | flops 14499053568 | bytes 35389440 | tf_op jit(solution)/shard_map/dot_general | solution.py:30
  976.8 0.0 all-gather.15.cloned.1.call-start
  976.8 0.7 all-gather.15.cloned.1.call-update
  977.6 0.7 all-gather.23.cloned.1.call-update
  978.3 30.2 %all-gather.21.cloned.1.call-done = bf16[6144,768]{1,0:T(8,128)(2,1)} async-done(((bf16[1536,768]{1,0:T(8,128)(2,1)}), bf16[6144,768]{1,0:T(8,128)(2,1)}) %all-gather.21.cloned.1.call-update) | async-done | bytes 9437200 | tf_op jit(solution)/shard_map/all_gather | solution.py:24
  1008.4 363.5 %all-gather.13.cloned.1.call-done = bf16[1536,6144]{1,0:T(8,128)(2,1)} async-done(((bf16[1536,768]{1,0:T(8,128)(2,1)}), bf16[1536,6144]{1,0:T(8,128)(2,1)}) %all-gather.13.cloned.1.call-update) | async-done | bytes 18874384 | tf_op jit(solution)/shard_map/all_gather | solution.py:27
  1371.9 21.2 %fusion.18 = f32[1536,768]{1,0:T(8,128)} fusion(bf16[1536,6144]{1,0:T(8,128)(2,1)} %all-gather.13.cloned.1.call-done, bf16[6144,768]{1,0:T(8,128)(2,1)} %all-gather.21.cloned.1.call-done), kind=kOutput, calls=%fused_computation.51 | convolution fusion | flops 14495514624 | bytes 33030144 | tf_op jit(solution)/shard_map/dot_general | solution.py:31
  1393.1 45.0 %all-gather.15.cloned.1.call-done = bf16[6144,768]{1,0:T(8,128)(2,1)} async-done(((bf16[1536,768]{1,0:T(8,128)(2,1)}), bf16[6144,768]{1,0:T(8,128)(2,1)}) %all-gather.15.cloned.1.call-update) | async-done | bytes 9437200 | tf_op jit(solution)/shard_map/all_gather | solution.py:23
  1438.1 22.9 %subtract_multiply_fusion.1 = f32[1536,768]{1,0:T(8,128)} fusion(f32[1536,768]{1,0:T(8,128)} %copy.29, bf16[1536,768]{1,0:T(8,128)(2,1)} %multiply_convert_fusion, bf16[1536,6144]{1,0:T(8,128)(2,1)} %all-gather.13.cloned.1.call-done, bf16[6144,768]{1,0:T(8,128)(2,1)} %all-gather.15.cloned.1.call-done), kind=kOutput, calls=%fused_computation.12 | convolution fusion | flops 14501412864 | bytes 40108032 | tf_op jit(solution)/shard_map/dot_general | solution.py:30
  1461.1 340.7 %all-gather.23.cloned.1.call-done = bf16[1536,6144]{1,0:T(8,128)(2,1)} async-done(((bf16[1536,768]{1,0:T(8,128)(2,1)}), bf16[1536,6144]{1,0:T(8,128)(2,1)}) %all-gather.23.cloned.1.call-update) | async-done | bytes 18874384 | tf_op jit(solution)/shard_map/all_gather | solution.py:28
  1801.8 23.3 %subtract_multiply_fusion = f32[1536,768]{1,0:T(8,128)} fusion(f32[1536,768]{1,0:T(8,128)} %copy.40, f32[1536,768]{1,0:T(8,128)} %fusion.18, bf16[1536,768]{1,0:T(8,128)(2,1)S(1)} %copy-done, bf16[1536,6144]{1,0:T(8,128)(2,1)} %all-gather.23.cloned.1.call-done, bf16[6144,768]{1,0:T(8,128)(2,1)} %all-gather.15.cloned.1.call-done), kind=kOutput, calls=%fused_computation.11 | convolution fusion | flops 14502592512 | bytes 44826624 | tf_op jit(solution)/shard_map/dot_general | solution.py:32
  (17 shorter events, 0.3 us)
Async XLA Ops:
  11.0 14.6 all-to-all-start
  25.6 12.5 all-to-all-start.1
  38.1 10.6 all-to-all-start.2
  40.9 86.2 %all-gather.17.cloned.1.call-start = ((), (), s32[]{:S(2)}) async-start(), calls=%async_computation.7 | async-start | bytes 11796480 | tf_op jit(solution)/shard_map/all_gather | solution.py:24
  64.8 425.9 %all-gather.9.cloned.1.call-start = ((), (), s32[]{:S(2)}) async-start(), calls=%async_computation.3 | async-start | bytes 21233664 | tf_op jit(solution)/shard_map/all_gather | solution.py:27
  65.6 491.4 %all-gather.11.cloned.1.call-start = ((), (), s32[]{:S(2)}) async-start(), calls=%async_computation.4 | async-start | bytes 11796480 | tf_op jit(solution)/shard_map/all_gather | solution.py:23
  66.3 854.1 %all-gather.19.cloned.1.call-start = ((), (), s32[]{:S(2)}) async-start(), calls=%async_computation.8 | async-start | bytes 21233664 | tf_op jit(solution)/shard_map/all_gather | solution.py:28
  66.9 941.5 %all-gather.21.cloned.1.call-start = ((), (), s32[]{:S(2)}) async-start(), calls=%async_computation.9 | async-start | bytes 11796480 | tf_op jit(solution)/shard_map/all_gather | solution.py:24
  943.7 428.3 %all-gather.13.cloned.1.call-start = ((), (), s32[]{:S(2)}) async-start(), calls=%async_computation.5 | async-start | bytes 21233664 | tf_op jit(solution)/shard_map/all_gather | solution.py:27
  976.8 461.4 %all-gather.15.cloned.1.call-start = ((), (), s32[]{:S(2)}) async-start(), calls=%async_computation.6 | async-start | bytes 11796480 | tf_op jit(solution)/shard_map/all_gather | solution.py:23
  977.5 824.2 %all-gather.23.cloned.1.call-start = ((), (), s32[]{:S(2)}) async-start(), calls=%async_computation.10 | async-start | bytes 21233664 | tf_op jit(solution)/shard_map/all_gather | solution.py:28
  1393.1 408.7 %copy-start = (bf16[1536,768]{1,0:T(8,128)(2,1)S(1)}, bf16[1536,768]{1,0:T(8,128)(2,1)}, u32[]{:S(2)}) copy-start(bf16[1536,768]{1,0:T(8,128)(2,1)} %fusion.2) | copy-start | bytes 7077892
Sparse Core Ops, SparseCore 0:
  65.0 62.1 all-gather.16
  128.7 362.0 all-gather.8
  492.3 64.6 all-gather.10
  558.4 362.0 all-gather.18
  943.8 64.6 all-gather.20
  1009.8 362.0 all-gather.12
  1373.5 64.6 all-gather.14
  1439.7 362.0 all-gather.22
where the time goes:
time: 1830 us
  waiting for transfers between devices  1620 us (89%)
  matrix products  136 us (7%)
  local copies, waits for them, and re-layouts  39.4 us (2%)
    all_gather x2, waiting for transfers between devices, products(): lax.all_gather(zeroth, 'col', axis=1, tiled=True)  727 us
    all_gather x2, waiting for transfers between devices, products(): lax.all_gather(linear, 'col', axis=1, tiled=True)  704 us
    all_gather x2, waiting for transfers between devices, products(): lax.all_gather(zeroth, 'row', axis=0, tiled=True)  89.9 us
    all_gather x2, waiting for transfers between devices, products(): lax.all_gather(linear, 'row', axis=0, tiled=True)  80.7 us
    dot_general x2, matrix products, products(): square = jnp.dot(pieces[0], col_zero, preferred_element_type=jnp.float32)  46.8 us
    dot_general x2, matrix products, products(): jnp.dot(pieces[1], col_zero, preferred_element_type=jnp.float32)  46.4 us
    dot_general x2, matrix products, products(): jnp.dot(pieces[0], col_first, preferred_element_type=jnp.float32)  42.5 us
  transfers between devices with their start and end apart: 11, of which 10 were waited for; matrix products, arithmetic and copies ran while one was open for 6% of the time, Pallas kernels for 0%

commit v1 on v0

v1 whole, which is shorter than its diff:
```python
import functools
import math

import jax
import jax.numpy as jnp
from jax import lax
from jax.experimental import pallas as pl
from jax.experimental.pallas import tpu as pltpu
from jax.sharding import PartitionSpec as P

CAPACITY = 2
AXES = ("row", "col")
VMEM_BYTES = 56 * 1024 * 1024
COST_SHARE = 1


class Layout:
    def __init__(self, rows, cols):
        self.rows, self.cols = rows, cols
        self.nx, self.ny = rows // 2, cols // 4

    def index(self, x, k, zh, zl, y):
        return (2 * x + k) * self.cols + (2 * zh + zl) * self.ny + y

    def perm(self, source):
        pairs = []
        for x in range(self.nx):
            for k in range(2):
                for zh in range(2):
                    for zl in range(2):
                        for y in range(self.ny):
                            here = (x, k, zh, zl, y)
                            pairs.append((self.index(*source(*here)), self.index(*here)))
        return pairs

    def send(self, value, source):
        return lax.ppermute(value, AXES, self.perm(source))


def tie(*values):
    return lax.optimization_barrier(values)


class Rounds:
    def __init__(self, lay, **held):
        self.lay, self.held = lay, held

    def run(self, sends, **computed):
        held = dict(self.held, **computed)
        last = {}
        for link, name, source, route in sends:
            value = held[source]
            if link in last:
                value, held[last[link]] = tie(value, held[last[link]])
            held[name] = self.lay.send(value, route)
            last[link] = name
        self.held = dict(zip(held, tie(*held.values())))

    def __getitem__(self, name):
        return self.held[name]


def product(terms, mask, own, base, tile, scale, out_dtype, wait=(), span=None):
    height = sum(v.shape[0] for v in terms[0][0][0])
    width = terms[0][2][0][0].shape[1]
    order = sum(v.shape[0] for unit in terms[0][2] for v in unit)
    block = 128
    first_tile, end_tile = span or (0, height // tile)
    tiles = end_tile - first_tile
    arrays, plan_a, plan_b, places = [], [], [], []
    panels = 0
    for row_units, row_places, col_units, col_places in terms:
        if col_units is not None:
            for unit, place in zip(col_units, col_places):
                tall, first = sum(v.shape[0] for v in unit), 0
                for v in unit:
                    plan_b.append((panels, len(places), tall, first, len(arrays)))
                    arrays.append(v)
                    first += v.shape[0]
                places.append(place)
            panels += 1
        for unit, place in zip(row_units, row_places):
            first, parts = 0, []
            for v in unit:
                parts.append((len(arrays), first // tile, (first + v.shape[0]) // tile))
                arrays.append(v)
                first += v.shape[0]
            plan_a.append((panels - 1, len(places), unit[0].shape[1], parts))
            places.append(place)
    places = jnp.stack([jnp.asarray(p, jnp.int32) for p in places])
    count = len(arrays)
    deep = sum(wide for _, _, wide, _ in plan_a)

    def kernel(places_ref, *refs):
        refs = list(refs)
        del refs[: len(wait)]
        mask_ref = refs.pop(0) if mask is not None else None
        operands = [refs.pop(0) for _ in range(count)]
        own_ref = refs.pop(0) if own is not None else None
        base_ref = refs.pop(0) if base is not None else None
        out_ref, a_buf, b_buf, a_sem, b_sem = refs
        step = pl.program_id(0)
        slot = step % 2

        def row_copy(j, at, slot, act):
            offset = sum(wide for _, _, wide, _ in plan_a[:j])
            _, _, wide, parts = plan_a[j]
            for which, low, high in parts:
                if high <= first_tile or low >= end_tile:
                    continue

                def go():
                    start = pl.multiple_of((at - low) * tile, tile)
                    act(
                        pltpu.make_async_copy(
                            operands[which].at[pl.ds(start, tile), :],
                            a_buf.at[slot, :, pl.ds(offset, wide)],
                            a_sem.at[slot, j],
                        )
                    )

                if low <= first_tile and high >= end_tile:
                    go()
                else:
                    pl.when((at >= low) & (at < high))(go)

        def col_copy(j, act):
            panel, place, tall, first, which = plan_b[j]
            offset = pl.multiple_of(places_ref[place] * tall + first, 128)
            rows = pl.ds(offset, arrays[which].shape[0])
            act(pltpu.make_async_copy(operands[which], b_buf.at[panel, rows, :], b_sem.at[j]))

        @pl.when(step == 0)
        def _():
            for j in range(len(plan_b)):
                col_copy(j, lambda c: c.start())
            for j in range(len(plan_a)):
                row_copy(j, first_tile, 0, lambda c: c.start())

        @pl.when(step + 1 < tiles)
        def _():
            for j in range(len(plan_a)):
                row_copy(j, first_tile + step + 1, (step + 1) % 2, lambda c: c.start())

        @pl.when(step == 0)
        def _():
            for j in range(len(plan_b)):
                col_copy(j, lambda c: c.wait())

        for j in range(len(plan_a)):
            row_copy(j, first_tile + step, slot, lambda c: c.wait())
        total = None
        offset = 0
        for panel, place, wide, _ in plan_a:
            if wide == order:
                right = b_buf[panel]
            else:
                right = b_buf[panel, pl.ds(pl.multiple_of(places_ref[place] * wide, 128), wide), :]
            part = jnp.dot(a_buf[slot, :, offset : offset + wide], right, preferred_element_type=jnp.float32)
            total = part if total is None else total + part
            offset += wide
        if base is not None:
            total = total + base_ref[...]
        if mask is None:
            out_ref[...] = total
            return
        for i in range(tile // block):
            for j in range(width // block):
                at = (pl.ds(i * block, block), pl.ds(j * block, block))
                value = total[i * block : (i + 1) * block, j * block : (j + 1) * block] * scale
                if own is not None:
                    value = 2.0 * own_ref[at].astype(jnp.float32) - value
                kept = mask_ref[(first_tile + step) * (tile // block) + i, j]
                out_ref[at] = (value * kept).astype(out_dtype)

    smem = pl.BlockSpec(memory_space=pltpu.SMEM)
    tiled = pl.BlockSpec((tile, width), lambda i: (first_tile + i, 0))
    in_specs, operands = [smem], [places]
    in_specs, operands = in_specs + [pl.BlockSpec(memory_space=pl.ANY)] * len(wait), operands + list(wait)
    if mask is not None:
        in_specs, operands = in_specs + [smem], operands + [mask]
    in_specs = in_specs + [pl.BlockSpec(memory_space=pl.ANY)] * count
    operands = operands + arrays
    for extra in (own, base):
        if extra is not None:
            in_specs, operands = in_specs + [tiled], operands + [extra]
    return pl.pallas_call(
        kernel,
        grid=(tiles,),
        out_shape=jax.ShapeDtypeStruct((tiles * tile, width), out_dtype),
        in_specs=in_specs,
        out_specs=pl.BlockSpec((tile, width), lambda i: (i, 0)),
        scratch_shapes=[
            pltpu.VMEM((2, tile, deep), jnp.bfloat16),
            pltpu.VMEM((panels, order, width), jnp.bfloat16),
            pltpu.SemaphoreType.DMA((2, len(plan_a))),
            pltpu.SemaphoreType.DMA((len(plan_b),)),
        ],
        compiler_params=pltpu.CompilerParams(
            dimension_semantics=("arbitrary",), vmem_limit_bytes=VMEM_BYTES
        ),
        cost_estimate=pl.CostEstimate(
            flops=2 * tiles * tile * width * deep // COST_SHARE,
            bytes_accessed=(2 * deep * height + 2 * panels * order * width + 4 * height * width) // COST_SHARE,
            transcendentals=0,
        ),
    )(*operands)


def field_panel(strips, tables, pattern, slabs, first, stride, block_row, block_col, height, width, along_rows):
    block = strips.shape[1]
    atom_width = 8
    senders, slots = tables.shape[1], tables.shape[2]
    sent = strips.shape[0] // senders
    scalars = jnp.stack([jnp.asarray(v, jnp.int32) for v in (block_row, block_col, first)])
    tall, wide = height // block, width // block

    def kernel(scalar_ref, table_ref, pattern_ref, strips_ref, out_ref, field):
        step = pl.program_id(0)
        owner = (scalar_ref[2] + step * stride) * CAPACITY
        field[...] = jnp.zeros(field.shape, field.dtype)

        def one(sender, carry):
            for rank in range(CAPACITY):
                source = table_ref[0, sender, owner + rank]

                @pl.when(source >= 0)
                def _():
                    pair = lax.div(source, 2)
                    start = pl.multiple_of(sender * sent + pair * (2 * atom_width), 2 * atom_width)
                    both = strips_ref[pl.ds(start, 2 * atom_width), :].astype(jnp.float32)
                    strip = jnp.where(source > 2 * pair, both[atom_width:], both[:atom_width])
                    row = pl.multiple_of(table_ref[1, sender, owner + rank] * atom_width, atom_width)
                    col = pl.multiple_of(table_ref[2, sender, owner + rank] * block, block)
                    at = (pl.ds(row, atom_width), pl.ds(col, block))
                    field[at] = field[at] + strip

            return carry

        lax.fori_loop(0, senders, one, 0)
        first_row = scalar_ref[0] + (0 if along_rows else step * tall)
        first_col = scalar_ref[1] + (step * wide if along_rows else 0)
        for i in range(tall):
            for j in range(wide):
                at = (pl.ds(i * block, block), pl.ds(j * block, block))
                row, col = first_row + i, first_col + j
                kept = jnp.where((pattern_ref[row, col] > 0) | (row == col), -1.0, 0.0)
                out_ref[at] = (field[at] * kept).astype(out_ref.dtype)

    smem = pl.BlockSpec(memory_space=pltpu.SMEM)
    if along_rows:
        shape, out_spec = (height, slabs * width), pl.BlockSpec((height, width), lambda s: (0, s))
    else:
        shape, out_spec = (slabs * height, width), pl.BlockSpec((height, width), lambda s: (s, 0))
    return pl.pallas_call(
        kernel,
        grid=(slabs,),
        out_shape=jax.ShapeDtypeStruct(shape, jnp.bfloat16),
        in_specs=[smem, smem, smem, pl.BlockSpec(strips.shape, lambda s: (0, 0), pipeline_mode=pl.Buffered(1))],
        out_specs=out_spec,
        scratch_shapes=[pltpu.VMEM((height, width), jnp.float32)],
        compiler_params=pltpu.CompilerParams(
            dimension_semantics=("arbitrary",), vmem_limit_bytes=VMEM_BYTES
        ),
        cost_estimate=pl.CostEstimate(
            flops=slabs * height * width * 8, bytes_accessed=slabs * height * width * 8, transcendentals=0
        ),
    )(scalars, tables, pattern, strips)


def gather_strips(strips, targets, atoms, blocks, devices):
    count, atom_width, block = strips.shape
    matches = targets[:, None] == lax.iota(jnp.int32, devices)[None, :]
    before = jnp.cumsum(matches.astype(jnp.int32), axis=0) - 1
    lists = []
    for value in (lax.iota(jnp.int32, count), atoms, blocks):
        picked = [
            jnp.max(jnp.where(matches & (before == rank), value[:, None], -1), axis=0) for rank in range(CAPACITY)
        ]
        lists.append(jnp.stack(picked, axis=1).reshape(-1))
    table = jnp.stack(lists)
    slots = devices * CAPACITY
    lines = -(-3 * slots // block)
    lines = -(-lines // 16) * 16
    table = jnp.pad(table.reshape(-1), (0, lines * block - 3 * slots)).reshape(lines, block)
    sent = jnp.concatenate([strips.reshape(count * atom_width, block), table.astype(strips.dtype)])
    rows = sent.shape[0]
    all_sent = lax.all_gather(sent, AXES, axis=0, tiled=True)
    tables = all_sent.reshape(devices, rows, block)[:, count * atom_width :]
    tables = tables.astype(jnp.int32).reshape(devices, -1)[:, : 3 * slots]
    return all_sent, tables.reshape(devices, 3, slots).transpose(1, 0, 2)


def kept_blocks(pattern, first_row, first_col, tall, wide):
    window = lax.dynamic_slice(pattern, (first_row, first_col), (tall, wide))
    rows = first_row + lax.iota(jnp.int32, tall)
    cols = first_col + lax.iota(jnp.int32, wide)
    return jnp.maximum(window, (rows[:, None] == cols[None, :]).astype(jnp.int32)).astype(jnp.float32)


def on_device(density, strips, dest_device, atom_slot, block_slot, patterns):
    height, width = density.shape
    lay = Layout(lax.axis_size("row"), lax.axis_size("col"))
    nx, ny = lay.nx, lay.ny
    devices = lay.rows * lay.cols
    order = height * lay.rows
    block = strips.shape[2]
    tall, wide = height // block, width // block
    tile = 256
    inv_root = 1.0 / math.sqrt(order)

    row, col = lax.axis_index("row"), lax.axis_index("col")
    x, k = row // 2, row % 2
    zh, zl, y = col // (2 * ny), (col // ny) % 2, col % ny
    my_row = 2 * x + zl
    my_col = (2 * zh + k) * ny + y
    own_places = [(2 * zh + b) * ny + (y + s) % ny for b in (k, 1 - k) for s in range(ny)]
    far_places = [(2 * (1 - zh) + b) * ny + (y + s) % ny for b in (k, 1 - k) for s in range(ny)]
    row_places = own_places + far_places
    col_places = [2 * ((x + s) % nx) + b for b in (zl, 1 - zl) for s in range(nx)]
    kept_zero = kept_blocks(patterns[0], my_row * tall, my_col * wide, tall, wide)
    kept_first = kept_blocks(patterns[1], my_row * tall, my_col * wide, tall, wide)

    to_x = lambda x, k, zh, zl, y: ((x + 1) % nx, k, zh, zl, y)
    to_y = lambda x, k, zh, zl, y: (x, k, zh, zl, (y + 1) % ny)
    to_core = lambda x, k, zh, zl, y: (x, 1 - k, zh, zl, y)
    to_zh = lambda x, k, zh, zl, y: (x, k, 1 - zh, zl, y)
    to_zl = lambda x, k, zh, zl, y: (x, k, zh, 1 - zl, y)
    swap = lambda x, k, zh, zl, y: (x, zl, zh, k, y)

    def cut(v, *heights):
        ends = [0]
        for h in heights:
            ends.append(ends[-1] + h)
        return [v[p:q] for p, q in zip(ends, ends[1:])]

    def partial(rows, places, cols, col_places, base=None, wait=()):
        return product([(rows, places, cols, col_places)], None, None, base, tile, 1.0, jnp.float32, wait)

    def finish(terms, kept, own, base, wait=(), span=None):
        return product(terms, kept, own, base, tile, inv_root, jnp.bfloat16, wait, span)

    half = height // tile // 2 * tile
    most = height // tile * 2 // 3 * tile

    def along_x(unit):
        return [unit] + [f"{unit}_x{s}" for s in range(1, nx)]

    def along_y(unit):
        return [unit] + [f"{unit}_y{s}" for s in range(1, ny)]

    def sends_x(*units):
        return [("x", b, a, to_x) for u in units for a, b in zip(along_x(u), along_x(u)[1:])]

    def sends_y(*units):
        return [("y", b, a, to_y) for u in units for a, b in zip(along_y(u), along_y(u)[1:])]

    def sends_core(*units):
        return [("core", u + "_k", u, to_core) for u in units]

    def rest_core(*units):
        return sends_core(*[u for unit in units for u in along_y(unit)[1:]])

    def rows_of(*chunks):
        units = [list(unit) for unit in zip(*[along_y(u) for u in chunks])]
        units = units + [[u + "_k" for u in unit] for unit in units]
        return [[r[u] for u in unit] for unit in units]

    def cols_of(*chunks):
        return [[r[u] for u in unit] for unit in zip(*[along_x(u) for u in chunks])]

    r = Rounds(lay)
    v0, v1 = cut(density, half, height - half)
    r.held = dict(density=density, v0=v0, v1=v1)
    from_far = lambda x, k, zh, zl, y: (x, zl, 1 - zh, k, y)
    from_beside = lambda x, k, zh, zl, y: (x, 1 - zl, zh, k, y)
    r.run([("zh", "f0", "v0", from_far), ("zl", "own", "density", swap)])
    all_strips, tables = gather_strips(strips, dest_device[:, 0], atom_slot, block_slot, devices)
    r.run(
        [("zh", "f1", "v1", from_far), ("zl", "zl", "density", from_beside)]
        + sends_x("own")
        + sends_y("own")
        + sends_core("own")
    )
    r.run(sends_x("zl") + sends_y("f0", "f1") + rest_core("own") + sends_core("f0", "f1") + rest_core("f0"))
    zero_cols = cols_of("own") + cols_of("zl")
    base = partial(rows_of("own"), own_places, zero_cols, col_places)
    r.run(rest_core("f1"), base=base)
    zero_cols = cols_of("own") + cols_of("zl")
    far_rows = rows_of("f0", "f1")
    old_rows = rows_of("own") + far_rows
    zeroth = finish([(far_rows, far_places, zero_cols, col_places)], kept_zero, None, r["base"])

    tables, zeroth = tie(tables, zeroth)
    field_cols = field_panel(
        all_strips, tables, patterns[2], lay.rows, my_col, lay.cols, 0, my_col * wide, height, width, False
    )
    field_rows = field_panel(
        all_strips, tables, patterns[2], lay.cols, my_row * lay.cols, 1, my_row * tall, 0, height, width, True
    )

    def start(v, tag):
        one, two = cut(v, most, height - most)
        return {"own" + tag: v, "v0" + tag: one, "v1" + tag: two}

    def first_sends(tag):
        return (
            [("zh", "f0" + tag, "v0" + tag, to_zh), ("zl", "z0" + tag, "v0" + tag, to_zl)]
            + sends_x("own" + tag)
            + sends_y("own" + tag)
            + sends_core("own" + tag)
        )

    def second_sends(tag):
        return (
            [("zh", "f1" + tag, "v1" + tag, to_zh), ("zl", "z1" + tag, "v1" + tag, to_zl)]
            + sends_x("z0" + tag)
            + sends_y("f0" + tag)
            + rest_core("own" + tag)
            + sends_core("f0" + tag)
        )

    def third_sends(tag):
        return sends_x("z1" + tag) + sends_y("f1" + tag) + sends_core("f1" + tag) + rest_core("f0" + tag)

    def col_panel(tag):
        return cols_of("own" + tag) + cols_of("z0" + tag, "z1" + tag)

    r = Rounds(lay)
    r.held = start(zeroth, "p")
    first = partial(old_rows, row_places, [[field_cols]], [0], None, (zeroth,))
    linear = finish([([[field_rows]], [0], zero_cols, col_places)], kept_first, None, first)
    r.run(first_sends("p"), linear=linear)
    r.run(second_sends("p"))
    r.held.update(start(r["linear"], "q"))
    r.run(third_sends("p") + rest_core("f1p") + first_sends("q"))
    zero_rows = rows_of("ownp") + rows_of("f0p", "f1p")
    new_zeroth = finish([(zero_rows, row_places, col_panel("p"), col_places)], kept_zero, r["ownp"], None)
    r.run(second_sends("q"), new_zeroth=new_zeroth)
    base = partial(rows_of("ownq"), own_places, col_panel("p"), col_places)
    r.run([("zl", "back", "new_zeroth", swap)] + third_sends("q"), base=base)
    zero_rows = rows_of("ownp") + rows_of("f0p", "f1p")
    spans = ((0, most // tile), (most // tile, height // tile))

    def last(far_rows, base, span):
        terms = [
            (zero_rows, row_places, col_panel("q"), col_places),
            (far_rows, far_places, col_panel("p"), col_places),
        ]
        return finish(terms, kept_first, r["ownq"], base, (), span)

    far_rows = rows_of("f0q")
    top = last(far_rows, r["base"], spans[0])
    r.run(rest_core("f1q"), top=top)
    back_top = lay.send(r["top"], swap)
    bottom = last(rows_of("f0q", "f1q"), r["base"], spans[1])
    back_bottom = lay.send(bottom, swap)
    new_linear = jnp.concatenate([back_top, back_bottom]).astype(jnp.float32)
    return (r["back"].astype(jnp.float32), new_linear)


def solution(mesh):
    return jax.shard_map(
        on_device,
        mesh=mesh,
        in_specs=(
            P("row", "col"),
            P(("row", "col"), None, None),
            P(("row", "col"), None),
            P(("row", "col")),
            P(("row", "col")),
            P(),
        ),
        out_specs=(P("row", "col"), P("row", "col")),
        check_vma=False,
    )
```

time: 1830 us -> 606 us (0.33)
  waiting for transfers between devices: 1620 us -> 309 us
  Pallas kernels: 0 us -> 190 us
  matrix products: 136 us -> 0 us
  starting transfers between devices: 16.5 us -> 60.1 us
    all_gather x8 -> x1, waiting for transfers between devices: 1600 us -> 0.01 us  [gather_strips(): all_sent = lax.all_gather(sent, AXES, axis=0, tiled=True)]
    ppermute x0 -> x50, waiting for transfers between devices: none -> 309 us  [send(): return lax.ppermute(value, AXES, self.perm(source))]
    pallas_call x0 -> x10, Pallas kernels: none -> 190 us  [the longest x8 161 us: product(): pl.pallas_call(kernel, grid=(tiles,), out_shape=jax.ShapeDtypeStruct((til...]
    dot_general x7 -> x0, matrix products: 136 us -> none  [the longest x2 46.8 us: products(): square = jnp.dot(pieces[0], col_zero, preferred_element_type=jnp.float32)]
    ppermute x0 -> x50, starting transfers between devices: none -> 60.1 us  [send(): return lax.ppermute(value, AXES, self.perm(source))]
    reshape x3 -> x1, local copies, waits for them, and re-layouts: 18.7 us -> 0.08 us  [gather_strips(): table.reshape(-1)]
  transfers between devices with their start and end apart: 11 -> 51, of which waited for: 10 -> 22; matrix products, arithmetic and copies ran while one was open for 6% -> 3% of each run, Pallas kernels for 0% -> 29%
where the time goes in v1:
time: 606 us; the launch traced here: 604 us
  waiting for transfers between devices  309 us (51%)
  Pallas kernels  190 us (31%)
  starting transfers between devices  60.1 us (10%)
  local copies, waits for them, and re-layouts  22.8 us (4%)
  between operations  14.6 us (2%)
  other arithmetic  7.4 us (1%)
    ppermute x50, waiting for transfers between devices, send(): return lax.ppermute(value, AXES, self.perm(source))  309 us
    pallas_call x8, Pallas kernels, product(): pl.pallas_call(kernel, grid=(tiles,), out_shape=jax.ShapeDtypeStruct((til...  161 us
    ppermute x50, starting transfers between devices, send(): return lax.ppermute(value, AXES, self.perm(source))  60.1 us
    pallas_call x2, Pallas kernels, field_panel(): pl.pallas_call(kernel, grid=(slabs,), out_shape=jax.ShapeDtypeStruct(shap...  29 us
  transfers between devices with their start and end apart: 51, of which 22 were waited for; matrix products, arithmetic and copies ran while one was open for 3% of the time, Pallas kernels for 29%

profile of v1, /device:TPU:1, one launch (start us, length us, event | category | flops | bytes accessed | tf_op | source)
XLA Modules:
  0.0 604.2 jit_solution(9500950098960625348)
XLA Ops:
  7.3 4.7 collective-permute-start.1
  12.0 1.8 fusion.5
  13.8 2.1 collective-permute-start
  15.9 50.2 %collective-permute-done.refs_5_.refs_6_ = bf16[768,768]{1,0:T(8,128)(2,1)S(1)} collective-permute-done((bf16[768,768]{1,0:T(8,128)(2,1)S(1)}, bf16[768,768]{1,0:T(8,128)(2,1)S(1)}, u32[]{:S(2)}, u32[]{:S(2)}) %collective-permute-start) | collective-permute-done | bytes 1179680 | tf_op jit(solution)/shard_map/ppermute | solution.py:37
  66.1 1.0 copy-done.30
  67.2 1.3 collective-permute-start.3
  69.4 1.5 collective-permute-start.5
  70.9 1.2 collective-permute-start.4
  72.1 2.3 collective-permute-start.2
  74.4 27.9 %collective-permute-done.2.refs_6_.refs_7_ = bf16[768,768]{1,0:T(8,128)(2,1)S(1)} collective-permute-done((bf16[768,768]{1,0:T(8,128)(2,1)S(1)}, bf16[768,768]{1,0:T(8,128)(2,1)S(1)}, u32[]{:S(2)}, u32[]{:S(2)}) %collective-permute-start.2) | collective-permute-done | bytes 1179680 | tf_op jit(solution)/shard_map/ppermute | solution.py:37
  102.3 16.1 %collective-permute-done.3.refs_2_.refs_3_ = bf16[1536,768]{1,0:T(8,128)(2,1)S(1)} collective-permute-done((bf16[1536,768]{1,0:T(8,128)(2,1)S(1)}, bf16[1536,768]{1,0:T(8,128)(2,1)S(1)}, u32[]{:S(2)}, u32[]{:S(2)}) %collective-permute-start.3) | collective-permute-done | bytes 2359328 | tf_op jit(solution)/shard_map/ppermute | solution.py:37
  118.3 4.2 collective-permute-done.5.refs_5_.refs_3_
  123.5 2.5 collective-permute-start.10
  127.8 2.5 collective-permute-done.10.refs_7_.refs_5_
  131.2 2.6 collective-permute-done.11.refs_9_.refs_10_
  134.4 25.9 %collective-permute-done.8.refs_7_.refs_8_ = bf16[768,768]{1,0:T(8,128)(2,1)} collective-permute-done((bf16[768,768]{1,0:T(8,128)(2,1)}, bf16[768,768]{1,0:T(8,128)(2,1)}, u32[]{:S(2)}, u32[]{:S(2)}) %collective-permute-start.8) | collective-permute-done | bytes 1179680 | tf_op jit(solution)/shard_map/ppermute | solution.py:37
  160.6 1.1 collective-permute-start.13
  163.0 28.2 %collective-permute-done.9.refs_8_.refs_9_ = bf16[768,768]{1,0:T(8,128)(2,1)} collective-permute-done((bf16[768,768]{1,0:T(8,128)(2,1)}, bf16[768,768]{1,0:T(8,128)(2,1)}, u32[]{:S(2)}, u32[]{:S(2)}) %collective-permute-start.9) | collective-permute-done | bytes 1179680 | tf_op jit(solution)/shard_map/ppermute | solution.py:37
  191.2 2.5 collective-permute-done.7.refs_3_.refs_4_
  199.6 15.3 %shard_map.77.refs_13_ = f32[1536,768]{1,0:T(8,128)} custom-call(s32[8]{0:T(128)} %stack.101.places_ref, bf16[1536,768]{1,0:T(8,128)(2,1)} %copy-done.22, bf16[1536,768]{1,0:T(8,128)(2,1)} %copy-done.24, bf16[1536,768]{1,0:T(8,128)(2,1)} %copy-done.23, bf16[1536,768]{1,0:T(8,128)(2,1)} %collective-permute-done.7.refs_3_.refs_4_, ...), custom_call_target="tpu_custom_call" | custom-call | flops 7247757312 | bytes 23592960 | tf_op jit(solution)/shard_map/pallas_call | solution.py:187
  215.0 15.6 %shard_map.78.refs_0_.refs_1_.refs_7_.refs_19_ = bf16[1536,768]{1,0:T(8,128)(2,1)} custom-call(s32[8]{0:T(128)} %stack.96.places_ref, f32[12,6]{1,0:T(8,128)} %get-tuple-element.410.refs_0_, bf16[1536,768]{1,0:T(8,128)(2,1)} %copy-done.22, bf16[1536,768]{1,0:T(8,128)(2,1)} %copy-done.24, bf16[1536,768]{1,0:T(8,128)(2,1)} %copy-done.23, ...), custom_call_target="tpu_custom_call" | custom-call | flops 7247757312 | bytes 23592960 | tf_op jit(solution)/shard_map/pallas_call | solution.py:187
  230.6 2.7 slice.40
  233.2 1.5 collective-permute-start.15
  235.8 10.9 %shard_map.80.refs_1_ = bf16[6144,768]{1,0:T(8,128)(2,1)} custom-call(s32[3]{0:T(128)} %get-tuple-element.421.scalar_ref, s32[3,32,64]{2,1,0:T(8,128)} %bitcast.50, s32[48,48]{1,0:T(8,128)} %get-tuple-element.404.pattern_ref, bf16[8704,128]{1,0:T(8,128)(2,1)} %all-gather.2.cloned.1.call-done.strips_ref), custom_call_target="tpu_custom_call" | custom-call | flops 37748736 | bytes 37748736 | tf_op jit(solution)/shard_map/pallas_call | solution.py:255
  246.7 23.4 %shard_map.81.refs_6_ = f32[1536,768]{1,0:T(8,128)} custom-call(s32[9]{0:T(128)} %stack.106.places_ref, bf16[1536,768]{1,0:T(8,128)(2,1)} %shard_map.78.refs_0_.refs_1_.refs_7_.refs_19_, bf16[6144,768]{1,0:T(8,128)(2,1)} %shard_map.80.refs_1_, bf16[1536,768]{1,0:T(8,128)(2,1)} %copy-done.22, bf16[1536,768]{1,0:T(8,128)(2,1)} %collective-permute-done.5.refs_5_.refs_3_, ...), custom_call_target="tpu_custom_call" | custom-call | flops 14495514624 | bytes 33030144 | tf_op jit(solution)/shard_map/pallas_call | solution.py:187
  270.1 1.2 slice.41
  271.3 18.1 %shard_map.79.refs_5_ = bf16[1536,6144]{1,0:T(8,128)(2,1)} custom-call(s32[3]{0:T(128)} %get-tuple-element.420.scalar_ref, s32[3,32,64]{2,1,0:T(8,128)} %bitcast.51, s32[48,48]{1,0:T(8,128)} %get-tuple-element.404.pattern_ref, bf16[8704,128]{1,0:T(8,128)(2,1)} %all-gather.2.cloned.1.call-done.strips_ref), custom_call_target="tpu_custom_call" | custom-call | flops 75497472 | bytes 75497472 | tf_op jit(solution)/shard_map/pallas_call | solution.py:255
  289.4 22.6 %shard_map.82.refs_6_.refs_1_.refs_29_.refs_33_ = bf16[1536,768]{1,0:T(8,128)(2,1)} custom-call(s32[5]{0:T(128)} %stack.102.places_ref, f32[12,6]{1,0:T(8,128)} %get-tuple-element.409.refs_0_, bf16[1536,768]{1,0:T(8,128)(2,1)} %copy-done.22, bf16[1536,768]{1,0:T(8,128)(2,1)} %copy-done.24, bf16[1536,768]{1,0:T(8,128)(2,1)} %copy-done.23, ...), custom_call_target="tpu_custom_call" | custom-call | flops 14495514624 | bytes 33030144 | tf_op jit(solution)/shard_map/pallas_call | solution.py:187
  312.4 1.5 collective-permute-start.22
  313.9 1.3 collective-permute-start.23
  315.2 1.5 collective-permute-done.24.refs_10_
  316.7 1.4 copy-done.3
  318.4 1.3 collective-permute-start.21
  319.6 1.8 collective-permute-start.20
  321.4 31.9 %collective-permute-done.21.refs_4_.refs_3_.refs_22_ = bf16[512,768]{1,0:T(8,128)(2,1)S(1)} collective-permute-done((bf16[512,768]{1,0:T(8,128)(2,1)S(1)}, bf16[512,768]{1,0:T(8,128)(2,1)S(1)}, u32[]{:S(2)}, u32[]{:S(2)}) %collective-permute-start.21) | collective-permute-done | bytes 786464 | tf_op jit(solution)/shard_map/ppermute | solution.py:37
  353.4 4.1 collective-permute-start.28
  357.5 2.0 collective-permute-done.28.refs_16_
  360.6 1.0 collective-permute-start.26
  361.6 17.3 %collective-permute-done.27.refs_14_ = bf16[512,768]{1,0:T(8,128)(2,1)S(1)} collective-permute-done((bf16[512,768]{1,0:T(8,128)(2,1)S(1)}, bf16[512,768]{1,0:T(8,128)(2,1)S(1)}, u32[]{:S(2)}, u32[]{:S(2)}) %collective-permute-start.27) | collective-permute-done | bytes 786464 | tf_op jit(solution)/shard_map/ppermute | solution.py:37
  382.8 1.5 collective-permute-start.35
  384.3 1.5 slice.44
  385.9 2.3 collective-permute-start.31
  388.2 2.1 slice.45
  390.3 65.1 %collective-permute-done.32.refs_3_ = bf16[1024,768]{1,0:T(8,128)(2,1)} collective-permute-done((bf16[1024,768]{1,0:T(8,128)(2,1)S(1)}, bf16[1024,768]{1,0:T(8,128)(2,1)}, u32[]{:S(2)}, u32[]{:S(2)}) %collective-permute-start.32) | collective-permute-done | bytes 1572896 | tf_op jit(solution)/shard_map/ppermute | solution.py:37
  455.4 2.2 collective-permute-start.40
  458.0 1.3 collective-permute-start.39
  459.3 2.4 collective-permute-done.40.refs_9_
  461.8 1.4 copy-done.29
  464.2 2.4 collective-permute-start.36
  466.6 23.8 %shard_map.83 = bf16[1536,768]{1,0:T(8,128)(2,1)} custom-call(s32[12]{0:T(128)} %stack.110.places_ref, f32[12,6]{1,0:T(8,128)} %get-tuple-element.410.refs_0_, bf16[1536,768]{1,0:T(8,128)(2,1)} %shard_map.78.refs_0_.refs_1_.refs_7_.refs_19_, bf16[1536,768]{1,0:T(8,128)(2,1)} %copy-done.2, bf16[1024,768]{1,0:T(8,128)(2,1)} %collective-permute-done.16.refs_3_.refs_2_.refs_21_, ...), custom_call_target="tpu_custom_call" | custom-call | flops 14495514624 | bytes 33030144 | tf_op jit(solution)/shard_map/pallas_call | solution.py:187
  490.4 9.7 %collective-permute-done.37.refs_4_ = bf16[512,768]{1,0:T(8,128)(2,1)} collective-permute-done((bf16[512,768]{1,0:T(8,128)(2,1)}, bf16[512,768]{1,0:T(8,128)(2,1)}, u32[]{:S(2)}, u32[]{:S(2)}) %collective-permute-start.37) | collective-permute-done | bytes 786464 | tf_op jit(solution)/shard_map/ppermute | solution.py:37
  500.2 1.1 copy-done.8
  501.8 2.2 collective-permute-start.45
  504.0 1.9 collective-permute-start.42
  508.5 15.1 %shard_map.84.refs_30_.refs_34_ = f32[1536,768]{1,0:T(8,128)} custom-call(s32[8]{0:T(128)} %stack.101.places_ref, bf16[1536,768]{1,0:T(8,128)(2,1)} %shard_map.78.refs_0_.refs_1_.refs_7_.refs_19_, bf16[1536,768]{1,0:T(8,128)(2,1)} %copy-done.2, bf16[1024,768]{1,0:T(8,128)(2,1)} %collective-permute-done.16.refs_3_.refs_2_.refs_21_, ...), custom_call_target="tpu_custom_call" | custom-call | flops 7247757312 | bytes 23592960 | tf_op jit(solution)/shard_map/pallas_call | solution.py:187
  523.6 2.3 collective-permute-done.43.refs_6_
  526.1 8.3 %collective-permute-done.42 = bf16[1536,768]{1,0:T(8,128)(2,1)S(1)} collective-permute-done((bf16[1536,768]{1,0:T(8,128)(2,1)}, bf16[1536,768]{1,0:T(8,128)(2,1)S(1)}, u32[]{:S(2)}, u32[]{:S(2)}) %collective-permute-start.42) | collective-permute-done | bytes 2359328 | tf_op jit(solution)/shard_map/ppermute | solution.py:37
  534.4 27.0 %shard_map.85 = bf16[1024,768]{1,0:T(8,128)(2,1)} custom-call(s32[20]{0:T(128)} %stack.111.places_ref, f32[12,6]{1,0:T(8,128)} %get-tuple-element.409.refs_0_, bf16[1536,768]{1,0:T(8,128)(2,1)} %shard_map.82.refs_6_.refs_1_.refs_29_.refs_33_, bf16[1536,768]{1,0:T(8,128)(2,1)} %collective-permute-done.33.refs_2_, ...), custom_call_target="tpu_custom_call" | custom-call | flops 14495514624 | bytes 51904512 | tf_op jit(solution)/shard_map/pallas_call | solution.py:187
  561.4 1.9 collective-permute-start.48
  563.3 18.0 %shard_map.86 = bf16[512,768]{1,0:T(8,128)(2,1)} custom-call(s32[20]{0:T(128)} %stack.111.places_ref, f32[12,6]{1,0:T(8,128)} %get-tuple-element.409.refs_0_, bf16[1536,768]{1,0:T(8,128)(2,1)} %shard_map.82.refs_6_.refs_1_.refs_29_.refs_33_, bf16[1536,768]{1,0:T(8,128)(2,1)} %collective-permute-done.33.refs_2_, ...), custom_call_target="tpu_custom_call" | custom-call | flops 7247757312 | bytes 51904512 | tf_op jit(solution)/shard_map/pallas_call | solution.py:187
  581.3 3.6 collective-permute-start.49
  584.9 2.5 convert_element_type.29
  587.5 7.3 %collective-permute-done.49 = bf16[512,768]{1,0:T(8,128)(2,1)S(1)} collective-permute-done((bf16[512,768]{1,0:T(8,128)(2,1)}, bf16[512,768]{1,0:T(8,128)(2,1)S(1)}, u32[]{:S(2)}, u32[]{:S(2)}) %collective-permute-start.49) | collective-permute-done | bytes 786464 | tf_op jit(solution)/shard_map/ppermute | solution.py:37
  594.8 2.5 maximum_convert_fusion
  (156 shorter events, 24.2 us)
Async XLA Ops:
  7.2 60.0 %copy-start.4 = (bf16[1536,768]{1,0:T(8,128)(2,1)S(1)}, bf16[1536,768]{1,0:T(8,128)(2,1)}, u32[]{:S(2)}) copy-start(bf16[1536,768]{1,0:T(8,128)(2,1)} %param.6) | copy-start | bytes 7077892
  7.2 118.8 %copy-start.19 = (s32[32,1]{0,1:T(1,128)S(1)}, s32[32,1]{0,1:T(1,128)}, u32[]{:S(2)}) copy-start(s32[32,1]{0,1:T(1,128)} %param.8) | copy-start | bytes 388
  7.2 119.0 %copy-start.20 = (s32[32]{0:T(128)S(1)}, s32[32]{0:T(128)}, u32[]{:S(2)}) copy-start(s32[32]{0:T(128)} %param.10) | copy-start | bytes 388
  7.2 119.0 %copy-start.21 = (s32[32]{0:T(128)S(1)}, s32[32]{0:T(128)}, u32[]{:S(2)}) copy-start(s32[32]{0:T(128)} %param.9) | copy-start | bytes 388
  7.2 119.9 %copy-start.18 = (bf16[32,8,128]{2,1,0:T(8,128)(2,1)S(1)}, bf16[32,8,128]{2,1,0:T(8,128)(2,1)}, u32[]{:S(2)}) copy-start(bf16[32,8,128]{2,1,0:T(8,128)(2,1)} %param.7) | copy-start | bytes 196612
  7.2 155.1 %copy-start.17 = (s32[3,48,48]{2,1,0:T(8,128)S(1)}, s32[3,48,48]{2,1,0:T(8,128)}, u32[]{:S(2)}) copy-start(s32[3,48,48]{2,1,0:T(8,128)} %param.11) | copy-start | bytes 82948
  7.2 190.7 %all-gather.2.cloned.1.call-start = ((), (), s32[]{:S(2)}) async-start(), calls=%async_computation | async-start | bytes 2297856 | tf_op jit(solution)/shard_map/all_gather | solution.py:288
  7.3 58.9 %collective-permute-start.1 = (bf16[1536,768]{1,0:T(8,128)(2,1)}, bf16[1536,768]{1,0:T(8,128)(2,1)S(1)}, u32[]{:S(2)}, u32[]{:S(2)}) collective-permute-start(bf16[1536,768]{1,0:T(8,128)(2,1)} %param.6), channel_id=1, source_target_pairs={{0,0},{1,1},{8,2},{9,3},{4,4},{5,5},{12,6},{13,7},{2,8},{3,9},{10,... | collective-permute-start | bytes 7077896 | tf_op jit(solution)/shard_map/ppermute | solution.py:37
  13.8 52.3 %collective-permute-start = (bf16[768,768]{1,0:T(8,128)(2,1)S(1)}, bf16[768,768]{1,0:T(8,128)(2,1)S(1)}, u32[]{:S(2)}, u32[]{:S(2)}) collective-permute-start(bf16[768,768]{1,0:T(8,128)(2,1)S(1)} %get-tuple-element.403), channel_id=1, source_target_pairs={{4,0},{5,1},{12,2},{13,3},{0,4},{1,5},{8,6},{9,7},{6,8},{7,9},{14,... | collective-permute-start | bytes 3538952 | tf_op jit(solution)/shard_map/ppermute | solution.py:37
  67.2 58.8 %copy-start.22 = (bf16[1536,768]{1,0:T(8,128)(2,1)}, bf16[1536,768]{1,0:T(8,128)(2,1)S(1)}, u32[]{:S(2)}) copy-start(bf16[1536,768]{1,0:T(8,128)(2,1)S(1)} %collective-permute-done.1.refs_0_.refs_4_.refs_1_.refs_2_) | copy-start | bytes 7077892
  67.2 51.1 %collective-permute-start.3 = (bf16[1536,768]{1,0:T(8,128)(2,1)S(1)}, bf16[1536,768]{1,0:T(8,128)(2,1)S(1)}, u32[]{:S(2)}, u32[]{:S(2)}) collective-permute-start(bf16[1536,768]{1,0:T(8,128)(2,1)S(1)} %copy-done.4), channel_id=1, source_target_pairs={{8,0},{9,1},{0,2},{1,3},{12,4},{13,5},{4,6},{5,7},{10,8},{11,9},{2... | collective-permute-start | bytes 7077896 | tf_op jit(solution)/shard_map/ppermute | solution.py:37
  68.5 49.9 %collective-permute-start.6 = (bf16[1536,768]{1,0:T(8,128)(2,1)S(1)}, bf16[1536,768]{1,0:T(8,128)(2,1)S(1)}, u32[]{:S(2)}, u32[]{:S(2)}) collective-permute-start(bf16[1536,768]{1,0:T(8,128)(2,1)S(1)} %collective-permute-done.1.refs_0_.refs_4_.refs_1_.refs_2_), channel_id=1, source_target_pairs={{8,0},{9,1},{10,2},{11,3},{12,4},{13,5},{14,6},{15,7},{0,8},{1,9},... | collective-permute-start | bytes 7077896 | tf_op jit(solution)/shard_map/ppermute | solution.py:37
  69.4 53.1 %collective-permute-start.5 = (bf16[1536,768]{1,0:T(8,128)(2,1)S(1)}, bf16[1536,768]{1,0:T(8,128)(2,1)}, u32[]{:S(2)}, u32[]{:S(2)}) collective-permute-start(bf16[1536,768]{1,0:T(8,128)(2,1)S(1)} %collective-permute-done.1.refs_0_.refs_4_.refs_1_.refs_2_), channel_id=1, source_target_pairs={{1,0},{0,1},{3,2},{2,3},{5,4},{4,5},{7,6},{6,7},{9,8},{8,9},{11,10... | collective-permute-start | bytes 7077896 | tf_op jit(solution)/shard_map/ppermute | solution.py:37
  70.9 52.6 %collective-permute-start.4 = (bf16[1536,768]{1,0:T(8,128)(2,1)S(1)}, bf16[1536,768]{1,0:T(8,128)(2,1)S(1)}, u32[]{:S(2)}, u32[]{:S(2)}) collective-permute-start(bf16[1536,768]{1,0:T(8,128)(2,1)S(1)} %collective-permute-done.1.refs_0_.refs_4_.refs_1_.refs_2_), channel_id=1, source_target_pairs={{16,0},{17,1},{18,2},{19,3},{20,4},{21,5},{22,6},{23,7},{24,8},{25... | collective-permute-start | bytes 7077896 | tf_op jit(solution)/shard_map/ppermute | solution.py:37
  72.1 30.1 %collective-permute-start.2 = (bf16[768,768]{1,0:T(8,128)(2,1)S(1)}, bf16[768,768]{1,0:T(8,128)(2,1)S(1)}, u32[]{:S(2)}, u32[]{:S(2)}) collective-permute-start(bf16[768,768]{1,0:T(8,128)(2,1)S(1)} %get-tuple-element.200), channel_id=1, source_target_pairs={{4,0},{5,1},{12,2},{13,3},{0,4},{1,5},{8,6},{9,7},{6,8},{7,9},{14,... | collective-permute-start | bytes 3538952 | tf_op jit(solution)/shard_map/ppermute | solution.py:37
  123.5 6.8 %collective-permute-start.10 = (bf16[1536,768]{1,0:T(8,128)(2,1)}, bf16[1536,768]{1,0:T(8,128)(2,1)S(1)}, u32[]{:S(2)}, u32[]{:S(2)}) collective-permute-start(bf16[1536,768]{1,0:T(8,128)(2,1)} %collective-permute-done.5.refs_5_.refs_3_), channel_id=1, source_target_pairs={{8,0},{9,1},{10,2},{11,3},{12,4},{13,5},{14,6},{15,7},{0,8},{1,9},... | collective-permute-start | bytes 7077896 | tf_op jit(solution)/shard_map/ppermute | solution.py:37
  130.3 69.3 %copy-start.26 = (bf16[1536,768]{1,0:T(8,128)(2,1)}, bf16[1536,768]{1,0:T(8,128)(2,1)S(1)}, u32[]{:S(2)}) copy-start(bf16[1536,768]{1,0:T(8,128)(2,1)S(1)} %collective-permute-done.10.refs_7_.refs_5_) | copy-start | bytes 7077892
  130.3 3.5 collective-permute-start.11
  131.0 29.4 %collective-permute-start.8 = (bf16[768,768]{1,0:T(8,128)(2,1)}, bf16[768,768]{1,0:T(8,128)(2,1)}, u32[]{:S(2)}, u32[]{:S(2)}) collective-permute-start(bf16[768,768]{1,0:T(8,128)(2,1)} %copy-done.30), channel_id=1, source_target_pairs={{1,0},{0,1},{3,2},{2,3},{5,4},{4,5},{7,6},{6,7},{9,8},{8,9},{11,10... | collective-permute-start | bytes 3538952 | tf_op jit(solution)/shard_map/ppermute | solution.py:37
  133.8 26.8 %collective-permute-start.12 = (bf16[768,768]{1,0:T(8,128)(2,1)}, bf16[768,768]{1,0:T(8,128)(2,1)}, u32[]{:S(2)}, u32[]{:S(2)}) collective-permute-start(bf16[768,768]{1,0:T(8,128)(2,1)} %copy-done.31), channel_id=1, source_target_pairs={{8,0},{9,1},{10,2},{11,3},{12,4},{13,5},{14,6},{15,7},{0,8},{1,9},... | collective-permute-start | bytes 3538952 | tf_op jit(solution)/shard_map/ppermute | solution.py:37
  134.2 59.5 %collective-permute-start.7 = (bf16[1536,768]{1,0:T(8,128)(2,1)}, bf16[1536,768]{1,0:T(8,128)(2,1)}, u32[]{:S(2)}, u32[]{:S(2)}) collective-permute-start(bf16[1536,768]{1,0:T(8,128)(2,1)} %copy-done.23), channel_id=1, source_target_pairs={{16,0},{17,1},{18,2},{19,3},{20,4},{21,5},{22,6},{23,7},{24,8},{25... | collective-permute-start | bytes 7077896 | tf_op jit(solution)/shard_map/ppermute | solution.py:37
  160.4 30.8 %collective-permute-start.9 = (bf16[768,768]{1,0:T(8,128)(2,1)}, bf16[768,768]{1,0:T(8,128)(2,1)}, u32[]{:S(2)}, u32[]{:S(2)}) collective-permute-start(bf16[768,768]{1,0:T(8,128)(2,1)} %copy-done.31), channel_id=1, source_target_pairs={{1,0},{0,1},{3,2},{2,3},{5,4},{4,5},{7,6},{6,7},{9,8},{8,9},{11,10... | collective-permute-start | bytes 3538952 | tf_op jit(solution)/shard_map/ppermute | solution.py:37
  160.6 33.1 %collective-permute-start.13 = (bf16[768,768]{1,0:T(8,128)(2,1)}, bf16[768,768]{1,0:T(8,128)(2,1)}, u32[]{:S(2)}, u32[]{:S(2)}) collective-permute-start(bf16[768,768]{1,0:T(8,128)(2,1)} %collective-permute-done.8.refs_7_.refs_8_), channel_id=1, source_target_pairs={{8,0},{9,1},{10,2},{11,3},{12,4},{13,5},{14,6},{15,7},{0,8},{1,9},... | collective-permute-start | bytes 3538952 | tf_op jit(solution)/shard_map/ppermute | solution.py:37
  193.7 21.3 %collective-permute-start.14 = (bf16[768,768]{1,0:T(8,128)(2,1)}, bf16[768,768]{1,0:T(8,128)(2,1)}, u32[]{:S(2)}, u32[]{:S(2)}) collective-permute-start(bf16[768,768]{1,0:T(8,128)(2,1)} %collective-permute-done.9.refs_8_.refs_9_), channel_id=1, source_target_pairs={{8,0},{9,1},{10,2},{11,3},{12,4},{13,5},{14,6},{15,7},{0,8},{1,9},... | collective-permute-start | bytes 3538952 | tf_op jit(solution)/shard_map/ppermute | solution.py:37
  233.2 78.8 %collective-permute-start.16 = (bf16[1024,768]{1,0:T(8,128)(2,1)}, bf16[1024,768]{1,0:T(8,128)(2,1)}, u32[]{:S(2)}, u32[]{:S(2)}) collective-permute-start(bf16[1024,768]{1,0:T(8,128)(2,1)} %slice.40), channel_id=1, source_target_pairs={{2,0},{3,1},{0,2},{1,3},{6,4},{7,5},{4,6},{5,7},{10,8},{11,9},{8,1... | collective-permute-start | bytes 4718600 | tf_op jit(solution)/shard_map/ppermute | solution.py:37
  233.2 78.8 %collective-permute-start.15 = (bf16[1024,768]{1,0:T(8,128)(2,1)}, bf16[1024,768]{1,0:T(8,128)(2,1)}, u32[]{:S(2)}, u32[]{:S(2)}) collective-permute-start(bf16[1024,768]{1,0:T(8,128)(2,1)} %slice.40), channel_id=1, source_target_pairs={{4,0},{5,1},{6,2},{7,3},{0,4},{1,5},{2,6},{3,7},{12,8},{13,9},{14,... | collective-permute-start | bytes 4718600 | tf_op jit(solution)/shard_map/ppermute | solution.py:37
  234.7 77.3 %collective-permute-start.19 = (bf16[1536,768]{1,0:T(8,128)(2,1)}, bf16[1536,768]{1,0:T(8,128)(2,1)S(1)}, u32[]{:S(2)}, u32[]{:S(2)}) collective-permute-start(bf16[1536,768]{1,0:T(8,128)(2,1)} %shard_map.78.refs_0_.refs_1_.refs_7_.refs_19_), channel_id=1, source_target_pairs={{8,0},{9,1},{10,2},{11,3},{12,4},{13,5},{14,6},{15,7},{0,8},{1,9},... | collective-permute-start | bytes 7077896 | tf_op jit(solution)/shard_map/ppermute | solution.py:37
  235.3 76.7 %collective-permute-start.18 = (bf16[1536,768]{1,0:T(8,128)(2,1)}, bf16[1536,768]{1,0:T(8,128)(2,1)S(1)}, u32[]{:S(2)}, u32[]{:S(2)}) collective-permute-start(bf16[1536,768]{1,0:T(8,128)(2,1)} %shard_map.78.refs_0_.refs_1_.refs_7_.refs_19_), channel_id=1, source_target_pairs={{1,0},{0,1},{3,2},{2,3},{5,4},{4,5},{7,6},{6,7},{9,8},{8,9},{11,10... | collective-permute-start | bytes 7077896 | tf_op jit(solution)/shard_map/ppermute | solution.py:37
  235.6 76.5 %collective-permute-start.17 = (bf16[1536,768]{1,0:T(8,128)(2,1)}, bf16[1536,768]{1,0:T(8,128)(2,1)S(1)}, u32[]{:S(2)}, u32[]{:S(2)}) collective-permute-start(bf16[1536,768]{1,0:T(8,128)(2,1)} %shard_map.78.refs_0_.refs_1_.refs_7_.refs_19_), channel_id=1, source_target_pairs={{16,0},{17,1},{18,2},{19,3},{20,4},{21,5},{22,6},{23,7},{24,8},{25... | collective-permute-start | bytes 7077896 | tf_op jit(solution)/shard_map/ppermute | solution.py:37
  312.0 78.3 %copy-start = (bf16[1536,768]{1,0:T(8,128)(2,1)}, bf16[1536,768]{1,0:T(8,128)(2,1)S(1)}, u32[]{:S(2)}) copy-start(bf16[1536,768]{1,0:T(8,128)(2,1)S(1)} %collective-permute-done.19.refs_9_) | copy-start | bytes 7077892
  312.0 78.2 %copy-start.1 = (bf16[1536,768]{1,0:T(8,128)(2,1)}, bf16[1536,768]{1,0:T(8,128)(2,1)S(1)}, u32[]{:S(2)}) copy-start(bf16[1536,768]{1,0:T(8,128)(2,1)S(1)} %collective-permute-done.18.refs_8_) | copy-start | bytes 7077892
  312.1 143.3 %copy-start.2 = (bf16[1536,768]{1,0:T(8,128)(2,1)}, bf16[1536,768]{1,0:T(8,128)(2,1)S(1)}, u32[]{:S(2)}) copy-start(bf16[1536,768]{1,0:T(8,128)(2,1)S(1)} %collective-permute-done.17.refs_2_.refs_1_.refs_20_) | copy-start | bytes 7077892
  312.1 4.6 collective-permute-start.24
  312.4 40.9 %collective-permute-start.22 = (bf16[1024,768]{1,0:T(8,128)(2,1)}, bf16[1024,768]{1,0:T(8,128)(2,1)}, u32[]{:S(2)}, u32[]{:S(2)}) collective-permute-start(bf16[1024,768]{1,0:T(8,128)(2,1)} %collective-permute-done.16.refs_3_.refs_2_.refs_21_), channel_id=1, source_target_pairs={{16,0},{17,1},{18,2},{19,3},{20,4},{21,5},{22,6},{23,7},{24,8},{25... | collective-permute-start | bytes 4718600 | tf_op jit(solution)/shard_map/ppermute | solution.py:37
  313.9 39.4 %collective-permute-start.23 = (bf16[1024,768]{1,0:T(8,128)(2,1)}, bf16[1024,768]{1,0:T(8,128)(2,1)S(1)}, u32[]{:S(2)}, u32[]{:S(2)}) collective-permute-start(bf16[1024,768]{1,0:T(8,128)(2,1)} %collective-permute-done.15.refs_11_), channel_id=1, source_target_pairs={{1,0},{0,1},{3,2},{2,3},{5,4},{4,5},{7,6},{6,7},{9,8},{8,9},{11,10... | collective-permute-start | bytes 4718600 | tf_op jit(solution)/shard_map/ppermute | solution.py:37
  318.1 35.3 %collective-permute-start.25 = (bf16[1024,768]{1,0:T(8,128)(2,1)}, bf16[1024,768]{1,0:T(8,128)(2,1)S(1)}, u32[]{:S(2)}, u32[]{:S(2)}) collective-permute-start(bf16[1024,768]{1,0:T(8,128)(2,1)} %collective-permute-done.15.refs_11_), channel_id=1, source_target_pairs={{8,0},{9,1},{10,2},{11,3},{12,4},{13,5},{14,6},{15,7},{0,8},{1,9},... | collective-permute-start | bytes 4718600 | tf_op jit(solution)/shard_map/ppermute | solution.py:37
  318.4 34.9 %collective-permute-start.21 = (bf16[512,768]{1,0:T(8,128)(2,1)S(1)}, bf16[512,768]{1,0:T(8,128)(2,1)S(1)}, u32[]{:S(2)}, u32[]{:S(2)}) collective-permute-start(bf16[512,768]{1,0:T(8,128)(2,1)S(1)} %slice.41), channel_id=1, source_target_pairs={{2,0},{3,1},{0,2},{1,3},{6,4},{7,5},{4,6},{5,7},{10,8},{11,9},{8,1... | collective-permute-start | bytes 2359304 | tf_op jit(solution)/shard_map/ppermute | solution.py:37
  319.6 33.7 %collective-permute-start.20 = (bf16[512,768]{1,0:T(8,128)(2,1)S(1)}, bf16[512,768]{1,0:T(8,128)(2,1)S(1)}, u32[]{:S(2)}, u32[]{:S(2)}) collective-permute-start(bf16[512,768]{1,0:T(8,128)(2,1)S(1)} %slice.41), channel_id=1, source_target_pairs={{4,0},{5,1},{6,2},{7,3},{0,4},{1,5},{2,6},{3,7},{12,8},{13,9},{14,... | collective-permute-start | bytes 2359304 | tf_op jit(solution)/shard_map/ppermute | solution.py:37
  353.3 28.6 %copy-start.10 = (bf16[512,768]{1,0:T(8,128)(2,1)}, bf16[512,768]{1,0:T(8,128)(2,1)S(1)}, u32[]{:S(2)}) copy-start(bf16[512,768]{1,0:T(8,128)(2,1)S(1)} %collective-permute-done.21.refs_4_.refs_3_.refs_22_) | copy-start | bytes 2359300
  353.3 28.5 %copy-start.11 = (bf16[512,768]{1,0:T(8,128)(2,1)}, bf16[512,768]{1,0:T(8,128)(2,1)S(1)}, u32[]{:S(2)}) copy-start(bf16[512,768]{1,0:T(8,128)(2,1)S(1)} %collective-permute-done.20.refs_12_) | copy-start | bytes 2359300
  353.4 6.2 %collective-permute-start.28 = (bf16[512,768]{1,0:T(8,128)(2,1)S(1)}, bf16[512,768]{1,0:T(8,128)(2,1)}, u32[]{:S(2)}, u32[]{:S(2)}) collective-permute-start(bf16[512,768]{1,0:T(8,128)(2,1)S(1)} %collective-permute-done.20.refs_12_), channel_id=1, source_target_pairs={{8,0},{9,1},{10,2},{11,3},{12,4},{13,5},{14,6},{15,7},{0,8},{1,9},... | collective-permute-start | bytes 2359304 | tf_op jit(solution)/shard_map/ppermute | solution.py:37
  359.5 19.4 %collective-permute-start.29 = (bf16[1024,768]{1,0:T(8,128)(2,1)S(1)}, bf16[1024,768]{1,0:T(8,128)(2,1)S(1)}, u32[]{:S(2)}, u32[]{:S(2)}) collective-permute-start(bf16[1024,768]{1,0:T(8,128)(2,1)S(1)} %collective-permute-done.23.refs_13_), channel_id=1, source_target_pairs={{8,0},{9,1},{10,2},{11,3},{12,4},{13,5},{14,6},{15,7},{0,8},{1,9},... | collective-permute-start | bytes 4718600 | tf_op jit(solution)/shard_map/ppermute | solution.py:37
  359.9 19.0 %collective-permute-start.27 = (bf16[512,768]{1,0:T(8,128)(2,1)S(1)}, bf16[512,768]{1,0:T(8,128)(2,1)S(1)}, u32[]{:S(2)}, u32[]{:S(2)}) collective-permute-start(bf16[512,768]{1,0:T(8,128)(2,1)S(1)} %collective-permute-done.20.refs_12_), channel_id=1, source_target_pairs={{1,0},{0,1},{3,2},{2,3},{5,4},{4,5},{7,6},{6,7},{9,8},{8,9},{11,10... | collective-permute-start | bytes 2359304 | tf_op jit(solution)/shard_map/ppermute | solution.py:37
  360.6 19.5 %collective-permute-start.26 = (bf16[512,768]{1,0:T(8,128)(2,1)S(1)}, bf16[512,768]{1,0:T(8,128)(2,1)S(1)}, u32[]{:S(2)}, u32[]{:S(2)}) collective-permute-start(bf16[512,768]{1,0:T(8,128)(2,1)S(1)} %collective-permute-done.21.refs_4_.refs_3_.refs_22_), channel_id=1, source_target_pairs={{16,0},{17,1},{18,2},{19,3},{20,4},{21,5},{22,6},{23,7},{24,8},{25... | collective-permute-start | bytes 2359304 | tf_op jit(solution)/shard_map/ppermute | solution.py:37
  378.9 2.9 collective-permute-start.30
  380.1 75.3 %collective-permute-start.34 = (bf16[1536,768]{1,0:T(8,128)(2,1)}, bf16[1536,768]{1,0:T(8,128)(2,1)S(1)}, u32[]{:S(2)}, u32[]{:S(2)}) collective-permute-start(bf16[1536,768]{1,0:T(8,128)(2,1)} %shard_map.82.refs_6_.refs_1_.refs_29_.refs_33_), channel_id=1, source_target_pairs={{1,0},{0,1},{3,2},{2,3},{5,4},{4,5},{7,6},{6,7},{9,8},{8,9},{11,10... | collective-permute-start | bytes 7077896 | tf_op jit(solution)/shard_map/ppermute | solution.py:37
  380.8 74.6 %collective-permute-start.33 = (bf16[1536,768]{1,0:T(8,128)(2,1)}, bf16[1536,768]{1,0:T(8,128)(2,1)}, u32[]{:S(2)}, u32[]{:S(2)}) collective-permute-start(bf16[1536,768]{1,0:T(8,128)(2,1)} %shard_map.82.refs_6_.refs_1_.refs_29_.refs_33_), channel_id=1, source_target_pairs={{16,0},{17,1},{18,2},{19,3},{20,4},{21,5},{22,6},{23,7},{24,8},{25... | collective-permute-start | bytes 7077896 | tf_op jit(solution)/shard_map/ppermute | solution.py:37
  382.8 72.7 %collective-permute-start.35 = (bf16[1536,768]{1,0:T(8,128)(2,1)}, bf16[1536,768]{1,0:T(8,128)(2,1)S(1)}, u32[]{:S(2)}, u32[]{:S(2)}) collective-permute-start(bf16[1536,768]{1,0:T(8,128)(2,1)} %shard_map.82.refs_6_.refs_1_.refs_29_.refs_33_), channel_id=1, source_target_pairs={{8,0},{9,1},{10,2},{11,3},{12,4},{13,5},{14,6},{15,7},{0,8},{1,9},... | collective-permute-start | bytes 7077896 | tf_op jit(solution)/shard_map/ppermute | solution.py:37
  385.8 69.6 %collective-permute-start.32 = (bf16[1024,768]{1,0:T(8,128)(2,1)S(1)}, bf16[1024,768]{1,0:T(8,128)(2,1)}, u32[]{:S(2)}, u32[]{:S(2)}) collective-permute-start(bf16[1024,768]{1,0:T(8,128)(2,1)S(1)} %slice.44), channel_id=1, source_target_pairs={{2,0},{3,1},{0,2},{1,3},{6,4},{7,5},{4,6},{5,7},{10,8},{11,9},{8,1... | collective-permute-start | bytes 4718600 | tf_op jit(solution)/shard_map/ppermute | solution.py:37
  385.9 69.5 %collective-permute-start.31 = (bf16[1024,768]{1,0:T(8,128)(2,1)S(1)}, bf16[1024,768]{1,0:T(8,128)(2,1)}, u32[]{:S(2)}, u32[]{:S(2)}) collective-permute-start(bf16[1024,768]{1,0:T(8,128)(2,1)S(1)} %slice.44), channel_id=1, source_target_pairs={{4,0},{5,1},{6,2},{7,3},{0,4},{1,5},{2,6},{3,7},{12,8},{13,9},{14,... | collective-permute-start | bytes 4718600 | tf_op jit(solution)/shard_map/ppermute | solution.py:37
  455.4 6.3 %collective-permute-start.40 = (bf16[1536,768]{1,0:T(8,128)(2,1)S(1)}, bf16[1536,768]{1,0:T(8,128)(2,1)S(1)}, u32[]{:S(2)}, u32[]{:S(2)}) collective-permute-start(bf16[1536,768]{1,0:T(8,128)(2,1)S(1)} %collective-permute-done.34.refs_7_), channel_id=1, source_target_pairs={{8,0},{9,1},{10,2},{11,3},{12,4},{13,5},{14,6},{15,7},{0,8},{1,9},... | collective-permute-start | bytes 7077896 | tf_op jit(solution)/shard_map/ppermute | solution.py:37
  457.6 42.5 %collective-permute-start.38 = (bf16[1024,768]{1,0:T(8,128)(2,1)}, bf16[1024,768]{1,0:T(8,128)(2,1)S(1)}, u32[]{:S(2)}, u32[]{:S(2)}) collective-permute-start(bf16[1024,768]{1,0:T(8,128)(2,1)} %collective-permute-done.32.refs_3_), channel_id=1, source_target_pairs={{16,0},{17,1},{18,2},{19,3},{20,4},{21,5},{22,6},{23,7},{24,8},{25... | collective-permute-start | bytes 4718600 | tf_op jit(solution)/shard_map/ppermute | solution.py:37
  458.0 42.1 %collective-permute-start.39 = (bf16[1024,768]{1,0:T(8,128)(2,1)}, bf16[1024,768]{1,0:T(8,128)(2,1)S(1)}, u32[]{:S(2)}, u32[]{:S(2)}) collective-permute-start(bf16[1024,768]{1,0:T(8,128)(2,1)} %collective-permute-done.31.refs_25_), channel_id=1, source_target_pairs={{1,0},{0,1},{3,2},{2,3},{5,4},{4,5},{7,6},{6,7},{9,8},{8,9},{11,10... | collective-permute-start | bytes 4718600 | tf_op jit(solution)/shard_map/ppermute | solution.py:37
  463.2 37.0 %collective-permute-start.41 = (bf16[1024,768]{1,0:T(8,128)(2,1)}, bf16[1024,768]{1,0:T(8,128)(2,1)}, u32[]{:S(2)}, u32[]{:S(2)}) collective-permute-start(bf16[1024,768]{1,0:T(8,128)(2,1)} %collective-permute-done.31.refs_25_), channel_id=1, source_target_pairs={{8,0},{9,1},{10,2},{11,3},{12,4},{13,5},{14,6},{15,7},{0,8},{1,9},... | collective-permute-start | bytes 4718600 | tf_op jit(solution)/shard_map/ppermute | solution.py:37
  464.2 35.9 %collective-permute-start.37 = (bf16[512,768]{1,0:T(8,128)(2,1)}, bf16[512,768]{1,0:T(8,128)(2,1)}, u32[]{:S(2)}, u32[]{:S(2)}) collective-permute-start(bf16[512,768]{1,0:T(8,128)(2,1)} %slice.45), channel_id=1, source_target_pairs={{2,0},{3,1},{0,2},{1,3},{6,4},{7,5},{4,6},{5,7},{10,8},{11,9},{8,1... | collective-permute-start | bytes 2359304 | tf_op jit(solution)/shard_map/ppermute | solution.py:37
  464.2 35.9 %collective-permute-start.36 = (bf16[512,768]{1,0:T(8,128)(2,1)}, bf16[512,768]{1,0:T(8,128)(2,1)}, u32[]{:S(2)}, u32[]{:S(2)}) collective-permute-start(bf16[512,768]{1,0:T(8,128)(2,1)} %slice.45), channel_id=1, source_target_pairs={{4,0},{5,1},{6,2},{7,3},{0,4},{1,5},{2,6},{3,7},{12,8},{13,9},{14,... | collective-permute-start | bytes 2359304 | tf_op jit(solution)/shard_map/ppermute | solution.py:37
  501.8 4.4 collective-permute-start.45
  504.0 30.4 %collective-permute-start.42 = (bf16[1536,768]{1,0:T(8,128)(2,1)}, bf16[1536,768]{1,0:T(8,128)(2,1)S(1)}, u32[]{:S(2)}, u32[]{:S(2)}) collective-permute-start(bf16[1536,768]{1,0:T(8,128)(2,1)} %shard_map.83), channel_id=1, source_target_pairs={{0,0},{1,1},{8,2},{9,3},{4,4},{5,5},{12,6},{13,7},{2,8},{3,9},{10,... | collective-permute-start | bytes 7077896 | tf_op jit(solution)/shard_map/ppermute | solution.py:37
  506.3 19.8 %collective-permute-start.46 = (bf16[1024,768]{1,0:T(8,128)(2,1)}, bf16[1024,768]{1,0:T(8,128)(2,1)}, u32[]{:S(2)}, u32[]{:S(2)}) collective-permute-start(bf16[1024,768]{1,0:T(8,128)(2,1)} %copy-done.9), channel_id=1, source_target_pairs={{8,0},{9,1},{10,2},{11,3},{12,4},{13,5},{14,6},{15,7},{0,8},{1,9},... | collective-permute-start | bytes 4718600 | tf_op jit(solution)/shard_map/ppermute | solution.py:37
  506.6 19.3 %collective-permute-start.43 = (bf16[512,768]{1,0:T(8,128)(2,1)}, bf16[512,768]{1,0:T(8,128)(2,1)S(1)}, u32[]{:S(2)}, u32[]{:S(2)}) collective-permute-start(bf16[512,768]{1,0:T(8,128)(2,1)} %collective-permute-done.37.refs_4_), channel_id=1, source_target_pairs={{16,0},{17,1},{18,2},{19,3},{20,4},{21,5},{22,6},{23,7},{24,8},{25... | collective-permute-start | bytes 2359304 | tf_op jit(solution)/shard_map/ppermute | solution.py:37
  507.1 19.0 %collective-permute-start.44 = (bf16[512,768]{1,0:T(8,128)(2,1)}, bf16[512,768]{1,0:T(8,128)(2,1)}, u32[]{:S(2)}, u32[]{:S(2)}) collective-permute-start(bf16[512,768]{1,0:T(8,128)(2,1)} %collective-permute-done.36.refs_26_), channel_id=1, source_target_pairs={{1,0},{0,1},{3,2},{2,3},{5,4},{4,5},{7,6},{6,7},{9,8},{8,9},{11,10... | collective-permute-start | bytes 2359304 | tf_op jit(solution)/shard_map/ppermute | solution.py:37
  534.4 27.0 %collective-permute-start.47 = (bf16[512,768]{1,0:T(8,128)(2,1)}, bf16[512,768]{1,0:T(8,128)(2,1)S(1)}, u32[]{:S(2)}, u32[]{:S(2)}) collective-permute-start(bf16[512,768]{1,0:T(8,128)(2,1)} %collective-permute-done.44.refs_28_), channel_id=1, source_target_pairs={{8,0},{9,1},{10,2},{11,3},{12,4},{13,5},{14,6},{15,7},{0,8},{1,9},... | collective-permute-start | bytes 2359304 | tf_op jit(solution)/shard_map/ppermute | solution.py:37
  561.4 33.4 %collective-permute-start.48 = (bf16[1024,768]{1,0:T(8,128)(2,1)}, bf16[1024,768]{1,0:T(8,128)(2,1)S(1)}, u32[]{:S(2)}, u32[]{:S(2)}) collective-permute-start(bf16[1024,768]{1,0:T(8,128)(2,1)} %shard_map.85), channel_id=1, source_target_pairs={{0,0},{1,1},{8,2},{9,3},{4,4},{5,5},{12,6},{13,7},{2,8},{3,9},{10,... | collective-permute-start | bytes 4718600 | tf_op jit(solution)/shard_map/ppermute | solution.py:37
  581.3 13.5 %collective-permute-start.49 = (bf16[512,768]{1,0:T(8,128)(2,1)}, bf16[512,768]{1,0:T(8,128)(2,1)S(1)}, u32[]{:S(2)}, u32[]{:S(2)}) collective-permute-start(bf16[512,768]{1,0:T(8,128)(2,1)} %shard_map.86), channel_id=1, source_target_pairs={{0,0},{1,1},{8,2},{9,3},{4,4},{5,5},{12,6},{13,7},{2,8},{3,9},{10,... | collective-permute-start | bytes 2359304 | tf_op jit(solution)/shard_map/ppermute | solution.py:37
  (19 other events, 105.5 us)
Sparse Core Ops, SparseCore 0:
  127.9 61.6 all-gather.1

commit v2 on v1

--- a/solution.py
+++ b/solution.py
@@ -70,29 +70,33 @@
     arrays, plan_a, plan_b, places = [], [], [], []
     panels = 0
     for row_units, row_places, col_units, col_places in terms:
+        places = places + [row_places, col_places]
         if col_units is not None:
-            for unit, place in zip(col_units, col_places):
+            for place, unit in enumerate(col_units):
+                place = (len(places) - 1, place)
                 tall, first = sum(v.shape[0] for v in unit), 0
                 for v in unit:
-                    plan_b.append((panels, len(places), tall, first, len(arrays)))
+                    plan_b.append((panels, place, tall, first, len(arrays)))
                     arrays.append(v)
                     first += v.shape[0]
-                places.append(place)
             panels += 1
-        for unit, place in zip(row_units, row_places):
+        for place, unit in enumerate(row_units):
             first, parts = 0, []
             for v in unit:
                 parts.append((len(arrays), first // tile, (first + v.shape[0]) // tile))
                 arrays.append(v)
                 first += v.shape[0]
-            plan_a.append((panels - 1, len(places), unit[0].shape[1], parts))
-            places.append(place)
-    places = jnp.stack([jnp.asarray(p, jnp.int32) for p in places])
+            plan_a.append((panels - 1, (len(places) - 2, place), unit[0].shape[1], parts))
     count = len(arrays)
     deep = sum(wide for _, _, wide, _ in plan_a)
 
-    def kernel(places_ref, *refs):
+    def kernel(*refs):
         refs = list(refs)
+        place_refs = [refs.pop(0) for _ in places]
+
+        def place_of(which):
+            return place_refs[which[0]][which[1]]
+
         del refs[: len(wait)]
         mask_ref = refs.pop(0) if mask is not None else None
         operands = [refs.pop(0) for _ in range(count)]
@@ -126,7 +130,7 @@
 
         def col_copy(j, act):
             panel, place, tall, first, which = plan_b[j]
-            offset = pl.multiple_of(places_ref[place] * tall + first, 128)
+            offset = pl.multiple_of(place_of(place) * tall + first, 128)
             rows = pl.ds(offset, arrays[which].shape[0])
             act(pltpu.make_async_copy(operands[which], b_buf.at[panel, rows, :], b_sem.at[j]))
 
@@ -155,7 +159,7 @@
             if wide == order:
                 right = b_buf[panel]
             else:
-                right = b_buf[panel, pl.ds(pl.multiple_of(places_ref[place] * wide, 128), wide), :]
+                right = b_buf[panel, pl.ds(pl.multiple_of(place_of(place) * wide, 128), wide), :]
             part = jnp.dot(a_buf[slot, :, offset : offset + wide], right, preferred_element_type=jnp.float32)
             total = part if total is None else total + part
             offset += wide
@@ -175,7 +179,7 @@
 
     smem = pl.BlockSpec(memory_space=pltpu.SMEM)
     tiled = pl.BlockSpec((tile, width), lambda i: (first_tile + i, 0))
-    in_specs, operands = [smem], [places]
+    in_specs, operands = [smem] * len(places), list(places)
     in_specs, operands = in_specs + [pl.BlockSpec(memory_space=pl.ANY)] * len(wait), operands + list(wait)
     if mask is not None:
         in_specs, operands = in_specs + [smem], operands + [mask]
@@ -268,7 +272,7 @@
     )(scalars, tables, pattern, strips)
 
 
-def gather_strips(strips, targets, atoms, blocks, devices):
+def to_send(strips, targets, atoms, blocks, devices):
     count, atom_width, block = strips.shape
     matches = targets[:, None] == lax.iota(jnp.int32, devices)[None, :]
     before = jnp.cumsum(matches.astype(jnp.int32), axis=0) - 1
@@ -283,10 +287,13 @@
     lines = -(-3 * slots // block)
     lines = -(-lines // 16) * 16
     table = jnp.pad(table.reshape(-1), (0, lines * block - 3 * slots)).reshape(lines, block)
-    sent = jnp.concatenate([strips.reshape(count * atom_width, block), table.astype(strips.dtype)])
-    rows = sent.shape[0]
+    return jnp.concatenate([strips.reshape(count * atom_width, block), table.astype(strips.dtype)])
+
+
+def gather_strips(sent, lines, devices):
+    slots, block = devices * CAPACITY, sent.shape[1]
     all_sent = lax.all_gather(sent, AXES, axis=0, tiled=True)
-    tables = all_sent.reshape(devices, rows, block)[:, count * atom_width :]
+    tables = all_sent.reshape(devices, -1, block)[:, lines:]
     tables = tables.astype(jnp.int32).reshape(devices, -1)[:, : 3 * slots]
     return all_sent, tables.reshape(devices, 3, slots).transpose(1, 0, 2)
 
@@ -341,7 +348,6 @@
         return product(terms, kept, own, base, tile, inv_root, jnp.bfloat16, wait, span)
 
     half = height // tile // 2 * tile
-    most = height // tile * 2 // 3 * tile
 
     def along_x(unit):
         return [unit] + [f"{unit}_x{s}" for s in range(1, nx)]
@@ -371,26 +377,41 @@
 
     r = Rounds(lay)
     v0, v1 = cut(density, half, height - half)
-    r.held = dict(density=density, v0=v0, v1=v1)
+    r.held = dict(
+        density=density,
+        v0=v0,
+        v1=v1,
+        sent=to_send(strips, dest_device[:, 0], atom_slot, block_slot, devices),
+        own_at=jnp.stack(own_places),
+        far_at=jnp.stack(far_places),
+        row_at=jnp.stack(row_places),
+        col_at=jnp.stack(col_places),
+        kept_zero=kept_zero,
+        kept_first=kept_first,
+    )
     from_far = lambda x, k, zh, zl, y: (x, zl, 1 - zh, k, y)
     from_beside = lambda x, k, zh, zl, y: (x, 1 - zl, zh, k, y)
     r.run([("zh", "f0", "v0", from_far), ("zl", "own", "density", swap)])
-    all_strips, tables = gather_strips(strips, dest_device[:, 0], atom_slot, block_slot, devices)
+    own_places, far_places, row_places, col_places = (r["own_at"], r["far_at"], r["row_at"], r["col_at"])
+    kept_zero, kept_first = r["kept_zero"], r["kept_first"]
     r.run(
         [("zh", "f1", "v1", from_far), ("zl", "zl", "density", from_beside)]
         + sends_x("own")
         + sends_y("own")
         + sends_core("own")
     )
-    r.run(sends_x("zl") + sends_y("f0", "f1") + rest_core("own") + sends_core("f0", "f1") + rest_core("f0"))
+    all_strips, tables = gather_strips(r["sent"], strips.shape[0] * strips.shape[1], devices)
+    r.run(sends_x("zl") + sends_y("f0", "f1") + rest_core("own") + sends_core("f0"))
     zero_cols = cols_of("own") + cols_of("zl")
     base = partial(rows_of("own"), own_places, zero_cols, col_places)
-    r.run(rest_core("f1"), base=base)
+    apart = sends_core("f1") + rest_core("f0", "f1")
+    r.run([(f"core{i}",) + send[1:] for i, send in enumerate(apart)], base=base)
     zero_cols = cols_of("own") + cols_of("zl")
     far_rows = rows_of("f0", "f1")
     old_rows = rows_of("own") + far_rows
     zeroth = finish([(far_rows, far_places, zero_cols, col_places)], kept_zero, None, r["base"])
 
+    lone = jnp.zeros((1,), jnp.int32)
     tables, zeroth = tie(tables, zeroth)
     field_cols = field_panel(
         all_strips, tables, patterns[2], lay.rows, my_col, lay.cols, 0, my_col * wide, height, width, False
@@ -399,48 +420,51 @@
         all_strips, tables, patterns[2], lay.cols, my_row * lay.cols, 1, my_row * tall, 0, height, width, True
     )
 
+    tiles = height // tile
+    few, some = max(1, tiles // 6), max(1, tiles // 3)
+    parts = {"p": [tiles - some, some], "q": [few, tiles - some - few, some]}
+
     def start(v, tag):
-        one, two = cut(v, most, height - most)
-        return {"own" + tag: v, "v0" + tag: one, "v1" + tag: two}
-
-    def first_sends(tag):
-        return (
-            [("zh", "f0" + tag, "v0" + tag, to_zh), ("zl", "z0" + tag, "v0" + tag, to_zl)]
-            + sends_x("own" + tag)
-            + sends_y("own" + tag)
-            + sends_core("own" + tag)
-        )
-
-    def second_sends(tag):
-        return (
-            [("zh", "f1" + tag, "v1" + tag, to_zh), ("zl", "z1" + tag, "v1" + tag, to_zl)]
-            + sends_x("z0" + tag)
-            + sends_y("f0" + tag)
-            + rest_core("own" + tag)
-            + sends_core("f0" + tag)
-        )
-
-    def third_sends(tag):
-        return sends_x("z1" + tag) + sends_y("f1" + tag) + sends_core("f1" + tag) + rest_core("f0" + tag)
+        pieces = cut(v, *[part * tile for part in parts[tag]])
+        return dict({f"v{i}{tag}": piece for i, piece in enumerate(pieces)}, **{"own" + tag: v})
+
+    def sends_z(tag, i):
+        return [("zh", f"f{i}{tag}", f"v{i}{tag}", to_zh), ("zl", f"z{i}{tag}", f"v{i}{tag}", to_zl)]
+
+    def chunks(kind, tag):
+        return [f"{kind}{i}{tag}" for i in range(len(parts[tag]))]
 
     def col_panel(tag):
-        return cols_of("own" + tag) + cols_of("z0" + tag, "z1" + tag)
+        return cols_of("own" + tag) + cols_of(*chunks("z", tag))
 
     r = Rounds(lay)
     r.held = start(zeroth, "p")
-    first = partial(old_rows, row_places, [[field_cols]], [0], None, (zeroth,))
-    linear = finish([([[field_rows]], [0], zero_cols, col_places)], kept_first, None, first)
-    r.run(first_sends("p"), linear=linear)
-    r.run(second_sends("p"))
-    r.held.update(start(r["linear"], "q"))
-    r.run(third_sends("p") + rest_core("f1p") + first_sends("q"))
-    zero_rows = rows_of("ownp") + rows_of("f0p", "f1p")
+    first = partial(old_rows, row_places, [[field_cols]], lone, None, (zeroth,))
+    r.run(
+        sends_z("p", 0) + sends_x("ownp") + sends_y("ownp") + sends_core("ownp"),
+        first=first,
+        field_rows=field_rows,
+    )
+    linear = finish([([[r["field_rows"]]], lone, zero_cols, col_places)], kept_first, None, r["first"])
+    r.run(
+        sends_z("p", 1) + sends_x("z0p") + sends_y("f0p") + rest_core("ownp") + sends_core("f0p"),
+        **start(linear, "q"),
+    )
+    r.run(sends_z("q", 0) + sends_x("z1p") + sends_y("f1p") + sends_core("f1p") + rest_core("f0p"))
+    r.run(sends_z("q", 1) + sends_x("ownq") + sends_y("ownq") + rest_core("f1p") + sends_core("ownq"))
+    zero_rows = rows_of("ownp") + rows_of(*chunks("f", "p"))
     new_zeroth = finish([(zero_rows, row_places, col_panel("p"), col_places)], kept_zero, r["ownp"], None)
-    r.run(second_sends("q"), new_zeroth=new_zeroth)
+    r.run(
+        sends_z("q", 2)
+        + sends_x("z0q", "z1q")
+        + sends_y("f0q", "f1q")
+        + rest_core("ownq")
+        + sends_core("f0q", "f1q"),
+        new_zeroth=new_zeroth,
+    )
     base = partial(rows_of("ownq"), own_places, col_panel("p"), col_places)
-    r.run([("zl", "back", "new_zeroth", swap)] + third_sends("q"), base=base)
-    zero_rows = rows_of("ownp") + rows_of("f0p", "f1p")
-    spans = ((0, most // tile), (most // tile, height // tile))
+    r.run(sends_x("z2q") + sends_y("f2q") + sends_core("f2q") + rest_core("f0q", "f1q"), base=base)
+    zero_rows = rows_of("ownp") + rows_of(*chunks("f", "p"))
 
     def last(far_rows, base, span):
         terms = [
@@ -449,11 +473,10 @@
         ]
         return finish(terms, kept_first, r["ownq"], base, (), span)
 
-    far_rows = rows_of("f0q")
-    top = last(far_rows, r["base"], spans[0])
-    r.run(rest_core("f1q"), top=top)
+    top = last(rows_of("f0q", "f1q"), r["base"], (0, tiles - some))
+    r.run([("zl", "back", "new_zeroth", swap)] + rest_core("f2q"), top=top)
     back_top = lay.send(r["top"], swap)
-    bottom = last(rows_of("f0q", "f1q"), r["base"], spans[1])
+    bottom = last(rows_of(*chunks("f", "q")), r["base"], (tiles - some, tiles))
     back_bottom = lay.send(bottom, swap)
     new_linear = jnp.concatenate([back_top, back_bottom]).astype(jnp.float32)
     return (r["back"].astype(jnp.float32), new_linear)

time: 606 us -> 571 us (0.942)
  waiting for transfers between devices: 309 us -> 258 us
  starting transfers between devices: 60.1 us -> 70.9 us
  other arithmetic: 7.4 us -> 15.9 us
    ppermute x50 -> x56, waiting for transfers between devices: 309 us -> 258 us  [send(): return lax.ppermute(value, AXES, self.perm(source))]
    ppermute x50 -> x56, starting transfers between devices: 60.1 us -> 70.8 us  [send(): return lax.ppermute(value, AXES, self.perm(source))]
  transfers between devices with their start and end apart: 51 -> 57, of which waited for: 22 -> 24; matrix products, arithmetic and copies ran while one was open for 3% -> 5% of each run, Pallas kernels for 29% -> 31%
where the time goes in v2:
time: 571 us; the launch traced here: 569 us
  waiting for transfers between devices  258 us (45%)
  Pallas kernels  190 us (33%)
  starting transfers between devices  70.9 us (12%)
  local copies, waits for them, and re-layouts  19.4 us (3%)
  other arithmetic  15.9 us (3%)
  between operations  14.5 us (3%)
    ppermute x56, waiting for transfers between devices, send(): return lax.ppermute(value, AXES, self.perm(source))  258 us
    pallas_call x8, Pallas kernels, product(): pl.pallas_call(kernel, grid=(tiles,), out_shape=jax.ShapeDtypeStruct((til...  161 us
    ppermute x56, starting transfers between devices, send(): return lax.ppermute(value, AXES, self.perm(source))  70.8 us
    pallas_call x2, Pallas kernels, field_panel(): pl.pallas_call(kernel, grid=(slabs,), out_shape=jax.ShapeDtypeStruct(shap...  28.7 us
  transfers between devices with their start and end apart: 57, of which 24 were waited for; matrix products, arithmetic and copies ran while one was open for 5% of the time, Pallas kernels for 31%

profile of v2, /device:TPU:1, one launch (start us, length us, event | category | flops | bytes accessed | tf_op | source)
XLA Modules:
  0.0 568.6 jit_solution(14705124828399390224)
XLA Ops:
  7.2 4.7 collective-permute-start.1
  12.0 2.8 fusion.5
  14.8 2.0 collective-permute-start
  19.0 1.4 select_reduce_fusion.5
  26.8 1.5 pad_maximum_fusion
  28.3 1.4 slice_bitcast_fusion
  30.3 35.9 %collective-permute-done.refs_7_.refs_8_ = bf16[768,768]{1,0:T(8,128)(2,1)} collective-permute-done((bf16[768,768]{1,0:T(8,128)(2,1)}, bf16[768,768]{1,0:T(8,128)(2,1)}, u32[]{:S(2)}, u32[]{:S(2)}) %collective-permute-start) | collective-permute-done | bytes 1179680 | tf_op jit(solution)/shard_map/ppermute | solution.py:37
  66.2 7.1 %collective-permute-start.3 = (bf16[1536,768]{1,0:T(8,128)(2,1)S(1)}, bf16[1536,768]{1,0:T(8,128)(2,1)S(1)}, u32[]{:S(2)}, u32[]{:S(2)}) collective-permute-start(bf16[1536,768]{1,0:T(8,128)(2,1)S(1)} %copy-done.4), channel_id=1, source_target_pairs={{8,0},{9,1},{0,2},{1,3},{12,4},{13,5},{4,6},{5,7},{10,8},{11,9},{2... | collective-permute-start | bytes 7077896 | tf_op jit(solution)/shard_map/ppermute | solution.py:37
  73.4 1.5 collective-permute-start.5
  74.9 1.2 collective-permute-start.4
  76.1 2.5 collective-permute-start.2
  78.7 27.6 %collective-permute-done.2.refs_8_.refs_9_ = bf16[768,768]{1,0:T(8,128)(2,1)S(1)} collective-permute-done((bf16[768,768]{1,0:T(8,128)(2,1)S(1)}, bf16[768,768]{1,0:T(8,128)(2,1)S(1)}, u32[]{:S(2)}, u32[]{:S(2)}) %collective-permute-start.2) | collective-permute-done | bytes 1179680 | tf_op jit(solution)/shard_map/ppermute | solution.py:37
  106.3 16.3 %collective-permute-done.3.refs_4_.refs_5_ = bf16[1536,768]{1,0:T(8,128)(2,1)S(1)} collective-permute-done((bf16[1536,768]{1,0:T(8,128)(2,1)S(1)}, bf16[1536,768]{1,0:T(8,128)(2,1)S(1)}, u32[]{:S(2)}, u32[]{:S(2)}) %collective-permute-start.3) | collective-permute-done | bytes 2359328 | tf_op jit(solution)/shard_map/ppermute | solution.py:37
  122.6 1.4 copy-done.24
  124.0 1.4 copy-done.26
  127.3 5.2 collective-permute-start.10
  133.0 28.9 %collective-permute-done.8.refs_9_.refs_10_ = bf16[768,768]{1,0:T(8,128)(2,1)} collective-permute-done((bf16[768,768]{1,0:T(8,128)(2,1)}, bf16[768,768]{1,0:T(8,128)(2,1)}, u32[]{:S(2)}, u32[]{:S(2)}) %collective-permute-start.8) | collective-permute-done | bytes 1179680 | tf_op jit(solution)/shard_map/ppermute | solution.py:37
  163.3 29.6 %collective-permute-done.9.refs_10_.refs_11_ = bf16[768,768]{1,0:T(8,128)(2,1)} collective-permute-done((bf16[768,768]{1,0:T(8,128)(2,1)}, bf16[768,768]{1,0:T(8,128)(2,1)}, u32[]{:S(2)}, u32[]{:S(2)}) %collective-permute-start.9) | collective-permute-done | bytes 1179680 | tf_op jit(solution)/shard_map/ppermute | solution.py:37
  192.9 1.7 collective-permute-start.12
  195.1 15.5 %shard_map.77.refs_15_ = f32[1536,768]{1,0:T(8,128)} custom-call(s32[4]{0:T(128)} %get-tuple-element.250.refs_0_, s32[4]{0:T(128)} %pad_add_fusion.2.refs_1_.refs_3_, bf16[1536,768]{1,0:T(8,128)(2,1)} %collective-permute-done.1.refs_2_.refs_6_.refs_3_.refs_4_, bf16[1536,768]{1,0:T(8,128)(2,1)} %collective-permute-done.4.refs_3_.refs_4_, ...), custom_call_target="tpu_custom_call" | custom-call | flops 7247757312 | bytes 23592960 | tf_op jit(solution)/shard_map/pallas_call | solution.py:191
  212.3 15.6 %shard_map.78.refs_2_.refs_3_.refs_9_.refs_21_.refs_13_.refs_25_ = bf16[1536,768]{1,0:T(8,128)(2,1)} custom-call(s32[4]{0:T(128)} %get-tuple-element.251.refs_0_.refs_2_, s32[4]{0:T(128)} %pad_add_fusion.2.refs_1_.refs_3_, f32[12,6]{1,0:T(8,128)} %get-tuple-element.254.refs_2_, bf16[1536,768]{1,0:T(8,128)(2,1)} %collective-permute-done.1.refs_2_.refs_6_.refs_3_.refs_4_, ...), custom_call_target="tpu_custom_call" | custom-call | flops 7247757312 | bytes 23592960 | tf_op jit(solution)/shard_map/pallas_call | solution.py:191
  229.3 1.5 slice.44
  233.1 2.1 slice.45
  235.2 10.5 %shard_map.79.refs_3_ = bf16[6144,768]{1,0:T(8,128)(2,1)} custom-call(s32[3]{0:T(128)} %pad_add_fusion.3.scalar_ref, s32[3,32,64]{2,1,0:T(8,128)} %bitcast.50, s32[48,48]{1,0:T(8,128)} %get-tuple-element.500.pattern_ref, bf16[8704,128]{1,0:T(8,128)(2,1)} %all-gather.2.cloned.1.call-done.strips_ref), custom_call_target="tpu_custom_call" | custom-call | flops 37748736 | bytes 37748736 | tf_op jit(solution)/shard_map/pallas_call | solution.py:259
  245.7 18.2 %shard_map.81.refs_7_ = bf16[1536,6144]{1,0:T(8,128)(2,1)} custom-call(s32[3]{0:T(128)} %pad_add_fusion.4.scalar_ref, s32[3,32,64]{2,1,0:T(8,128)} %bitcast.51, s32[48,48]{1,0:T(8,128)} %get-tuple-element.500.pattern_ref, bf16[8704,128]{1,0:T(8,128)(2,1)} %all-gather.2.cloned.1.call-done.strips_ref), custom_call_target="tpu_custom_call" | custom-call | flops 75497472 | bytes 75497472 | tf_op jit(solution)/shard_map/pallas_call | solution.py:259
  263.9 23.4 %shard_map.80.refs_8_ = f32[1536,768]{1,0:T(8,128)} custom-call(s32[8]{0:T(128)} %stack.134.refs_0_, s32[1]{0:T(128)} %constant.112.clone.1.refs_1_.refs_0_, bf16[1536,768]{1,0:T(8,128)(2,1)} %shard_map.78.refs_2_.refs_3_.refs_9_.refs_21_.refs_13_.refs_25_, bf16[6144,768]{1,0:T(8,128)(2,1)} %shard_map.79.refs_3_, ...), custom_call_target="tpu_custom_call" | custom-call | flops 14495514624 | bytes 33030144 | tf_op jit(solution)/shard_map/pallas_call | solution.py:191
  287.2 12.4 %collective-permute-done.16.refs_5_.refs_4_.refs_27_ = bf16[1024,768]{1,0:T(8,128)(2,1)} collective-permute-done((bf16[1024,768]{1,0:T(8,128)(2,1)S(1)}, bf16[1024,768]{1,0:T(8,128)(2,1)}, u32[]{:S(2)}, u32[]{:S(2)}) %collective-permute-start.16) | collective-permute-done | bytes 1572896 | tf_op jit(solution)/shard_map/ppermute | solution.py:37
  299.7 3.0 collective-permute-start.24
  302.7 1.2 collective-permute-start.22
  303.9 1.2 collective-permute-start.23
  305.1 1.9 collective-permute-done.24.refs_12_.refs_16_
  307.4 2.2 collective-permute-start.20
  309.6 22.6 %shard_map.82.refs_8_.refs_5_.refs_39_.refs_43_ = bf16[1536,768]{1,0:T(8,128)(2,1)} custom-call(s32[1]{0:T(128)} %constant.112.clone.1.refs_1_.refs_0_, s32[4]{0:T(128)} %pad_add_fusion.2.refs_1_.refs_3_, f32[12,6]{1,0:T(8,128)} %get-tuple-element.255.refs_2_.refs_4_, bf16[1536,768]{1,0:T(8,128)(2,1)} %collective-permute-done.1.refs_2_.refs_6_.refs_3_.refs_4_, ...), custom_call_target="tpu_custom_call" | custom-call | flops 14495514624 | bytes 33030144 | tf_op jit(solution)/shard_map/pallas_call | solution.py:191
  334.6 1.3 slice.53
  336.0 7.2 %collective-permute-done.21.refs_6_.refs_5_.refs_28_ = bf16[512,768]{1,0:T(8,128)(2,1)} collective-permute-done((bf16[512,768]{1,0:T(8,128)(2,1)}, bf16[512,768]{1,0:T(8,128)(2,1)}, u32[]{:S(2)}, u32[]{:S(2)}) %collective-permute-start.21) | collective-permute-done | bytes 786464 | tf_op jit(solution)/shard_map/ppermute | solution.py:37
  343.2 2.4 collective-permute-start.30
  345.6 2.1 collective-permute-done.30.refs_18_.refs_22_
  349.3 1.2 collective-permute-start.29
  350.5 1.5 collective-permute-start.26
  352.0 16.0 %collective-permute-done.27.refs_7_ = bf16[256,768]{1,0:T(8,128)(2,1)S(1)} collective-permute-done((bf16[256,768]{1,0:T(8,128)(2,1)S(1)}, bf16[256,768]{1,0:T(8,128)(2,1)S(1)}, u32[]{:S(2)}, u32[]{:S(2)}) %collective-permute-start.27) | collective-permute-done | bytes 393248 | tf_op jit(solution)/shard_map/ppermute | solution.py:37
  368.2 3.4 collective-permute-start.36
  372.0 1.4 collective-permute-done.36.refs_20_.refs_24_
  373.8 1.5 collective-permute-start.32
  375.3 50.2 %collective-permute-done.33.refs_8_ = bf16[768,768]{1,0:T(8,128)(2,1)S(1)} collective-permute-done((bf16[768,768]{1,0:T(8,128)(2,1)S(1)}, bf16[768,768]{1,0:T(8,128)(2,1)S(1)}, u32[]{:S(2)}, u32[]{:S(2)}) %collective-permute-start.33) | collective-permute-done | bytes 1179680 | tf_op jit(solution)/shard_map/ppermute | solution.py:37
  425.6 2.0 collective-permute-done.32.refs_32_
  430.0 2.8 collective-permute-done.44.refs_11_
  433.2 1.5 collective-permute-start.38
  434.7 4.7 collective-permute-done.40.refs_10_
  441.7 1.7 collective-permute-start.46
  443.4 24.0 %shard_map.83 = bf16[1536,768]{1,0:T(8,128)(2,1)} custom-call(s32[8]{0:T(128)} %stack.134.refs_0_, s32[4]{0:T(128)} %pad_add_fusion.2.refs_1_.refs_3_, f32[12,6]{1,0:T(8,128)} %get-tuple-element.254.refs_2_, bf16[1536,768]{1,0:T(8,128)(2,1)} %shard_map.78.refs_2_.refs_3_.refs_9_.refs_21_.refs_13_.refs_25_, ...), custom_call_target="tpu_custom_call" | custom-call | flops 14495514624 | bytes 33030144 | tf_op jit(solution)/shard_map/pallas_call | solution.py:191
  468.1 2.0 collective-permute-done.38.refs_33_
  471.1 2.1 collective-permute-done.49.refs_39_
  473.6 1.6 collective-permute-done.50.refs_37_.refs_40_
  476.9 15.1 %shard_map.84.refs_40_.refs_44_ = f32[1536,768]{1,0:T(8,128)} custom-call(s32[4]{0:T(128)} %get-tuple-element.250.refs_0_, s32[4]{0:T(128)} %pad_add_fusion.2.refs_1_.refs_3_, bf16[1536,768]{1,0:T(8,128)(2,1)} %shard_map.78.refs_2_.refs_3_.refs_9_.refs_21_.refs_13_.refs_25_, bf16[1536,768]{1,0:T(8,128)(2,1)} %collective-permute-done.17.refs_4_.refs_3_.refs_26_, ...), custom_call_target="tpu_custom_call" | custom-call | flops 7247757312 | bytes 23592960 | tf_op jit(solution)/shard_map/pallas_call | solution.py:191
  492.1 2.7 collective-permute-done.47.refs_12_
  494.8 2.2 collective-permute-start.52
  497.0 1.3 collective-permute-start.53
  498.3 27.1 %shard_map.85 = bf16[1024,768]{1,0:T(8,128)(2,1)} custom-call(s32[8]{0:T(128)} %stack.134.refs_0_, s32[4]{0:T(128)} %pad_add_fusion.2.refs_1_.refs_3_, s32[4]{0:T(128)} %get-tuple-element.251.refs_0_.refs_2_, s32[4]{0:T(128)} %pad_add_fusion.2.refs_1_.refs_3_, f32[12,6]{1,0:T(8,128)} %get-tuple-element.255.refs_2_.refs_4_, ...), custom_call_target="tpu_custom_call" | custom-call | flops 14495514624 | bytes 51904512 | tf_op jit(solution)/shard_map/pallas_call | solution.py:191
  525.5 2.2 collective-permute-start.54
  527.7 18.0 %shard_map.86 = bf16[512,768]{1,0:T(8,128)(2,1)} custom-call(s32[8]{0:T(128)} %stack.134.refs_0_, s32[4]{0:T(128)} %pad_add_fusion.2.refs_1_.refs_3_, s32[4]{0:T(128)} %get-tuple-element.251.refs_0_.refs_2_, s32[4]{0:T(128)} %pad_add_fusion.2.refs_1_.refs_3_, f32[12,6]{1,0:T(8,128)} %get-tuple-element.255.refs_2_.refs_4_, ...), custom_call_target="tpu_custom_call" | custom-call | flops 7247757312 | bytes 51904512 | tf_op jit(solution)/shard_map/pallas_call | solution.py:191
  545.7 3.4 collective-permute-start.55
  549.1 2.5 convert_element_type.29
  551.6 7.6 %collective-permute-done.55 = bf16[512,768]{1,0:T(8,128)(2,1)S(1)} collective-permute-done((bf16[512,768]{1,0:T(8,128)(2,1)}, bf16[512,768]{1,0:T(8,128)(2,1)S(1)}, u32[]{:S(2)}, u32[]{:S(2)}) %collective-permute-start.55) | collective-permute-done | bytes 786464 | tf_op jit(solution)/shard_map/ppermute | solution.py:37
  559.2 2.5 maximum_convert_fusion
  (165 shorter events, 33.3 us)
Async XLA Ops:
  7.2 59.0 %copy-start.4 = (bf16[1536,768]{1,0:T(8,128)(2,1)S(1)}, bf16[1536,768]{1,0:T(8,128)(2,1)}, u32[]{:S(2)}) copy-start(bf16[1536,768]{1,0:T(8,128)(2,1)} %param.6) | copy-start | bytes 7077892
  7.2 203.4 %all-gather.2.cloned.1.call-start = ((), (), s32[]{:S(2)}) async-start(), calls=%async_computation | async-start | bytes 2297856 | tf_op jit(solution)/shard_map/all_gather | solution.py:295
  7.2 59.0 %collective-permute-start.1 = (bf16[1536,768]{1,0:T(8,128)(2,1)}, bf16[1536,768]{1,0:T(8,128)(2,1)}, u32[]{:S(2)}, u32[]{:S(2)}) collective-permute-start(bf16[1536,768]{1,0:T(8,128)(2,1)} %param.6), channel_id=1, source_target_pairs={{0,0},{1,1},{8,2},{9,3},{4,4},{5,5},{12,6},{13,7},{2,8},{3,9},{10,... | collective-permute-start | bytes 7077896 | tf_op jit(solution)/shard_map/ppermute | solution.py:37
  14.8 51.4 %collective-permute-start = (bf16[768,768]{1,0:T(8,128)(2,1)}, bf16[768,768]{1,0:T(8,128)(2,1)}, u32[]{:S(2)}, u32[]{:S(2)}) collective-permute-start(bf16[768,768]{1,0:T(8,128)(2,1)} %get-tuple-element.499), channel_id=1, source_target_pairs={{4,0},{5,1},{12,2},{13,3},{0,4},{1,5},{8,6},{9,7},{6,8},{7,9},{14,... | collective-permute-start | bytes 3538952 | tf_op jit(solution)/shard_map/ppermute | solution.py:37
  66.2 56.3 %collective-permute-start.3 = (bf16[1536,768]{1,0:T(8,128)(2,1)S(1)}, bf16[1536,768]{1,0:T(8,128)(2,1)S(1)}, u32[]{:S(2)}, u32[]{:S(2)}) collective-permute-start(bf16[1536,768]{1,0:T(8,128)(2,1)S(1)} %copy-done.4), channel_id=1, source_target_pairs={{8,0},{9,1},{0,2},{1,3},{12,4},{13,5},{4,6},{5,7},{10,8},{11,9},{2... | collective-permute-start | bytes 7077896 | tf_op jit(solution)/shard_map/ppermute | solution.py:37
  73.3 50.7 %collective-permute-start.6 = (bf16[1536,768]{1,0:T(8,128)(2,1)}, bf16[1536,768]{1,0:T(8,128)(2,1)S(1)}, u32[]{:S(2)}, u32[]{:S(2)}) collective-permute-start(bf16[1536,768]{1,0:T(8,128)(2,1)} %collective-permute-done.1.refs_2_.refs_6_.refs_3_.refs_4_), channel_id=1, source_target_pairs={{8,0},{9,1},{10,2},{11,3},{12,4},{13,5},{14,6},{15,7},{0,8},{1,9},... | collective-permute-start | bytes 7077896 | tf_op jit(solution)/shard_map/ppermute | solution.py:37
  73.4 52.9 %collective-permute-start.5 = (bf16[1536,768]{1,0:T(8,128)(2,1)}, bf16[1536,768]{1,0:T(8,128)(2,1)}, u32[]{:S(2)}, u32[]{:S(2)}) collective-permute-start(bf16[1536,768]{1,0:T(8,128)(2,1)} %collective-permute-done.1.refs_2_.refs_6_.refs_3_.refs_4_), channel_id=1, source_target_pairs={{1,0},{0,1},{3,2},{2,3},{5,4},{4,5},{7,6},{6,7},{9,8},{8,9},{11,10... | collective-permute-start | bytes 7077896 | tf_op jit(solution)/shard_map/ppermute | solution.py:37
  74.9 52.4 %collective-permute-start.4 = (bf16[1536,768]{1,0:T(8,128)(2,1)}, bf16[1536,768]{1,0:T(8,128)(2,1)}, u32[]{:S(2)}, u32[]{:S(2)}) collective-permute-start(bf16[1536,768]{1,0:T(8,128)(2,1)} %collective-permute-done.1.refs_2_.refs_6_.refs_3_.refs_4_), channel_id=1, source_target_pairs={{16,0},{17,1},{18,2},{19,3},{20,4},{21,5},{22,6},{23,7},{24,8},{25... | collective-permute-start | bytes 7077896 | tf_op jit(solution)/shard_map/ppermute | solution.py:37
  76.1 30.1 %collective-permute-start.2 = (bf16[768,768]{1,0:T(8,128)(2,1)S(1)}, bf16[768,768]{1,0:T(8,128)(2,1)S(1)}, u32[]{:S(2)}, u32[]{:S(2)}) collective-permute-start(bf16[768,768]{1,0:T(8,128)(2,1)S(1)} %get-tuple-element.248), channel_id=1, source_target_pairs={{4,0},{5,1},{12,2},{13,3},{0,4},{1,5},{8,6},{9,7},{6,8},{7,9},{14,... | collective-permute-start | bytes 3538952 | tf_op jit(solution)/shard_map/ppermute | solution.py:37
  127.3 34.9 %collective-permute-start.10 = (bf16[1536,768]{1,0:T(8,128)(2,1)}, bf16[1536,768]{1,0:T(8,128)(2,1)}, u32[]{:S(2)}, u32[]{:S(2)}) collective-permute-start(bf16[1536,768]{1,0:T(8,128)(2,1)} %collective-permute-done.5.refs_7_.refs_5_), channel_id=1, source_target_pairs={{8,0},{9,1},{10,2},{11,3},{12,4},{13,5},{14,6},{15,7},{0,8},{1,9},... | collective-permute-start | bytes 7077896 | tf_op jit(solution)/shard_map/ppermute | solution.py:37
  132.5 29.5 %collective-permute-start.8 = (bf16[768,768]{1,0:T(8,128)(2,1)}, bf16[768,768]{1,0:T(8,128)(2,1)}, u32[]{:S(2)}, u32[]{:S(2)}) collective-permute-start(bf16[768,768]{1,0:T(8,128)(2,1)} %collective-permute-done.refs_7_.refs_8_), channel_id=1, source_target_pairs={{1,0},{0,1},{3,2},{2,3},{5,4},{4,5},{7,6},{6,7},{9,8},{8,9},{11,10... | collective-permute-start | bytes 3538952 | tf_op jit(solution)/shard_map/ppermute | solution.py:37
  132.8 60.1 %collective-permute-start.7 = (bf16[1536,768]{1,0:T(8,128)(2,1)}, bf16[1536,768]{1,0:T(8,128)(2,1)S(1)}, u32[]{:S(2)}, u32[]{:S(2)}) collective-permute-start(bf16[1536,768]{1,0:T(8,128)(2,1)} %copy-done.24), channel_id=1, source_target_pairs={{16,0},{17,1},{18,2},{19,3},{20,4},{21,5},{22,6},{23,7},{24,8},{25... | collective-permute-start | bytes 7077896 | tf_op jit(solution)/shard_map/ppermute | solution.py:37
  162.0 30.9 %collective-permute-start.9 = (bf16[768,768]{1,0:T(8,128)(2,1)}, bf16[768,768]{1,0:T(8,128)(2,1)}, u32[]{:S(2)}, u32[]{:S(2)}) collective-permute-start(bf16[768,768]{1,0:T(8,128)(2,1)} %copy-done.30), channel_id=1, source_target_pairs={{1,0},{0,1},{3,2},{2,3},{5,4},{4,5},{7,6},{6,7},{9,8},{8,9},{11,10... | collective-permute-start | bytes 3538952 | tf_op jit(solution)/shard_map/ppermute | solution.py:37
  162.2 30.7 %collective-permute-start.11 = (bf16[768,768]{1,0:T(8,128)(2,1)}, bf16[768,768]{1,0:T(8,128)(2,1)}, u32[]{:S(2)}, u32[]{:S(2)}) collective-permute-start(bf16[768,768]{1,0:T(8,128)(2,1)} %collective-permute-done.refs_7_.refs_8_), channel_id=1, source_target_pairs={{8,0},{9,1},{10,2},{11,3},{12,4},{13,5},{14,6},{15,7},{0,8},{1,9},... | collective-permute-start | bytes 3538952 | tf_op jit(solution)/shard_map/ppermute | solution.py:37
  192.9 19.5 %collective-permute-start.12 = (bf16[768,768]{1,0:T(8,128)(2,1)}, bf16[768,768]{1,0:T(8,128)(2,1)}, u32[]{:S(2)}, u32[]{:S(2)}) collective-permute-start(bf16[768,768]{1,0:T(8,128)(2,1)} %copy-done.30), channel_id=1, source_target_pairs={{8,0},{9,1},{10,2},{11,3},{12,4},{13,5},{14,6},{15,7},{0,8},{1,9},... | collective-permute-start | bytes 3538952 | tf_op jit(solution)/shard_map/ppermute | solution.py:37
  194.6 17.7 %collective-permute-start.13 = (bf16[768,768]{1,0:T(8,128)(2,1)}, bf16[768,768]{1,0:T(8,128)(2,1)}, u32[]{:S(2)}, u32[]{:S(2)}) collective-permute-start(bf16[768,768]{1,0:T(8,128)(2,1)} %collective-permute-done.8.refs_9_.refs_10_), channel_id=1, source_target_pairs={{8,0},{9,1},{10,2},{11,3},{12,4},{13,5},{14,6},{15,7},{0,8},{1,9},... | collective-permute-start | bytes 3538952 | tf_op jit(solution)/shard_map/ppermute | solution.py:37
  194.7 17.6 %collective-permute-start.14 = (bf16[768,768]{1,0:T(8,128)(2,1)}, bf16[768,768]{1,0:T(8,128)(2,1)}, u32[]{:S(2)}, u32[]{:S(2)}) collective-permute-start(bf16[768,768]{1,0:T(8,128)(2,1)} %collective-permute-done.9.refs_10_.refs_11_), channel_id=1, source_target_pairs={{8,0},{9,1},{10,2},{11,3},{12,4},{13,5},{14,6},{15,7},{0,8},{1,9},... | collective-permute-start | bytes 3538952 | tf_op jit(solution)/shard_map/ppermute | solution.py:37
  227.9 71.7 %collective-permute-start.19 = (bf16[1536,768]{1,0:T(8,128)(2,1)}, bf16[1536,768]{1,0:T(8,128)(2,1)S(1)}, u32[]{:S(2)}, u32[]{:S(2)}) collective-permute-start(bf16[1536,768]{1,0:T(8,128)(2,1)} %shard_map.78.refs_2_.refs_3_.refs_9_.refs_21_.refs_13_.refs_25_), channel_id=1, source_target_pairs={{8,0},{9,1},{10,2},{11,3},{12,4},{13,5},{14,6},{15,7},{0,8},{1,9},... | collective-permute-start | bytes 7077896 | tf_op jit(solution)/shard_map/ppermute | solution.py:37
  228.8 70.9 %collective-permute-start.18 = (bf16[1536,768]{1,0:T(8,128)(2,1)}, bf16[1536,768]{1,0:T(8,128)(2,1)}, u32[]{:S(2)}, u32[]{:S(2)}) collective-permute-start(bf16[1536,768]{1,0:T(8,128)(2,1)} %shard_map.78.refs_2_.refs_3_.refs_9_.refs_21_.refs_13_.refs_25_), channel_id=1, source_target_pairs={{1,0},{0,1},{3,2},{2,3},{5,4},{4,5},{7,6},{6,7},{9,8},{8,9},{11,10... | collective-permute-start | bytes 7077896 | tf_op jit(solution)/shard_map/ppermute | solution.py:37
  229.1 70.6 %collective-permute-start.17 = (bf16[1536,768]{1,0:T(8,128)(2,1)}, bf16[1536,768]{1,0:T(8,128)(2,1)}, u32[]{:S(2)}, u32[]{:S(2)}) collective-permute-start(bf16[1536,768]{1,0:T(8,128)(2,1)} %shard_map.78.refs_2_.refs_3_.refs_9_.refs_21_.refs_13_.refs_25_), channel_id=1, source_target_pairs={{16,0},{17,1},{18,2},{19,3},{20,4},{21,5},{22,6},{23,7},{24,8},{25... | collective-permute-start | bytes 7077896 | tf_op jit(solution)/shard_map/ppermute | solution.py:37
  230.9 68.8 %collective-permute-start.16 = (bf16[1024,768]{1,0:T(8,128)(2,1)S(1)}, bf16[1024,768]{1,0:T(8,128)(2,1)}, u32[]{:S(2)}, u32[]{:S(2)}) collective-permute-start(bf16[1024,768]{1,0:T(8,128)(2,1)S(1)} %slice.44), channel_id=1, source_target_pairs={{2,0},{3,1},{0,2},{1,3},{6,4},{7,5},{4,6},{5,7},{10,8},{11,9},{8,1... | collective-permute-start | bytes 4718600 | tf_op jit(solution)/shard_map/ppermute | solution.py:37
  230.9 68.7 %collective-permute-start.15 = (bf16[1024,768]{1,0:T(8,128)(2,1)S(1)}, bf16[1024,768]{1,0:T(8,128)(2,1)}, u32[]{:S(2)}, u32[]{:S(2)}) collective-permute-start(bf16[1024,768]{1,0:T(8,128)(2,1)S(1)} %slice.44), channel_id=1, source_target_pairs={{4,0},{5,1},{6,2},{7,3},{0,4},{1,5},{2,6},{3,7},{12,8},{13,9},{14,... | collective-permute-start | bytes 4718600 | tf_op jit(solution)/shard_map/ppermute | solution.py:37
  299.7 7.3 %collective-permute-start.24 = (bf16[1536,768]{1,0:T(8,128)(2,1)}, bf16[1536,768]{1,0:T(8,128)(2,1)S(1)}, u32[]{:S(2)}, u32[]{:S(2)}) collective-permute-start(bf16[1536,768]{1,0:T(8,128)(2,1)} %collective-permute-done.18.refs_10_.refs_14_), channel_id=1, source_target_pairs={{8,0},{9,1},{10,2},{11,3},{12,4},{13,5},{14,6},{15,7},{0,8},{1,9},... | collective-permute-start | bytes 7077896 | tf_op jit(solution)/shard_map/ppermute | solution.py:37
  302.7 40.5 %collective-permute-start.22 = (bf16[1024,768]{1,0:T(8,128)(2,1)}, bf16[1024,768]{1,0:T(8,128)(2,1)}, u32[]{:S(2)}, u32[]{:S(2)}) collective-permute-start(bf16[1024,768]{1,0:T(8,128)(2,1)} %collective-permute-done.16.refs_5_.refs_4_.refs_27_), channel_id=1, source_target_pairs={{16,0},{17,1},{18,2},{19,3},{20,4},{21,5},{22,6},{23,7},{24,8},{25... | collective-permute-start | bytes 4718600 | tf_op jit(solution)/shard_map/ppermute | solution.py:37
  303.9 39.3 %collective-permute-start.23 = (bf16[1024,768]{1,0:T(8,128)(2,1)}, bf16[1024,768]{1,0:T(8,128)(2,1)}, u32[]{:S(2)}, u32[]{:S(2)}) collective-permute-start(bf16[1024,768]{1,0:T(8,128)(2,1)} %collective-permute-done.15.refs_13_.refs_17_), channel_id=1, source_target_pairs={{1,0},{0,1},{3,2},{2,3},{5,4},{4,5},{7,6},{6,7},{9,8},{8,9},{11,10... | collective-permute-start | bytes 4718600 | tf_op jit(solution)/shard_map/ppermute | solution.py:37
  307.0 36.2 %collective-permute-start.25 = (bf16[1024,768]{1,0:T(8,128)(2,1)}, bf16[1024,768]{1,0:T(8,128)(2,1)}, u32[]{:S(2)}, u32[]{:S(2)}) collective-permute-start(bf16[1024,768]{1,0:T(8,128)(2,1)} %collective-permute-done.15.refs_13_.refs_17_), channel_id=1, source_target_pairs={{8,0},{9,1},{10,2},{11,3},{12,4},{13,5},{14,6},{15,7},{0,8},{1,9},... | collective-permute-start | bytes 4718600 | tf_op jit(solution)/shard_map/ppermute | solution.py:37
  307.4 35.8 %collective-permute-start.21 = (bf16[512,768]{1,0:T(8,128)(2,1)}, bf16[512,768]{1,0:T(8,128)(2,1)}, u32[]{:S(2)}, u32[]{:S(2)}) collective-permute-start(bf16[512,768]{1,0:T(8,128)(2,1)} %slice.45), channel_id=1, source_target_pairs={{2,0},{3,1},{0,2},{1,3},{6,4},{7,5},{4,6},{5,7},{10,8},{11,9},{8,1... | collective-permute-start | bytes 2359304 | tf_op jit(solution)/shard_map/ppermute | solution.py:37
  307.4 35.8 %collective-permute-start.20 = (bf16[512,768]{1,0:T(8,128)(2,1)}, bf16[512,768]{1,0:T(8,128)(2,1)}, u32[]{:S(2)}, u32[]{:S(2)}) collective-permute-start(bf16[512,768]{1,0:T(8,128)(2,1)} %slice.45), channel_id=1, source_target_pairs={{4,0},{5,1},{6,2},{7,3},{0,4},{1,5},{2,6},{3,7},{12,8},{13,9},{14,... | collective-permute-start | bytes 2359304 | tf_op jit(solution)/shard_map/ppermute | solution.py:37
  343.2 4.5 collective-permute-start.30
  347.7 20.5 %collective-permute-start.31 = (bf16[1024,768]{1,0:T(8,128)(2,1)}, bf16[1024,768]{1,0:T(8,128)(2,1)S(1)}, u32[]{:S(2)}, u32[]{:S(2)}) collective-permute-start(bf16[1024,768]{1,0:T(8,128)(2,1)} %collective-permute-done.23.refs_15_.refs_19_), channel_id=1, source_target_pairs={{8,0},{9,1},{10,2},{11,3},{12,4},{13,5},{14,6},{15,7},{0,8},{1,9},... | collective-permute-start | bytes 4718600 | tf_op jit(solution)/shard_map/ppermute | solution.py:37
  348.1 19.9 %collective-permute-start.28 = (bf16[512,768]{1,0:T(8,128)(2,1)}, bf16[512,768]{1,0:T(8,128)(2,1)S(1)}, u32[]{:S(2)}, u32[]{:S(2)}) collective-permute-start(bf16[512,768]{1,0:T(8,128)(2,1)} %collective-permute-done.21.refs_6_.refs_5_.refs_28_), channel_id=1, source_target_pairs={{16,0},{17,1},{18,2},{19,3},{20,4},{21,5},{22,6},{23,7},{24,8},{25... | collective-permute-start | bytes 2359304 | tf_op jit(solution)/shard_map/ppermute | solution.py:37
  349.3 18.9 %collective-permute-start.29 = (bf16[512,768]{1,0:T(8,128)(2,1)}, bf16[512,768]{1,0:T(8,128)(2,1)S(1)}, u32[]{:S(2)}, u32[]{:S(2)}) collective-permute-start(bf16[512,768]{1,0:T(8,128)(2,1)} %collective-permute-done.20.refs_14_.refs_18_), channel_id=1, source_target_pairs={{1,0},{0,1},{3,2},{2,3},{5,4},{4,5},{7,6},{6,7},{9,8},{8,9},{11,10... | collective-permute-start | bytes 2359304 | tf_op jit(solution)/shard_map/ppermute | solution.py:37
  350.5 17.5 %collective-permute-start.27 = (bf16[256,768]{1,0:T(8,128)(2,1)S(1)}, bf16[256,768]{1,0:T(8,128)(2,1)S(1)}, u32[]{:S(2)}, u32[]{:S(2)}) collective-permute-start(bf16[256,768]{1,0:T(8,128)(2,1)S(1)} %slice.52), channel_id=1, source_target_pairs={{2,0},{3,1},{0,2},{1,3},{6,4},{7,5},{4,6},{5,7},{10,8},{11,9},{8,1... | collective-permute-start | bytes 1179656 | tf_op jit(solution)/shard_map/ppermute | solution.py:37
  350.5 17.5 %collective-permute-start.26 = (bf16[256,768]{1,0:T(8,128)(2,1)S(1)}, bf16[256,768]{1,0:T(8,128)(2,1)S(1)}, u32[]{:S(2)}, u32[]{:S(2)}) collective-permute-start(bf16[256,768]{1,0:T(8,128)(2,1)S(1)} %slice.52), channel_id=1, source_target_pairs={{4,0},{5,1},{6,2},{7,3},{0,4},{1,5},{2,6},{3,7},{12,8},{13,9},{14,... | collective-permute-start | bytes 1179656 | tf_op jit(solution)/shard_map/ppermute | solution.py:37
  368.0 71.5 %copy-start.18 = (bf16[256,768]{1,0:T(8,128)(2,1)}, bf16[256,768]{1,0:T(8,128)(2,1)S(1)}, u32[]{:S(2)}) copy-start(bf16[256,768]{1,0:T(8,128)(2,1)S(1)} %collective-permute-done.27.refs_7_) | copy-start | bytes 1179652
  368.0 72.9 %copy-start.19 = (bf16[256,768]{1,0:T(8,128)(2,1)}, bf16[256,768]{1,0:T(8,128)(2,1)S(1)}, u32[]{:S(2)}) copy-start(bf16[256,768]{1,0:T(8,128)(2,1)S(1)} %collective-permute-done.26.refs_31_) | copy-start | bytes 1179652
  368.2 71.3 %copy-start.12 = (bf16[512,768]{1,0:T(8,128)(2,1)}, bf16[512,768]{1,0:T(8,128)(2,1)S(1)}, u32[]{:S(2)}) copy-start(bf16[512,768]{1,0:T(8,128)(2,1)S(1)} %collective-permute-done.29.refs_16_.refs_20_) | copy-start | bytes 2359300
  368.2 75.2 %copy-start.5 = (bf16[1024,768]{1,0:T(8,128)(2,1)}, bf16[1024,768]{1,0:T(8,128)(2,1)S(1)}, u32[]{:S(2)}) copy-start(bf16[1024,768]{1,0:T(8,128)(2,1)S(1)} %collective-permute-done.31.refs_19_.refs_23_) | copy-start | bytes 4718596
  368.2 5.3 collective-permute-start.36
  371.5 56.0 %collective-permute-start.35 = (bf16[1536,768]{1,0:T(8,128)(2,1)S(1)}, bf16[1536,768]{1,0:T(8,128)(2,1)S(1)}, u32[]{:S(2)}, u32[]{:S(2)}) collective-permute-start(bf16[1536,768]{1,0:T(8,128)(2,1)S(1)} %copy-done), channel_id=1, source_target_pairs={{1,0},{0,1},{3,2},{2,3},{5,4},{4,5},{7,6},{6,7},{9,8},{8,9},{11,10... | collective-permute-start | bytes 7077896 | tf_op jit(solution)/shard_map/ppermute | solution.py:37
  371.8 55.8 %collective-permute-start.34 = (bf16[1536,768]{1,0:T(8,128)(2,1)S(1)}, bf16[1536,768]{1,0:T(8,128)(2,1)S(1)}, u32[]{:S(2)}, u32[]{:S(2)}) collective-permute-start(bf16[1536,768]{1,0:T(8,128)(2,1)S(1)} %copy-done), channel_id=1, source_target_pairs={{16,0},{17,1},{18,2},{19,3},{20,4},{21,5},{22,6},{23,7},{24,8},{25... | collective-permute-start | bytes 7077896 | tf_op jit(solution)/shard_map/ppermute | solution.py:37
  373.4 67.1 %copy-start.13 = (bf16[512,768]{1,0:T(8,128)(2,1)}, bf16[512,768]{1,0:T(8,128)(2,1)S(1)}, u32[]{:S(2)}) copy-start(bf16[512,768]{1,0:T(8,128)(2,1)S(1)} %collective-permute-done.36.refs_20_.refs_24_) | copy-start | bytes 2359300
  373.4 54.1 %collective-permute-start.37 = (bf16[1536,768]{1,0:T(8,128)(2,1)S(1)}, bf16[1536,768]{1,0:T(8,128)(2,1)S(1)}, u32[]{:S(2)}, u32[]{:S(2)}) collective-permute-start(bf16[1536,768]{1,0:T(8,128)(2,1)S(1)} %copy-done), channel_id=1, source_target_pairs={{8,0},{9,1},{10,2},{11,3},{12,4},{13,5},{14,6},{15,7},{0,8},{1,9},... | collective-permute-start | bytes 7077896 | tf_op jit(solution)/shard_map/ppermute | solution.py:37
  373.8 51.7 %collective-permute-start.33 = (bf16[768,768]{1,0:T(8,128)(2,1)S(1)}, bf16[768,768]{1,0:T(8,128)(2,1)S(1)}, u32[]{:S(2)}, u32[]{:S(2)}) collective-permute-start(bf16[768,768]{1,0:T(8,128)(2,1)S(1)} %slice.53), channel_id=1, source_target_pairs={{2,0},{3,1},{0,2},{1,3},{6,4},{7,5},{4,6},{5,7},{10,8},{11,9},{8,1... | collective-permute-start | bytes 3538952 | tf_op jit(solution)/shard_map/ppermute | solution.py:37
  373.8 53.7 %collective-permute-start.32 = (bf16[768,768]{1,0:T(8,128)(2,1)S(1)}, bf16[768,768]{1,0:T(8,128)(2,1)}, u32[]{:S(2)}, u32[]{:S(2)}) collective-permute-start(bf16[768,768]{1,0:T(8,128)(2,1)S(1)} %slice.53), channel_id=1, source_target_pairs={{4,0},{5,1},{6,2},{7,3},{0,4},{1,5},{2,6},{3,7},{12,8},{13,9},{14,... | collective-permute-start | bytes 3538952 | tf_op jit(solution)/shard_map/ppermute | solution.py:37
  425.6 41.9 %copy-start.6 = (bf16[768,768]{1,0:T(8,128)(2,1)}, bf16[768,768]{1,0:T(8,128)(2,1)S(1)}, u32[]{:S(2)}) copy-start(bf16[768,768]{1,0:T(8,128)(2,1)S(1)} %collective-permute-done.33.refs_8_) | copy-start | bytes 3538948
  427.6 5.2 collective-permute-start.44
  428.6 10.8 %collective-permute-start.40 = (bf16[256,768]{1,0:T(8,128)(2,1)S(1)}, bf16[256,768]{1,0:T(8,128)(2,1)S(1)}, u32[]{:S(2)}, u32[]{:S(2)}) collective-permute-start(bf16[256,768]{1,0:T(8,128)(2,1)S(1)} %collective-permute-done.27.refs_7_), channel_id=1, source_target_pairs={{16,0},{17,1},{18,2},{19,3},{20,4},{21,5},{22,6},{23,7},{24,8},{25... | collective-permute-start | bytes 1179656 | tf_op jit(solution)/shard_map/ppermute | solution.py:37
  428.9 10.5 %collective-permute-start.42 = (bf16[256,768]{1,0:T(8,128)(2,1)S(1)}, bf16[256,768]{1,0:T(8,128)(2,1)}, u32[]{:S(2)}, u32[]{:S(2)}) collective-permute-start(bf16[256,768]{1,0:T(8,128)(2,1)S(1)} %collective-permute-done.26.refs_31_), channel_id=1, source_target_pairs={{1,0},{0,1},{3,2},{2,3},{5,4},{4,5},{7,6},{6,7},{9,8},{8,9},{11,10... | collective-permute-start | bytes 1179656 | tf_op jit(solution)/shard_map/ppermute | solution.py:37
  432.8 8.1 %collective-permute-start.45 = (bf16[256,768]{1,0:T(8,128)(2,1)S(1)}, bf16[256,768]{1,0:T(8,128)(2,1)S(1)}, u32[]{:S(2)}, u32[]{:S(2)}) collective-permute-start(bf16[256,768]{1,0:T(8,128)(2,1)S(1)} %collective-permute-done.26.refs_31_), channel_id=1, source_target_pairs={{8,0},{9,1},{10,2},{11,3},{12,4},{13,5},{14,6},{15,7},{0,8},{1,9},... | collective-permute-start | bytes 1179656 | tf_op jit(solution)/shard_map/ppermute | solution.py:37
  433.2 34.9 %collective-permute-start.39 = (bf16[512,768]{1,0:T(8,128)(2,1)S(1)}, bf16[512,768]{1,0:T(8,128)(2,1)}, u32[]{:S(2)}, u32[]{:S(2)}) collective-permute-start(bf16[512,768]{1,0:T(8,128)(2,1)S(1)} %slice.54), channel_id=1, source_target_pairs={{2,0},{3,1},{0,2},{1,3},{6,4},{7,5},{4,6},{5,7},{10,8},{11,9},{8,1... | collective-permute-start | bytes 2359304 | tf_op jit(solution)/shard_map/ppermute | solution.py:37
  433.2 36.9 %collective-permute-start.38 = (bf16[512,768]{1,0:T(8,128)(2,1)S(1)}, bf16[512,768]{1,0:T(8,128)(2,1)}, u32[]{:S(2)}, u32[]{:S(2)}) collective-permute-start(bf16[512,768]{1,0:T(8,128)(2,1)S(1)} %slice.54), channel_id=1, source_target_pairs={{4,0},{5,1},{6,2},{7,3},{0,4},{1,5},{2,6},{3,7},{12,8},{13,9},{14,... | collective-permute-start | bytes 2359304 | tf_op jit(solution)/shard_map/ppermute | solution.py:37
  439.5 30.6 %collective-permute-start.43 = (bf16[768,768]{1,0:T(8,128)(2,1)}, bf16[768,768]{1,0:T(8,128)(2,1)S(1)}, u32[]{:S(2)}, u32[]{:S(2)}) collective-permute-start(bf16[768,768]{1,0:T(8,128)(2,1)} %collective-permute-done.32.refs_32_), channel_id=1, source_target_pairs={{1,0},{0,1},{3,2},{2,3},{5,4},{4,5},{7,6},{6,7},{9,8},{8,9},{11,10... | collective-permute-start | bytes 3538952 | tf_op jit(solution)/shard_map/ppermute | solution.py:37
  440.5 29.6 %collective-permute-start.41 = (bf16[768,768]{1,0:T(8,128)(2,1)S(1)}, bf16[768,768]{1,0:T(8,128)(2,1)S(1)}, u32[]{:S(2)}, u32[]{:S(2)}) collective-permute-start(bf16[768,768]{1,0:T(8,128)(2,1)S(1)} %collective-permute-done.33.refs_8_), channel_id=1, source_target_pairs={{16,0},{17,1},{18,2},{19,3},{20,4},{21,5},{22,6},{23,7},{24,8},{25... | collective-permute-start | bytes 3538952 | tf_op jit(solution)/shard_map/ppermute | solution.py:37
  441.7 28.4 %collective-permute-start.46 = (bf16[768,768]{1,0:T(8,128)(2,1)}, bf16[768,768]{1,0:T(8,128)(2,1)}, u32[]{:S(2)}, u32[]{:S(2)}) collective-permute-start(bf16[768,768]{1,0:T(8,128)(2,1)} %collective-permute-done.32.refs_32_), channel_id=1, source_target_pairs={{8,0},{9,1},{10,2},{11,3},{12,4},{13,5},{14,6},{15,7},{0,8},{1,9},... | collective-permute-start | bytes 3538952 | tf_op jit(solution)/shard_map/ppermute | solution.py:37
  470.1 3.1 collective-permute-start.49
  473.3 1.9 collective-permute-start.50
  475.2 19.6 %collective-permute-start.51 = (bf16[768,768]{1,0:T(8,128)(2,1)S(1)}, bf16[768,768]{1,0:T(8,128)(2,1)S(1)}, u32[]{:S(2)}, u32[]{:S(2)}) collective-permute-start(bf16[768,768]{1,0:T(8,128)(2,1)S(1)} %collective-permute-done.43.refs_34_.refs_35_), channel_id=1, source_target_pairs={{8,0},{9,1},{10,2},{11,3},{12,4},{13,5},{14,6},{15,7},{0,8},{1,9},... | collective-permute-start | bytes 3538952 | tf_op jit(solution)/shard_map/ppermute | solution.py:37
  475.6 19.2 %collective-permute-start.47 = (bf16[512,768]{1,0:T(8,128)(2,1)}, bf16[512,768]{1,0:T(8,128)(2,1)S(1)}, u32[]{:S(2)}, u32[]{:S(2)}) collective-permute-start(bf16[512,768]{1,0:T(8,128)(2,1)} %collective-permute-done.39.refs_9_), channel_id=1, source_target_pairs={{16,0},{17,1},{18,2},{19,3},{20,4},{21,5},{22,6},{23,7},{24,8},{25... | collective-permute-start | bytes 2359304 | tf_op jit(solution)/shard_map/ppermute | solution.py:37
  475.8 19.0 %collective-permute-start.48 = (bf16[512,768]{1,0:T(8,128)(2,1)}, bf16[512,768]{1,0:T(8,128)(2,1)S(1)}, u32[]{:S(2)}, u32[]{:S(2)}) collective-permute-start(bf16[512,768]{1,0:T(8,128)(2,1)} %collective-permute-done.38.refs_33_), channel_id=1, source_target_pairs={{1,0},{0,1},{3,2},{2,3},{5,4},{4,5},{7,6},{6,7},{9,8},{8,9},{11,10... | collective-permute-start | bytes 2359304 | tf_op jit(solution)/shard_map/ppermute | solution.py:37
  494.8 30.7 %collective-permute-start.52 = (bf16[1536,768]{1,0:T(8,128)(2,1)}, bf16[1536,768]{1,0:T(8,128)(2,1)S(1)}, u32[]{:S(2)}, u32[]{:S(2)}) collective-permute-start(bf16[1536,768]{1,0:T(8,128)(2,1)} %shard_map.83), channel_id=1, source_target_pairs={{0,0},{1,1},{8,2},{9,3},{4,4},{5,5},{12,6},{13,7},{2,8},{3,9},{10,... | collective-permute-start | bytes 7077896 | tf_op jit(solution)/shard_map/ppermute | solution.py:37
  497.0 28.4 %collective-permute-start.53 = (bf16[512,768]{1,0:T(8,128)(2,1)S(1)}, bf16[512,768]{1,0:T(8,128)(2,1)S(1)}, u32[]{:S(2)}, u32[]{:S(2)}) collective-permute-start(bf16[512,768]{1,0:T(8,128)(2,1)S(1)} %collective-permute-done.48.refs_36_), channel_id=1, source_target_pairs={{8,0},{9,1},{10,2},{11,3},{12,4},{13,5},{14,6},{15,7},{0,8},{1,9},... | collective-permute-start | bytes 2359304 | tf_op jit(solution)/shard_map/ppermute | solution.py:37
  525.5 33.7 %collective-permute-start.54 = (bf16[1024,768]{1,0:T(8,128)(2,1)}, bf16[1024,768]{1,0:T(8,128)(2,1)S(1)}, u32[]{:S(2)}, u32[]{:S(2)}) collective-permute-start(bf16[1024,768]{1,0:T(8,128)(2,1)} %shard_map.85), channel_id=1, source_target_pairs={{0,0},{1,1},{8,2},{9,3},{4,4},{5,5},{12,6},{13,7},{2,8},{3,9},{10,... | collective-permute-start | bytes 4718600 | tf_op jit(solution)/shard_map/ppermute | solution.py:37
  545.7 13.5 %collective-permute-start.55 = (bf16[512,768]{1,0:T(8,128)(2,1)}, bf16[512,768]{1,0:T(8,128)(2,1)S(1)}, u32[]{:S(2)}, u32[]{:S(2)}) collective-permute-start(bf16[512,768]{1,0:T(8,128)(2,1)} %shard_map.86), channel_id=1, source_target_pairs={{0,0},{1,1},{8,2},{9,3},{4,4},{5,5},{12,6},{13,7},{2,8},{3,9},{10,... | collective-permute-start | bytes 2359304 | tf_op jit(solution)/shard_map/ppermute | solution.py:37
  (24 other events, 357.7 us)
Sparse Core Ops, SparseCore 0:
  132.6 58.4 all-gather.1

commit v3 on v2

--- a/solution.py
+++ b/solution.py
@@ -60,13 +60,15 @@
         return self.held[name]
 
 
-def product(terms, mask, own, base, tile, scale, out_dtype, wait=(), span=None):
+def product(terms, mask, own, base, tile, scale, out_dtype, wait=(), span=None, cuts=()):
     height = sum(v.shape[0] for v in terms[0][0][0])
     width = terms[0][2][0][0].shape[1]
     order = sum(v.shape[0] for unit in terms[0][2] for v in unit)
     block = 128
     first_tile, end_tile = span or (0, height // tile)
     tiles = end_tile - first_tile
+    ends = [sum(cuts[:i]) for i in range(len(cuts) + 1)]
+    runs = list(zip(ends, ends[1:]))
     arrays, plan_a, plan_b, places = [], [], [], []
     panels = 0
     for row_units, row_places, col_units, col_places in terms:
@@ -102,7 +104,7 @@
         operands = [refs.pop(0) for _ in range(count)]
         own_ref = refs.pop(0) if own is not None else None
         base_ref = refs.pop(0) if base is not None else None
-        out_ref, a_buf, b_buf, a_sem, b_sem = refs
+        out_ref, *cut_refs, a_buf, b_buf, a_sem, b_sem = refs
         step = pl.program_id(0)
         slot = step % 2
 
@@ -176,8 +178,19 @@
                     value = 2.0 * own_ref[at].astype(jnp.float32) - value
                 kept = mask_ref[(first_tile + step) * (tile // block) + i, j]
                 out_ref[at] = (value * kept).astype(out_dtype)
+        for (low, high), cut_ref in zip(runs, cut_refs):
+
+            @pl.when((step >= low) & (step < high))
+            def _():
+                cut_ref[...] = out_ref[...]
 
     smem = pl.BlockSpec(memory_space=pltpu.SMEM)
+    out_shape = [jax.ShapeDtypeStruct((tiles * tile, width), out_dtype)]
+    out_specs = [pl.BlockSpec((tile, width), lambda i: (i, 0))]
+    for low, high in runs:
+        out_shape.append(jax.ShapeDtypeStruct(((high - low) * tile, width), out_dtype))
+        place = functools.partial(lambda low, high, i: (jnp.clip(i, low, high - 1) - low, 0), low, high)
+        out_specs.append(pl.BlockSpec((tile, width), place))
     tiled = pl.BlockSpec((tile, width), lambda i: (first_tile + i, 0))
     in_specs, operands = [smem] * len(places), list(places)
     in_specs, operands = in_specs + [pl.BlockSpec(memory_space=pl.ANY)] * len(wait), operands + list(wait)
@@ -191,9 +204,9 @@
     return pl.pallas_call(
         kernel,
         grid=(tiles,),
-        out_shape=jax.ShapeDtypeStruct((tiles * tile, width), out_dtype),
+        out_shape=out_shape if cuts else out_shape[0],
         in_specs=in_specs,
-        out_specs=pl.BlockSpec((tile, width), lambda i: (i, 0)),
+        out_specs=out_specs if cuts else out_specs[0],
         scratch_shapes=[
             pltpu.VMEM((2, tile, deep), jnp.bfloat16),
             pltpu.VMEM((panels, order, width), jnp.bfloat16),
@@ -344,8 +357,8 @@
     def partial(rows, places, cols, col_places, base=None, wait=()):
         return product([(rows, places, cols, col_places)], None, None, base, tile, 1.0, jnp.float32, wait)
 
-    def finish(terms, kept, own, base, wait=(), span=None):
-        return product(terms, kept, own, base, tile, inv_root, jnp.bfloat16, wait, span)
+    def finish(terms, kept, own, base, wait=(), span=None, cuts=()):
+        return product(terms, kept, own, base, tile, inv_root, jnp.bfloat16, wait, span, cuts)
 
     half = height // tile // 2 * tile
 
@@ -401,7 +414,8 @@
         + sends_core("own")
     )
     all_strips, tables = gather_strips(r["sent"], strips.shape[0] * strips.shape[1], devices)
-    r.run(sends_x("zl") + sends_y("f0", "f1") + rest_core("own") + sends_core("f0"))
+    beside = [("y also",) + send[1:] for send in sends_y("f1")]
+    r.run(sends_x("zl") + sends_y("f0") + beside + rest_core("own") + sends_core("f0"))
     zero_cols = cols_of("own") + cols_of("zl")
     base = partial(rows_of("own"), own_places, zero_cols, col_places)
     apart = sends_core("f1") + rest_core("f0", "f1")
@@ -409,7 +423,12 @@
     zero_cols = cols_of("own") + cols_of("zl")
     far_rows = rows_of("f0", "f1")
     old_rows = rows_of("own") + far_rows
-    zeroth = finish([(far_rows, far_places, zero_cols, col_places)], kept_zero, None, r["base"])
+    tiles = height // tile
+    few, some = max(1, tiles // 6), max(1, tiles // 3)
+    parts = {"p": [tiles - some, some], "q": [few, tiles - some - few, some]}
+    zeroth, v0, v1 = finish(
+        [(far_rows, far_places, zero_cols, col_places)], kept_zero, None, r["base"], cuts=parts["p"]
+    )
 
     lone = jnp.zeros((1,), jnp.int32)
     tables, zeroth = tie(tables, zeroth)
@@ -420,10 +439,6 @@
         all_strips, tables, patterns[2], lay.cols, my_row * lay.cols, 1, my_row * tall, 0, height, width, True
     )
 
-    tiles = height // tile
-    few, some = max(1, tiles // 6), max(1, tiles // 3)
-    parts = {"p": [tiles - some, some], "q": [few, tiles - some - few, some]}
-
     def start(v, tag):
         pieces = cut(v, *[part * tile for part in parts[tag]])
         return dict({f"v{i}{tag}": piece for i, piece in enumerate(pieces)}, **{"own" + tag: v})
@@ -438,7 +453,7 @@
         return cols_of("own" + tag) + cols_of(*chunks("z", tag))
 
     r = Rounds(lay)
-    r.held = start(zeroth, "p")
+    r.held = dict(ownp=zeroth, v0p=v0, v1p=v1)
     first = partial(old_rows, row_places, [[field_cols]], lone, None, (zeroth,))
     r.run(
         sends_z("p", 0) + sends_x("ownp") + sends_y("ownp") + sends_core("ownp"),

time: 571 us -> 569 us (level)
  transfers between devices with their start and end apart: 57 -> 57, of which waited for: 24 -> 28; matrix products, arithmetic and copies ran while one was open for 5% -> 4% of each run, Pallas kernels for 31% -> 31%
where the time goes in v3:
time: 569 us; the launch traced here: 566 us
  waiting for transfers between devices  258 us (45%)
  Pallas kernels  192 us (34%)
  starting transfers between devices  70.2 us (12%)
  other arithmetic  15.9 us (3%)
  local copies, waits for them, and re-layouts  15.8 us (3%)
  between operations  14.5 us (3%)
    ppermute x56, waiting for transfers between devices, send(): return lax.ppermute(value, AXES, self.perm(source))  258 us
    pallas_call x8, Pallas kernels, product(): pl.pallas_call(kernel, grid=(tiles,), out_shape=out_shape if cuts else ou...  162 us
    ppermute x56, starting transfers between devices, send(): return lax.ppermute(value, AXES, self.perm(source))  70.1 us
    pallas_call x2, Pallas kernels, field_panel(): pl.pallas_call(kernel, grid=(slabs,), out_shape=jax.ShapeDtypeStruct(shap...  29.6 us
  transfers between devices with their start and end apart: 57, of which 28 were waited for; matrix products, arithmetic and copies ran while one was open for 4% of the time, Pallas kernels for 31%

profile of v3, /device:TPU:1, one launch (start us, length us, event | category | flops | bytes accessed | tf_op | source)
XLA Modules:
  0.0 566.2 jit_solution(6725699283922432755)
XLA Ops:
  7.2 4.7 collective-permute-start.1
  12.0 2.8 fusion.5
  14.8 2.0 collective-permute-start
  19.0 1.3 select_reduce_fusion.5
  26.7 1.5 pad_maximum_fusion
  28.1 1.4 slice_bitcast_fusion
  30.2 36.0 %collective-permute-done.refs_7_.refs_8_ = bf16[768,768]{1,0:T(8,128)(2,1)} collective-permute-done((bf16[768,768]{1,0:T(8,128)(2,1)}, bf16[768,768]{1,0:T(8,128)(2,1)}, u32[]{:S(2)}, u32[]{:S(2)}) %collective-permute-start) | collective-permute-done | bytes 1179680 | tf_op jit(solution)/shard_map/ppermute | solution.py:37
  66.2 7.1 %collective-permute-start.3 = (bf16[1536,768]{1,0:T(8,128)(2,1)S(1)}, bf16[1536,768]{1,0:T(8,128)(2,1)S(1)}, u32[]{:S(2)}, u32[]{:S(2)}) collective-permute-start(bf16[1536,768]{1,0:T(8,128)(2,1)S(1)} %copy-done.4), channel_id=1, source_target_pairs={{8,0},{9,1},{0,2},{1,3},{12,4},{13,5},{4,6},{5,7},{10,8},{11,9},{2... | collective-permute-start | bytes 7077896 | tf_op jit(solution)/shard_map/ppermute | solution.py:37
  73.4 1.5 collective-permute-start.5
  74.9 1.2 collective-permute-start.4
  76.1 2.5 collective-permute-start.2
  78.7 27.6 %collective-permute-done.2.refs_8_.refs_9_ = bf16[768,768]{1,0:T(8,128)(2,1)S(1)} collective-permute-done((bf16[768,768]{1,0:T(8,128)(2,1)S(1)}, bf16[768,768]{1,0:T(8,128)(2,1)S(1)}, u32[]{:S(2)}, u32[]{:S(2)}) %collective-permute-start.2) | collective-permute-done | bytes 1179680 | tf_op jit(solution)/shard_map/ppermute | solution.py:37
  106.3 16.3 %collective-permute-done.3.refs_4_.refs_5_ = bf16[1536,768]{1,0:T(8,128)(2,1)S(1)} collective-permute-done((bf16[1536,768]{1,0:T(8,128)(2,1)S(1)}, bf16[1536,768]{1,0:T(8,128)(2,1)S(1)}, u32[]{:S(2)}, u32[]{:S(2)}) %collective-permute-start.3) | collective-permute-done | bytes 2359328 | tf_op jit(solution)/shard_map/ppermute | solution.py:37
  122.5 1.4 copy-done.24
  124.0 1.4 copy-done.26
  127.3 5.2 collective-permute-start.10
  133.0 1.2 collective-permute-start.8
  134.3 2.7 collective-permute-done.10.refs_9_.refs_7_
  137.3 24.6 %collective-permute-done.9.refs_10_.refs_11_ = bf16[768,768]{1,0:T(8,128)(2,1)} collective-permute-done((bf16[768,768]{1,0:T(8,128)(2,1)}, bf16[768,768]{1,0:T(8,128)(2,1)}, u32[]{:S(2)}, u32[]{:S(2)}) %collective-permute-start.9) | collective-permute-done | bytes 1179680 | tf_op jit(solution)/shard_map/ppermute | solution.py:37
  161.9 29.1 %collective-permute-done.8.refs_9_.refs_10_ = bf16[768,768]{1,0:T(8,128)(2,1)} collective-permute-done((bf16[768,768]{1,0:T(8,128)(2,1)}, bf16[768,768]{1,0:T(8,128)(2,1)}, u32[]{:S(2)}, u32[]{:S(2)}) %collective-permute-start.8) | collective-permute-done | bytes 1179680 | tf_op jit(solution)/shard_map/ppermute | solution.py:37
  193.5 15.5 %shard_map.77.refs_15_ = f32[1536,768]{1,0:T(8,128)} custom-call(s32[4]{0:T(128)} %get-tuple-element.251.refs_0_, s32[4]{0:T(128)} %pad_add_fusion.2.refs_1_.refs_3_, bf16[1536,768]{1,0:T(8,128)(2,1)} %collective-permute-done.1.refs_2_.refs_6_.refs_3_.refs_4_, bf16[1536,768]{1,0:T(8,128)(2,1)} %collective-permute-done.4.refs_3_.refs_4_, ...), custom_call_target="tpu_custom_call" | custom-call | flops 7247757312 | bytes 23592960 | tf_op jit(solution)/shard_map/pallas_call | solution.py:204
  210.7 16.3 %shard_map.78 = (bf16[1536,768]{1,0:T(8,128)(2,1)}, bf16[1024,768]{1,0:T(8,128)(2,1)}, bf16[512,768]{1,0:T(8,128)(2,1)}) custom-call(s32[4]{0:T(128)} %get-tuple-element.252.refs_0_.refs_2_, s32[4]{0:T(128)} %pad_add_fusion.2.refs_1_.refs_3_, f32[12,6]{1,0:T(8,128)} %get-tuple-element.255.refs_2_, ...), custom_call_target="tpu_custom_call" | custom-call | flops 7247757312 | bytes 23592960 | tf_op jit(solution)/shard_map/pallas_call | solution.py:204
  230.6 11.1 %shard_map.79.refs_3_ = bf16[6144,768]{1,0:T(8,128)(2,1)} custom-call(s32[3]{0:T(128)} %pad_add_fusion.3.scalar_ref, s32[3,32,64]{2,1,0:T(8,128)} %bitcast.50, s32[48,48]{1,0:T(8,128)} %get-tuple-element.502.pattern_ref, bf16[8704,128]{1,0:T(8,128)(2,1)} %all-gather.2.cloned.1.call-done.strips_ref), custom_call_target="tpu_custom_call" | custom-call | flops 37748736 | bytes 37748736 | tf_op jit(solution)/shard_map/pallas_call | solution.py:272
  241.8 18.4 %shard_map.81.refs_7_ = bf16[1536,6144]{1,0:T(8,128)(2,1)} custom-call(s32[3]{0:T(128)} %pad_add_fusion.4.scalar_ref, s32[3,32,64]{2,1,0:T(8,128)} %bitcast.51, s32[48,48]{1,0:T(8,128)} %get-tuple-element.502.pattern_ref, bf16[8704,128]{1,0:T(8,128)(2,1)} %all-gather.2.cloned.1.call-done.strips_ref), custom_call_target="tpu_custom_call" | custom-call | flops 75497472 | bytes 75497472 | tf_op jit(solution)/shard_map/pallas_call | solution.py:272
  260.2 23.5 %shard_map.80.refs_8_ = f32[1536,768]{1,0:T(8,128)} custom-call(s32[8]{0:T(128)} %stack.134.refs_0_, s32[1]{0:T(128)} %constant.112.clone.1.refs_1_.refs_0_, bf16[1536,768]{1,0:T(8,128)(2,1)} %get-tuple-element.475.refs_2_.refs_3_.refs_9_.refs_21_.refs_13_.refs_25_, bf16[6144,768]{1,0:T(8,128)(2,1)} %shard_map.79.refs_3_, ...), custom_call_target="tpu_custom_call" | custom-call | flops 14495514624 | bytes 33030144 | tf_op jit(solution)/shard_map/pallas_call | solution.py:204
  283.7 13.7 %collective-permute-done.16.refs_5_.refs_4_.refs_27_ = bf16[1024,768]{1,0:T(8,128)(2,1)} collective-permute-done((bf16[1024,768]{1,0:T(8,128)(2,1)}, bf16[1024,768]{1,0:T(8,128)(2,1)}, u32[]{:S(2)}, u32[]{:S(2)}) %collective-permute-start.16) | collective-permute-done | bytes 1572896 | tf_op jit(solution)/shard_map/ppermute | solution.py:37
  297.5 3.0 collective-permute-start.24
  301.4 1.2 collective-permute-start.23
  302.7 2.1 collective-permute-done.24.refs_12_.refs_16_
  305.2 2.0 collective-permute-start.20
  307.2 22.6 %shard_map.82.refs_8_.refs_5_.refs_39_.refs_43_ = bf16[1536,768]{1,0:T(8,128)(2,1)} custom-call(s32[1]{0:T(128)} %constant.112.clone.1.refs_1_.refs_0_, s32[4]{0:T(128)} %pad_add_fusion.2.refs_1_.refs_3_, f32[12,6]{1,0:T(8,128)} %get-tuple-element.256.refs_2_.refs_4_, bf16[1536,768]{1,0:T(8,128)(2,1)} %collective-permute-done.1.refs_2_.refs_6_.refs_3_.refs_4_, ...), custom_call_target="tpu_custom_call" | custom-call | flops 14495514624 | bytes 33030144 | tf_op jit(solution)/shard_map/pallas_call | solution.py:204
  329.9 1.2 slice.44
  331.1 1.2 slice.46
  332.2 1.3 slice.45
  333.6 7.0 %collective-permute-done.21.refs_6_.refs_5_.refs_28_ = bf16[512,768]{1,0:T(8,128)(2,1)} collective-permute-done((bf16[512,768]{1,0:T(8,128)(2,1)S(1)}, bf16[512,768]{1,0:T(8,128)(2,1)}, u32[]{:S(2)}, u32[]{:S(2)}) %collective-permute-start.21) | collective-permute-done | bytes 786464 | tf_op jit(solution)/shard_map/ppermute | solution.py:37
  340.6 2.5 collective-permute-start.30
  343.1 2.1 collective-permute-done.30.refs_18_.refs_22_
  346.6 1.2 collective-permute-start.29
  347.9 1.5 collective-permute-start.26
  349.4 15.9 %collective-permute-done.27.refs_7_ = bf16[256,768]{1,0:T(8,128)(2,1)S(1)} collective-permute-done((bf16[256,768]{1,0:T(8,128)(2,1)S(1)}, bf16[256,768]{1,0:T(8,128)(2,1)S(1)}, u32[]{:S(2)}, u32[]{:S(2)}) %collective-permute-start.27) | collective-permute-done | bytes 393248 | tf_op jit(solution)/shard_map/ppermute | solution.py:37
  365.5 3.4 collective-permute-start.36
  369.6 1.2 collective-permute-done.36.refs_20_.refs_24_
  371.2 1.5 collective-permute-start.32
  372.7 50.2 %collective-permute-done.33.refs_8_ = bf16[768,768]{1,0:T(8,128)(2,1)S(1)} collective-permute-done((bf16[768,768]{1,0:T(8,128)(2,1)S(1)}, bf16[768,768]{1,0:T(8,128)(2,1)S(1)}, u32[]{:S(2)}, u32[]{:S(2)}) %collective-permute-start.33) | collective-permute-done | bytes 1179680 | tf_op jit(solution)/shard_map/ppermute | solution.py:37
  422.9 2.0 collective-permute-done.32.refs_32_
  427.4 2.8 collective-permute-done.44.refs_11_
  430.5 1.5 collective-permute-start.38
  432.0 4.7 collective-permute-done.40.refs_10_
  439.1 1.7 collective-permute-start.46
  440.9 24.0 %shard_map.83 = bf16[1536,768]{1,0:T(8,128)(2,1)} custom-call(s32[8]{0:T(128)} %stack.134.refs_0_, s32[4]{0:T(128)} %pad_add_fusion.2.refs_1_.refs_3_, f32[12,6]{1,0:T(8,128)} %get-tuple-element.255.refs_2_, bf16[1536,768]{1,0:T(8,128)(2,1)} %get-tuple-element.475.refs_2_.refs_3_.refs_9_.refs_21_.refs_13_.refs_25_, ...), custom_call_target="tpu_custom_call" | custom-call | flops 14495514624 | bytes 33030144 | tf_op jit(solution)/shard_map/pallas_call | solution.py:204
  465.4 2.0 collective-permute-done.38.refs_33_
  468.5 2.1 collective-permute-done.49.refs_39_
  471.0 1.6 collective-permute-done.50.refs_37_.refs_40_
  474.3 15.1 %shard_map.84.refs_40_.refs_44_ = f32[1536,768]{1,0:T(8,128)} custom-call(s32[4]{0:T(128)} %get-tuple-element.251.refs_0_, s32[4]{0:T(128)} %pad_add_fusion.2.refs_1_.refs_3_, bf16[1536,768]{1,0:T(8,128)(2,1)} %get-tuple-element.475.refs_2_.refs_3_.refs_9_.refs_21_.refs_13_.refs_25_, bf16[1536,768]{1,0:T(8,128)(2,1)} %collective-permute-done.17.refs_4_.refs_3_.refs_26_, ...), custom_call_target="tpu_custom_call" | custom-call | flops 7247757312 | bytes 23592960 | tf_op jit(solution)/shard_map/pallas_call | solution.py:204
  489.5 2.7 collective-permute-done.47.refs_12_
  492.3 2.3 collective-permute-start.52
  494.6 1.3 collective-permute-start.53
  495.9 27.2 %shard_map.85 = bf16[1024,768]{1,0:T(8,128)(2,1)} custom-call(s32[8]{0:T(128)} %stack.134.refs_0_, s32[4]{0:T(128)} %pad_add_fusion.2.refs_1_.refs_3_, s32[4]{0:T(128)} %get-tuple-element.252.refs_0_.refs_2_, s32[4]{0:T(128)} %pad_add_fusion.2.refs_1_.refs_3_, f32[12,6]{1,0:T(8,128)} %get-tuple-element.256.refs_2_.refs_4_, ...), custom_call_target="tpu_custom_call" | custom-call | flops 14495514624 | bytes 51904512 | tf_op jit(solution)/shard_map/pallas_call | solution.py:204
  523.1 2.1 collective-permute-start.54
  525.2 18.0 %shard_map.86 = bf16[512,768]{1,0:T(8,128)(2,1)} custom-call(s32[8]{0:T(128)} %stack.134.refs_0_, s32[4]{0:T(128)} %pad_add_fusion.2.refs_1_.refs_3_, s32[4]{0:T(128)} %get-tuple-element.252.refs_0_.refs_2_, s32[4]{0:T(128)} %pad_add_fusion.2.refs_1_.refs_3_, f32[12,6]{1,0:T(8,128)} %get-tuple-element.256.refs_2_.refs_4_, ...), custom_call_target="tpu_custom_call" | custom-call | flops 7247757312 | bytes 51904512 | tf_op jit(solution)/shard_map/pallas_call | solution.py:204
  543.2 3.4 collective-permute-start.55
  546.7 2.5 convert_element_type.29
  549.2 7.5 %collective-permute-done.55 = bf16[512,768]{1,0:T(8,128)(2,1)S(1)} collective-permute-done((bf16[512,768]{1,0:T(8,128)(2,1)}, bf16[512,768]{1,0:T(8,128)(2,1)S(1)}, u32[]{:S(2)}, u32[]{:S(2)}) %collective-permute-start.55) | collective-permute-done | bytes 786464 | tf_op jit(solution)/shard_map/ppermute | solution.py:37
  556.8 2.5 maximum_convert_fusion
  (165 shorter events, 33.0 us)
Async XLA Ops:
  7.2 59.0 %copy-start.4 = (bf16[1536,768]{1,0:T(8,128)(2,1)S(1)}, bf16[1536,768]{1,0:T(8,128)(2,1)}, u32[]{:S(2)}) copy-start(bf16[1536,768]{1,0:T(8,128)(2,1)} %param.6) | copy-start | bytes 7077892
  7.2 201.8 %all-gather.2.cloned.1.call-start = ((), (), s32[]{:S(2)}) async-start(), calls=%async_computation | async-start | bytes 2297856 | tf_op jit(solution)/shard_map/all_gather | solution.py:308
  7.2 59.0 %collective-permute-start.1 = (bf16[1536,768]{1,0:T(8,128)(2,1)}, bf16[1536,768]{1,0:T(8,128)(2,1)}, u32[]{:S(2)}, u32[]{:S(2)}) collective-permute-start(bf16[1536,768]{1,0:T(8,128)(2,1)} %param.6), channel_id=1, source_target_pairs={{0,0},{1,1},{8,2},{9,3},{4,4},{5,5},{12,6},{13,7},{2,8},{3,9},{10,... | collective-permute-start | bytes 7077896 | tf_op jit(solution)/shard_map/ppermute | solution.py:37
  14.8 51.4 %collective-permute-start = (bf16[768,768]{1,0:T(8,128)(2,1)}, bf16[768,768]{1,0:T(8,128)(2,1)}, u32[]{:S(2)}, u32[]{:S(2)}) collective-permute-start(bf16[768,768]{1,0:T(8,128)(2,1)} %get-tuple-element.501), channel_id=1, source_target_pairs={{4,0},{5,1},{12,2},{13,3},{0,4},{1,5},{8,6},{9,7},{6,8},{7,9},{14,... | collective-permute-start | bytes 3538952 | tf_op jit(solution)/shard_map/ppermute | solution.py:37
  66.2 56.3 %collective-permute-start.3 = (bf16[1536,768]{1,0:T(8,128)(2,1)S(1)}, bf16[1536,768]{1,0:T(8,128)(2,1)S(1)}, u32[]{:S(2)}, u32[]{:S(2)}) collective-permute-start(bf16[1536,768]{1,0:T(8,128)(2,1)S(1)} %copy-done.4), channel_id=1, source_target_pairs={{8,0},{9,1},{0,2},{1,3},{12,4},{13,5},{4,6},{5,7},{10,8},{11,9},{2... | collective-permute-start | bytes 7077896 | tf_op jit(solution)/shard_map/ppermute | solution.py:37
  73.3 50.7 %collective-permute-start.6 = (bf16[1536,768]{1,0:T(8,128)(2,1)}, bf16[1536,768]{1,0:T(8,128)(2,1)S(1)}, u32[]{:S(2)}, u32[]{:S(2)}) collective-permute-start(bf16[1536,768]{1,0:T(8,128)(2,1)} %collective-permute-done.1.refs_2_.refs_6_.refs_3_.refs_4_), channel_id=1, source_target_pairs={{8,0},{9,1},{10,2},{11,3},{12,4},{13,5},{14,6},{15,7},{0,8},{1,9},... | collective-permute-start | bytes 7077896 | tf_op jit(solution)/shard_map/ppermute | solution.py:37
  73.4 52.9 %collective-permute-start.5 = (bf16[1536,768]{1,0:T(8,128)(2,1)}, bf16[1536,768]{1,0:T(8,128)(2,1)}, u32[]{:S(2)}, u32[]{:S(2)}) collective-permute-start(bf16[1536,768]{1,0:T(8,128)(2,1)} %collective-permute-done.1.refs_2_.refs_6_.refs_3_.refs_4_), channel_id=1, source_target_pairs={{1,0},{0,1},{3,2},{2,3},{5,4},{4,5},{7,6},{6,7},{9,8},{8,9},{11,10... | collective-permute-start | bytes 7077896 | tf_op jit(solution)/shard_map/ppermute | solution.py:37
  74.9 52.4 %collective-permute-start.4 = (bf16[1536,768]{1,0:T(8,128)(2,1)}, bf16[1536,768]{1,0:T(8,128)(2,1)}, u32[]{:S(2)}, u32[]{:S(2)}) collective-permute-start(bf16[1536,768]{1,0:T(8,128)(2,1)} %collective-permute-done.1.refs_2_.refs_6_.refs_3_.refs_4_), channel_id=1, source_target_pairs={{16,0},{17,1},{18,2},{19,3},{20,4},{21,5},{22,6},{23,7},{24,8},{25... | collective-permute-start | bytes 7077896 | tf_op jit(solution)/shard_map/ppermute | solution.py:37
  76.1 30.1 %collective-permute-start.2 = (bf16[768,768]{1,0:T(8,128)(2,1)S(1)}, bf16[768,768]{1,0:T(8,128)(2,1)S(1)}, u32[]{:S(2)}, u32[]{:S(2)}) collective-permute-start(bf16[768,768]{1,0:T(8,128)(2,1)S(1)} %get-tuple-element.249), channel_id=1, source_target_pairs={{4,0},{5,1},{12,2},{13,3},{0,4},{1,5},{8,6},{9,7},{6,8},{7,9},{14,... | collective-permute-start | bytes 3538952 | tf_op jit(solution)/shard_map/ppermute | solution.py:37
  127.3 9.7 %collective-permute-start.10 = (bf16[1536,768]{1,0:T(8,128)(2,1)}, bf16[1536,768]{1,0:T(8,128)(2,1)}, u32[]{:S(2)}, u32[]{:S(2)}) collective-permute-start(bf16[1536,768]{1,0:T(8,128)(2,1)} %collective-permute-done.5.refs_7_.refs_5_), channel_id=1, source_target_pairs={{8,0},{9,1},{10,2},{11,3},{12,4},{13,5},{14,6},{15,7},{0,8},{1,9},... | collective-permute-start | bytes 7077896 | tf_op jit(solution)/shard_map/ppermute | solution.py:37
  132.5 59.6 %collective-permute-start.7 = (bf16[1536,768]{1,0:T(8,128)(2,1)}, bf16[1536,768]{1,0:T(8,128)(2,1)S(1)}, u32[]{:S(2)}, u32[]{:S(2)}) collective-permute-start(bf16[1536,768]{1,0:T(8,128)(2,1)} %copy-done.24), channel_id=1, source_target_pairs={{16,0},{17,1},{18,2},{19,3},{20,4},{21,5},{22,6},{23,7},{24,8},{25... | collective-permute-start | bytes 7077896 | tf_op jit(solution)/shard_map/ppermute | solution.py:37
  132.8 29.1 %collective-permute-start.9 = (bf16[768,768]{1,0:T(8,128)(2,1)}, bf16[768,768]{1,0:T(8,128)(2,1)}, u32[]{:S(2)}, u32[]{:S(2)}) collective-permute-start(bf16[768,768]{1,0:T(8,128)(2,1)} %copy-done.30), channel_id=1, source_target_pairs={{1,0},{0,1},{3,2},{2,3},{5,4},{4,5},{7,6},{6,7},{9,8},{8,9},{11,10... | collective-permute-start | bytes 3538952 | tf_op jit(solution)/shard_map/ppermute | solution.py:37
  133.0 58.0 %collective-permute-start.8 = (bf16[768,768]{1,0:T(8,128)(2,1)}, bf16[768,768]{1,0:T(8,128)(2,1)}, u32[]{:S(2)}, u32[]{:S(2)}) collective-permute-start(bf16[768,768]{1,0:T(8,128)(2,1)} %collective-permute-done.refs_7_.refs_8_), channel_id=1, source_target_pairs={{1,0},{0,1},{3,2},{2,3},{5,4},{4,5},{7,6},{6,7},{9,8},{8,9},{11,10... | collective-permute-start | bytes 3538952 | tf_op jit(solution)/shard_map/ppermute | solution.py:37
  137.0 55.1 %collective-permute-start.11 = (bf16[768,768]{1,0:T(8,128)(2,1)}, bf16[768,768]{1,0:T(8,128)(2,1)}, u32[]{:S(2)}, u32[]{:S(2)}) collective-permute-start(bf16[768,768]{1,0:T(8,128)(2,1)} %collective-permute-done.refs_7_.refs_8_), channel_id=1, source_target_pairs={{8,0},{9,1},{10,2},{11,3},{12,4},{13,5},{14,6},{15,7},{0,8},{1,9},... | collective-permute-start | bytes 3538952 | tf_op jit(solution)/shard_map/ppermute | solution.py:37
  192.1 18.6 %collective-permute-start.12 = (bf16[768,768]{1,0:T(8,128)(2,1)}, bf16[768,768]{1,0:T(8,128)(2,1)}, u32[]{:S(2)}, u32[]{:S(2)}) collective-permute-start(bf16[768,768]{1,0:T(8,128)(2,1)} %copy-done.30), channel_id=1, source_target_pairs={{8,0},{9,1},{10,2},{11,3},{12,4},{13,5},{14,6},{15,7},{0,8},{1,9},... | collective-permute-start | bytes 3538952 | tf_op jit(solution)/shard_map/ppermute | solution.py:37
  192.9 17.8 %collective-permute-start.13 = (bf16[768,768]{1,0:T(8,128)(2,1)}, bf16[768,768]{1,0:T(8,128)(2,1)}, u32[]{:S(2)}, u32[]{:S(2)}) collective-permute-start(bf16[768,768]{1,0:T(8,128)(2,1)} %collective-permute-done.8.refs_9_.refs_10_), channel_id=1, source_target_pairs={{8,0},{9,1},{10,2},{11,3},{12,4},{13,5},{14,6},{15,7},{0,8},{1,9},... | collective-permute-start | bytes 3538952 | tf_op jit(solution)/shard_map/ppermute | solution.py:37
  193.0 17.7 %collective-permute-start.14 = (bf16[768,768]{1,0:T(8,128)(2,1)}, bf16[768,768]{1,0:T(8,128)(2,1)}, u32[]{:S(2)}, u32[]{:S(2)}) collective-permute-start(bf16[768,768]{1,0:T(8,128)(2,1)} %collective-permute-done.9.refs_10_.refs_11_), channel_id=1, source_target_pairs={{8,0},{9,1},{10,2},{11,3},{12,4},{13,5},{14,6},{15,7},{0,8},{1,9},... | collective-permute-start | bytes 3538952 | tf_op jit(solution)/shard_map/ppermute | solution.py:37
  227.0 70.5 %collective-permute-start.19 = (bf16[1536,768]{1,0:T(8,128)(2,1)}, bf16[1536,768]{1,0:T(8,128)(2,1)S(1)}, u32[]{:S(2)}, u32[]{:S(2)}) collective-permute-start(bf16[1536,768]{1,0:T(8,128)(2,1)} %get-tuple-element.475.refs_2_.refs_3_.refs_9_.refs_21_.refs_13_.refs_25_), channel_id=1, source_target_pairs={{8,0},{9,1},{10,2},{11,3},{12,4},{13,5},{14,6},{15,7},{0,8},{1,9},... | collective-permute-start | bytes 7077896 | tf_op jit(solution)/shard_map/ppermute | solution.py:37
  227.8 69.6 %collective-permute-start.18 = (bf16[1536,768]{1,0:T(8,128)(2,1)}, bf16[1536,768]{1,0:T(8,128)(2,1)}, u32[]{:S(2)}, u32[]{:S(2)}) collective-permute-start(bf16[1536,768]{1,0:T(8,128)(2,1)} %get-tuple-element.475.refs_2_.refs_3_.refs_9_.refs_21_.refs_13_.refs_25_), channel_id=1, source_target_pairs={{1,0},{0,1},{3,2},{2,3},{5,4},{4,5},{7,6},{6,7},{9,8},{8,9},{11,10... | collective-permute-start | bytes 7077896 | tf_op jit(solution)/shard_map/ppermute | solution.py:37
  228.1 69.4 %collective-permute-start.17 = (bf16[1536,768]{1,0:T(8,128)(2,1)}, bf16[1536,768]{1,0:T(8,128)(2,1)}, u32[]{:S(2)}, u32[]{:S(2)}) collective-permute-start(bf16[1536,768]{1,0:T(8,128)(2,1)} %get-tuple-element.475.refs_2_.refs_3_.refs_9_.refs_21_.refs_13_.refs_25_), channel_id=1, source_target_pairs={{16,0},{17,1},{18,2},{19,3},{20,4},{21,5},{22,6},{23,7},{24,8},{25... | collective-permute-start | bytes 7077896 | tf_op jit(solution)/shard_map/ppermute | solution.py:37
  228.6 68.9 %collective-permute-start.16 = (bf16[1024,768]{1,0:T(8,128)(2,1)}, bf16[1024,768]{1,0:T(8,128)(2,1)}, u32[]{:S(2)}, u32[]{:S(2)}) collective-permute-start(bf16[1024,768]{1,0:T(8,128)(2,1)} %get-tuple-element.296), channel_id=1, source_target_pairs={{2,0},{3,1},{0,2},{1,3},{6,4},{7,5},{4,6},{5,7},{10,8},{11,9},{8,1... | collective-permute-start | bytes 4718600 | tf_op jit(solution)/shard_map/ppermute | solution.py:37
  228.6 68.9 %collective-permute-start.15 = (bf16[1024,768]{1,0:T(8,128)(2,1)}, bf16[1024,768]{1,0:T(8,128)(2,1)}, u32[]{:S(2)}, u32[]{:S(2)}) collective-permute-start(bf16[1024,768]{1,0:T(8,128)(2,1)} %get-tuple-element.296), channel_id=1, source_target_pairs={{4,0},{5,1},{6,2},{7,3},{0,4},{1,5},{2,6},{3,7},{12,8},{13,9},{14,... | collective-permute-start | bytes 4718600 | tf_op jit(solution)/shard_map/ppermute | solution.py:37
  260.2 45.0 %copy-start.31 = (bf16[512,768]{1,0:T(8,128)(2,1)S(1)}, bf16[512,768]{1,0:T(8,128)(2,1)}, u32[]{:S(2)}) copy-start(bf16[512,768]{1,0:T(8,128)(2,1)} %get-tuple-element.303) | copy-start | bytes 2359300
  297.5 7.3 %collective-permute-start.24 = (bf16[1536,768]{1,0:T(8,128)(2,1)}, bf16[1536,768]{1,0:T(8,128)(2,1)S(1)}, u32[]{:S(2)}, u32[]{:S(2)}) collective-permute-start(bf16[1536,768]{1,0:T(8,128)(2,1)} %collective-permute-done.18.refs_10_.refs_14_), channel_id=1, source_target_pairs={{8,0},{9,1},{10,2},{11,3},{12,4},{13,5},{14,6},{15,7},{0,8},{1,9},... | collective-permute-start | bytes 7077896 | tf_op jit(solution)/shard_map/ppermute | solution.py:37
  300.4 40.2 %collective-permute-start.22 = (bf16[1024,768]{1,0:T(8,128)(2,1)}, bf16[1024,768]{1,0:T(8,128)(2,1)}, u32[]{:S(2)}, u32[]{:S(2)}) collective-permute-start(bf16[1024,768]{1,0:T(8,128)(2,1)} %collective-permute-done.16.refs_5_.refs_4_.refs_27_), channel_id=1, source_target_pairs={{16,0},{17,1},{18,2},{19,3},{20,4},{21,5},{22,6},{23,7},{24,8},{25... | collective-permute-start | bytes 4718600 | tf_op jit(solution)/shard_map/ppermute | solution.py:37
  301.4 39.2 %collective-permute-start.23 = (bf16[1024,768]{1,0:T(8,128)(2,1)}, bf16[1024,768]{1,0:T(8,128)(2,1)}, u32[]{:S(2)}, u32[]{:S(2)}) collective-permute-start(bf16[1024,768]{1,0:T(8,128)(2,1)} %collective-permute-done.15.refs_13_.refs_17_), channel_id=1, source_target_pairs={{1,0},{0,1},{3,2},{2,3},{5,4},{4,5},{7,6},{6,7},{9,8},{8,9},{11,10... | collective-permute-start | bytes 4718600 | tf_op jit(solution)/shard_map/ppermute | solution.py:37
  304.8 35.8 %collective-permute-start.25 = (bf16[1024,768]{1,0:T(8,128)(2,1)}, bf16[1024,768]{1,0:T(8,128)(2,1)}, u32[]{:S(2)}, u32[]{:S(2)}) collective-permute-start(bf16[1024,768]{1,0:T(8,128)(2,1)} %collective-permute-done.15.refs_13_.refs_17_), channel_id=1, source_target_pairs={{8,0},{9,1},{10,2},{11,3},{12,4},{13,5},{14,6},{15,7},{0,8},{1,9},... | collective-permute-start | bytes 4718600 | tf_op jit(solution)/shard_map/ppermute | solution.py:37
  305.2 35.4 %collective-permute-start.21 = (bf16[512,768]{1,0:T(8,128)(2,1)S(1)}, bf16[512,768]{1,0:T(8,128)(2,1)}, u32[]{:S(2)}, u32[]{:S(2)}) collective-permute-start(bf16[512,768]{1,0:T(8,128)(2,1)S(1)} %copy-done.31), channel_id=1, source_target_pairs={{2,0},{3,1},{0,2},{1,3},{6,4},{7,5},{4,6},{5,7},{10,8},{11,9},{8,1... | collective-permute-start | bytes 2359304 | tf_op jit(solution)/shard_map/ppermute | solution.py:37
  305.2 35.4 %collective-permute-start.20 = (bf16[512,768]{1,0:T(8,128)(2,1)S(1)}, bf16[512,768]{1,0:T(8,128)(2,1)}, u32[]{:S(2)}, u32[]{:S(2)}) collective-permute-start(bf16[512,768]{1,0:T(8,128)(2,1)S(1)} %copy-done.31), channel_id=1, source_target_pairs={{4,0},{5,1},{6,2},{7,3},{0,4},{1,5},{2,6},{3,7},{12,8},{13,9},{14,... | collective-permute-start | bytes 2359304 | tf_op jit(solution)/shard_map/ppermute | solution.py:37
  340.6 4.6 collective-permute-start.30
  345.2 20.3 %collective-permute-start.31 = (bf16[1024,768]{1,0:T(8,128)(2,1)}, bf16[1024,768]{1,0:T(8,128)(2,1)S(1)}, u32[]{:S(2)}, u32[]{:S(2)}) collective-permute-start(bf16[1024,768]{1,0:T(8,128)(2,1)} %collective-permute-done.23.refs_15_.refs_19_), channel_id=1, source_target_pairs={{8,0},{9,1},{10,2},{11,3},{12,4},{13,5},{14,6},{15,7},{0,8},{1,9},... | collective-permute-start | bytes 4718600 | tf_op jit(solution)/shard_map/ppermute | solution.py:37
  345.6 19.7 %collective-permute-start.28 = (bf16[512,768]{1,0:T(8,128)(2,1)}, bf16[512,768]{1,0:T(8,128)(2,1)S(1)}, u32[]{:S(2)}, u32[]{:S(2)}) collective-permute-start(bf16[512,768]{1,0:T(8,128)(2,1)} %collective-permute-done.21.refs_6_.refs_5_.refs_28_), channel_id=1, source_target_pairs={{16,0},{17,1},{18,2},{19,3},{20,4},{21,5},{22,6},{23,7},{24,8},{25... | collective-permute-start | bytes 2359304 | tf_op jit(solution)/shard_map/ppermute | solution.py:37
  346.6 18.9 %collective-permute-start.29 = (bf16[512,768]{1,0:T(8,128)(2,1)}, bf16[512,768]{1,0:T(8,128)(2,1)S(1)}, u32[]{:S(2)}, u32[]{:S(2)}) collective-permute-start(bf16[512,768]{1,0:T(8,128)(2,1)} %collective-permute-done.20.refs_14_.refs_18_), channel_id=1, source_target_pairs={{1,0},{0,1},{3,2},{2,3},{5,4},{4,5},{7,6},{6,7},{9,8},{8,9},{11,10... | collective-permute-start | bytes 2359304 | tf_op jit(solution)/shard_map/ppermute | solution.py:37
  347.9 17.5 %collective-permute-start.27 = (bf16[256,768]{1,0:T(8,128)(2,1)S(1)}, bf16[256,768]{1,0:T(8,128)(2,1)S(1)}, u32[]{:S(2)}, u32[]{:S(2)}) collective-permute-start(bf16[256,768]{1,0:T(8,128)(2,1)S(1)} %slice.44), channel_id=1, source_target_pairs={{2,0},{3,1},{0,2},{1,3},{6,4},{7,5},{4,6},{5,7},{10,8},{11,9},{8,1... | collective-permute-start | bytes 1179656 | tf_op jit(solution)/shard_map/ppermute | solution.py:37
  347.9 17.5 %collective-permute-start.26 = (bf16[256,768]{1,0:T(8,128)(2,1)S(1)}, bf16[256,768]{1,0:T(8,128)(2,1)S(1)}, u32[]{:S(2)}, u32[]{:S(2)}) collective-permute-start(bf16[256,768]{1,0:T(8,128)(2,1)S(1)} %slice.44), channel_id=1, source_target_pairs={{4,0},{5,1},{6,2},{7,3},{0,4},{1,5},{2,6},{3,7},{12,8},{13,9},{14,... | collective-permute-start | bytes 1179656 | tf_op jit(solution)/shard_map/ppermute | solution.py:37
  365.3 71.6 %copy-start.18 = (bf16[256,768]{1,0:T(8,128)(2,1)}, bf16[256,768]{1,0:T(8,128)(2,1)S(1)}, u32[]{:S(2)}) copy-start(bf16[256,768]{1,0:T(8,128)(2,1)S(1)} %collective-permute-done.27.refs_7_) | copy-start | bytes 1179652
  365.3 73.0 %copy-start.19 = (bf16[256,768]{1,0:T(8,128)(2,1)}, bf16[256,768]{1,0:T(8,128)(2,1)S(1)}, u32[]{:S(2)}) copy-start(bf16[256,768]{1,0:T(8,128)(2,1)S(1)} %collective-permute-done.26.refs_31_) | copy-start | bytes 1179652
  365.5 71.4 %copy-start.12 = (bf16[512,768]{1,0:T(8,128)(2,1)}, bf16[512,768]{1,0:T(8,128)(2,1)S(1)}, u32[]{:S(2)}) copy-start(bf16[512,768]{1,0:T(8,128)(2,1)S(1)} %collective-permute-done.29.refs_16_.refs_20_) | copy-start | bytes 2359300
  365.5 75.4 %copy-start.5 = (bf16[1024,768]{1,0:T(8,128)(2,1)}, bf16[1024,768]{1,0:T(8,128)(2,1)S(1)}, u32[]{:S(2)}) copy-start(bf16[1024,768]{1,0:T(8,128)(2,1)S(1)} %collective-permute-done.31.refs_19_.refs_23_) | copy-start | bytes 4718596
  365.5 5.3 collective-permute-start.36
  368.9 56.0 %collective-permute-start.35 = (bf16[1536,768]{1,0:T(8,128)(2,1)S(1)}, bf16[1536,768]{1,0:T(8,128)(2,1)S(1)}, u32[]{:S(2)}, u32[]{:S(2)}) collective-permute-start(bf16[1536,768]{1,0:T(8,128)(2,1)S(1)} %copy-done), channel_id=1, source_target_pairs={{1,0},{0,1},{3,2},{2,3},{5,4},{4,5},{7,6},{6,7},{9,8},{8,9},{11,10... | collective-permute-start | bytes 7077896 | tf_op jit(solution)/shard_map/ppermute | solution.py:37
  369.1 55.8 %collective-permute-start.34 = (bf16[1536,768]{1,0:T(8,128)(2,1)S(1)}, bf16[1536,768]{1,0:T(8,128)(2,1)S(1)}, u32[]{:S(2)}, u32[]{:S(2)}) collective-permute-start(bf16[1536,768]{1,0:T(8,128)(2,1)S(1)} %copy-done), channel_id=1, source_target_pairs={{16,0},{17,1},{18,2},{19,3},{20,4},{21,5},{22,6},{23,7},{24,8},{25... | collective-permute-start | bytes 7077896 | tf_op jit(solution)/shard_map/ppermute | solution.py:37
  370.8 67.1 %copy-start.13 = (bf16[512,768]{1,0:T(8,128)(2,1)}, bf16[512,768]{1,0:T(8,128)(2,1)S(1)}, u32[]{:S(2)}) copy-start(bf16[512,768]{1,0:T(8,128)(2,1)S(1)} %collective-permute-done.36.refs_20_.refs_24_) | copy-start | bytes 2359300
  370.8 54.1 %collective-permute-start.37 = (bf16[1536,768]{1,0:T(8,128)(2,1)S(1)}, bf16[1536,768]{1,0:T(8,128)(2,1)S(1)}, u32[]{:S(2)}, u32[]{:S(2)}) collective-permute-start(bf16[1536,768]{1,0:T(8,128)(2,1)S(1)} %copy-done), channel_id=1, source_target_pairs={{8,0},{9,1},{10,2},{11,3},{12,4},{13,5},{14,6},{15,7},{0,8},{1,9},... | collective-permute-start | bytes 7077896 | tf_op jit(solution)/shard_map/ppermute | solution.py:37
  371.2 51.7 %collective-permute-start.33 = (bf16[768,768]{1,0:T(8,128)(2,1)S(1)}, bf16[768,768]{1,0:T(8,128)(2,1)S(1)}, u32[]{:S(2)}, u32[]{:S(2)}) collective-permute-start(bf16[768,768]{1,0:T(8,128)(2,1)S(1)} %slice.45), channel_id=1, source_target_pairs={{2,0},{3,1},{0,2},{1,3},{6,4},{7,5},{4,6},{5,7},{10,8},{11,9},{8,1... | collective-permute-start | bytes 3538952 | tf_op jit(solution)/shard_map/ppermute | solution.py:37
  371.2 53.7 %collective-permute-start.32 = (bf16[768,768]{1,0:T(8,128)(2,1)S(1)}, bf16[768,768]{1,0:T(8,128)(2,1)}, u32[]{:S(2)}, u32[]{:S(2)}) collective-permute-start(bf16[768,768]{1,0:T(8,128)(2,1)S(1)} %slice.45), channel_id=1, source_target_pairs={{4,0},{5,1},{6,2},{7,3},{0,4},{1,5},{2,6},{3,7},{12,8},{13,9},{14,... | collective-permute-start | bytes 3538952 | tf_op jit(solution)/shard_map/ppermute | solution.py:37
  424.9 5.2 collective-permute-start.44
  426.0 10.8 %collective-permute-start.40 = (bf16[256,768]{1,0:T(8,128)(2,1)S(1)}, bf16[256,768]{1,0:T(8,128)(2,1)S(1)}, u32[]{:S(2)}, u32[]{:S(2)}) collective-permute-start(bf16[256,768]{1,0:T(8,128)(2,1)S(1)} %collective-permute-done.27.refs_7_), channel_id=1, source_target_pairs={{16,0},{17,1},{18,2},{19,3},{20,4},{21,5},{22,6},{23,7},{24,8},{25... | collective-permute-start | bytes 1179656 | tf_op jit(solution)/shard_map/ppermute | solution.py:37
  426.5 10.5 %collective-permute-start.42 = (bf16[256,768]{1,0:T(8,128)(2,1)S(1)}, bf16[256,768]{1,0:T(8,128)(2,1)}, u32[]{:S(2)}, u32[]{:S(2)}) collective-permute-start(bf16[256,768]{1,0:T(8,128)(2,1)S(1)} %collective-permute-done.26.refs_31_), channel_id=1, source_target_pairs={{1,0},{0,1},{3,2},{2,3},{5,4},{4,5},{7,6},{6,7},{9,8},{8,9},{11,10... | collective-permute-start | bytes 1179656 | tf_op jit(solution)/shard_map/ppermute | solution.py:37
  430.1 8.2 %collective-permute-start.45 = (bf16[256,768]{1,0:T(8,128)(2,1)S(1)}, bf16[256,768]{1,0:T(8,128)(2,1)S(1)}, u32[]{:S(2)}, u32[]{:S(2)}) collective-permute-start(bf16[256,768]{1,0:T(8,128)(2,1)S(1)} %collective-permute-done.26.refs_31_), channel_id=1, source_target_pairs={{8,0},{9,1},{10,2},{11,3},{12,4},{13,5},{14,6},{15,7},{0,8},{1,9},... | collective-permute-start | bytes 1179656 | tf_op jit(solution)/shard_map/ppermute | solution.py:37
  430.5 34.9 %collective-permute-start.39 = (bf16[512,768]{1,0:T(8,128)(2,1)S(1)}, bf16[512,768]{1,0:T(8,128)(2,1)}, u32[]{:S(2)}, u32[]{:S(2)}) collective-permute-start(bf16[512,768]{1,0:T(8,128)(2,1)S(1)} %slice.46), channel_id=1, source_target_pairs={{2,0},{3,1},{0,2},{1,3},{6,4},{7,5},{4,6},{5,7},{10,8},{11,9},{8,1... | collective-permute-start | bytes 2359304 | tf_op jit(solution)/shard_map/ppermute | solution.py:37
  430.5 36.9 %collective-permute-start.38 = (bf16[512,768]{1,0:T(8,128)(2,1)S(1)}, bf16[512,768]{1,0:T(8,128)(2,1)}, u32[]{:S(2)}, u32[]{:S(2)}) collective-permute-start(bf16[512,768]{1,0:T(8,128)(2,1)S(1)} %slice.46), channel_id=1, source_target_pairs={{4,0},{5,1},{6,2},{7,3},{0,4},{1,5},{2,6},{3,7},{12,8},{13,9},{14,... | collective-permute-start | bytes 2359304 | tf_op jit(solution)/shard_map/ppermute | solution.py:37
  436.9 30.5 %collective-permute-start.43 = (bf16[768,768]{1,0:T(8,128)(2,1)}, bf16[768,768]{1,0:T(8,128)(2,1)S(1)}, u32[]{:S(2)}, u32[]{:S(2)}) collective-permute-start(bf16[768,768]{1,0:T(8,128)(2,1)} %collective-permute-done.32.refs_32_), channel_id=1, source_target_pairs={{1,0},{0,1},{3,2},{2,3},{5,4},{4,5},{7,6},{6,7},{9,8},{8,9},{11,10... | collective-permute-start | bytes 3538952 | tf_op jit(solution)/shard_map/ppermute | solution.py:37
  437.8 29.6 %collective-permute-start.41 = (bf16[768,768]{1,0:T(8,128)(2,1)S(1)}, bf16[768,768]{1,0:T(8,128)(2,1)S(1)}, u32[]{:S(2)}, u32[]{:S(2)}) collective-permute-start(bf16[768,768]{1,0:T(8,128)(2,1)S(1)} %collective-permute-done.33.refs_8_), channel_id=1, source_target_pairs={{16,0},{17,1},{18,2},{19,3},{20,4},{21,5},{22,6},{23,7},{24,8},{25... | collective-permute-start | bytes 3538952 | tf_op jit(solution)/shard_map/ppermute | solution.py:37
  439.1 28.3 %collective-permute-start.46 = (bf16[768,768]{1,0:T(8,128)(2,1)}, bf16[768,768]{1,0:T(8,128)(2,1)}, u32[]{:S(2)}, u32[]{:S(2)}) collective-permute-start(bf16[768,768]{1,0:T(8,128)(2,1)} %collective-permute-done.32.refs_32_), channel_id=1, source_target_pairs={{8,0},{9,1},{10,2},{11,3},{12,4},{13,5},{14,6},{15,7},{0,8},{1,9},... | collective-permute-start | bytes 3538952 | tf_op jit(solution)/shard_map/ppermute | solution.py:37
  467.5 3.1 collective-permute-start.49
  470.6 1.9 collective-permute-start.50
  472.5 19.8 %collective-permute-start.51 = (bf16[768,768]{1,0:T(8,128)(2,1)S(1)}, bf16[768,768]{1,0:T(8,128)(2,1)S(1)}, u32[]{:S(2)}, u32[]{:S(2)}) collective-permute-start(bf16[768,768]{1,0:T(8,128)(2,1)S(1)} %collective-permute-done.43.refs_34_.refs_35_), channel_id=1, source_target_pairs={{8,0},{9,1},{10,2},{11,3},{12,4},{13,5},{14,6},{15,7},{0,8},{1,9},... | collective-permute-start | bytes 3538952 | tf_op jit(solution)/shard_map/ppermute | solution.py:37
  472.9 19.2 %collective-permute-start.47 = (bf16[512,768]{1,0:T(8,128)(2,1)}, bf16[512,768]{1,0:T(8,128)(2,1)S(1)}, u32[]{:S(2)}, u32[]{:S(2)}) collective-permute-start(bf16[512,768]{1,0:T(8,128)(2,1)} %collective-permute-done.39.refs_9_), channel_id=1, source_target_pairs={{16,0},{17,1},{18,2},{19,3},{20,4},{21,5},{22,6},{23,7},{24,8},{25... | collective-permute-start | bytes 2359304 | tf_op jit(solution)/shard_map/ppermute | solution.py:37
  473.4 18.9 %collective-permute-start.48 = (bf16[512,768]{1,0:T(8,128)(2,1)}, bf16[512,768]{1,0:T(8,128)(2,1)S(1)}, u32[]{:S(2)}, u32[]{:S(2)}) collective-permute-start(bf16[512,768]{1,0:T(8,128)(2,1)} %collective-permute-done.38.refs_33_), channel_id=1, source_target_pairs={{1,0},{0,1},{3,2},{2,3},{5,4},{4,5},{7,6},{6,7},{9,8},{8,9},{11,10... | collective-permute-start | bytes 2359304 | tf_op jit(solution)/shard_map/ppermute | solution.py:37
  492.3 30.8 %collective-permute-start.52 = (bf16[1536,768]{1,0:T(8,128)(2,1)}, bf16[1536,768]{1,0:T(8,128)(2,1)S(1)}, u32[]{:S(2)}, u32[]{:S(2)}) collective-permute-start(bf16[1536,768]{1,0:T(8,128)(2,1)} %shard_map.83), channel_id=1, source_target_pairs={{0,0},{1,1},{8,2},{9,3},{4,4},{5,5},{12,6},{13,7},{2,8},{3,9},{10,... | collective-permute-start | bytes 7077896 | tf_op jit(solution)/shard_map/ppermute | solution.py:37
  494.6 28.5 %collective-permute-start.53 = (bf16[512,768]{1,0:T(8,128)(2,1)S(1)}, bf16[512,768]{1,0:T(8,128)(2,1)S(1)}, u32[]{:S(2)}, u32[]{:S(2)}) collective-permute-start(bf16[512,768]{1,0:T(8,128)(2,1)S(1)} %collective-permute-done.48.refs_36_), channel_id=1, source_target_pairs={{8,0},{9,1},{10,2},{11,3},{12,4},{13,5},{14,6},{15,7},{0,8},{1,9},... | collective-permute-start | bytes 2359304 | tf_op jit(solution)/shard_map/ppermute | solution.py:37
  523.1 33.7 %collective-permute-start.54 = (bf16[1024,768]{1,0:T(8,128)(2,1)}, bf16[1024,768]{1,0:T(8,128)(2,1)S(1)}, u32[]{:S(2)}, u32[]{:S(2)}) collective-permute-start(bf16[1024,768]{1,0:T(8,128)(2,1)} %shard_map.85), channel_id=1, source_target_pairs={{0,0},{1,1},{8,2},{9,3},{4,4},{5,5},{12,6},{13,7},{2,8},{3,9},{10,... | collective-permute-start | bytes 4718600 | tf_op jit(solution)/shard_map/ppermute | solution.py:37
  543.2 13.5 %collective-permute-start.55 = (bf16[512,768]{1,0:T(8,128)(2,1)}, bf16[512,768]{1,0:T(8,128)(2,1)S(1)}, u32[]{:S(2)}, u32[]{:S(2)}) collective-permute-start(bf16[512,768]{1,0:T(8,128)(2,1)} %shard_map.86), channel_id=1, source_target_pairs={{0,0},{1,1},{8,2},{9,3},{4,4},{5,5},{12,6},{13,7},{2,8},{3,9},{10,... | collective-permute-start | bytes 2359304 | tf_op jit(solution)/shard_map/ppermute | solution.py:37
  (25 other events, 398.7 us)
Sparse Core Ops, SparseCore 0:
  132.6 58.4 all-gather.1
